TPU v7x, 32 devices: a whole 2x2x4 slice. The times are simulated.
32 devices in a mesh: section: 4 (over y, x), dp: 8 (over z, core).
Axes of the slice: x: 2, y: 2, z: 4, core: 2. Of those that a mesh axis runs over, the one named last changes fastest.
Arguments:
- node_table: bfloat16 [131072, 128], P('dp'), may hold values from -6 to 6
- owners: int32 [4, 245760, 1], P('section', 'dp'), may hold values from 0 to 7; in each aligned block of 30720 rows (0 to 30719, 30720 to 61439, ..., all dimensions but the last counted through in order) at most 7680 rows name the same one
- local_rows: int32 [4, 245760], P('section', 'dp'), may hold values from 0 to 16383
- inner_neighbours: int32 [4, 22528, 15], P(None, 'dp'), may hold values from 0 to 30719
- inner_counts: int32 [4, 22528], P(None, 'dp'), may hold values from 1 to 15
- outer_neighbours: int32 [4, 2048, 10], P(None, 'dp'), may hold values from 0 to 2815
- outer_counts: int32 [4, 2048], P(None, 'dp'), may hold values from 1 to 10
- labels: int32 [4, 2048], P(None, 'dp'), may hold values from 0 to 171
- label_mask: int32 [4, 2048], P(None, 'dp'), may hold values from 0 to 1, as said below
- weight_inner: float32 [256, 256], P(('section', 'dp')), may hold values from -0.375 to 0.375
- weight_outer: float32 [512, 256], P(('section', 'dp')), may hold values from -0.25 to 0.25
- weight_head: float32 [256, 172], P(('section', 'dp')), may hold values from -1.125 to 1.125
- biases: float32 [684], replicated, may hold values from -1.8 to 1.8
- first_inner: float32 [256, 256], P(('section', 'dp')), may hold values from -6.9211565e-05 to 6.9211565e-05
- first_outer: float32 [512, 256], P(('section', 'dp')), may hold values from -6.9211565e-05 to 6.9211565e-05
- first_head: float32 [256, 172], P(('section', 'dp')), may hold values from -6.9211565e-05 to 6.9211565e-05
- first_biases: float32 [684], replicated, may hold values from -0.00020356342 to 0.00020356342
- second_inner: float32 [256, 256], P(('section', 'dp')), may hold values from 1.0369886e-11 to 4.1479545e-11
- second_outer: float32 [512, 256], P(('section', 'dp')), may hold values from 1.0369886e-11 to 4.1479545e-11
- second_head: float32 [256, 172], P(('section', 'dp')), may hold values from 1.0369886e-11 to 4.1479545e-11
- second_biases: float32 [684], replicated, may hold values from 9.3328976e-11 to 3.733159e-10
- smooth_inner: float32 [256, 256], P(('section', 'dp')), may hold values from -0.375 to 0.375
- smooth_outer: float32 [512, 256], P(('section', 'dp')), may hold values from -0.25 to 0.25
- smooth_head: float32 [256, 172], P(('section', 'dp')), may hold values from -0.375 to 0.375
- smooth_biases: float32 [684], replicated, may hold values from -1.8 to 1.8
Outputs:
- loss_sum: float32 [], replicated
- label_count: float32 [], replicated
- clip_norm: float32 [], replicated
- matrix_norms: float32 [3, 2], replicated
- new_inner: float32 [256, 256], P(('section', 'dp'))
- new_outer: float32 [512, 256], P(('section', 'dp'))
- new_head: float32 [256, 172], P(('section', 'dp'))
- new_biases: float32 [684], replicated
- moment_inner: float32 [256, 256], P(('section', 'dp'))
- moment_outer: float32 [512, 256], P(('section', 'dp'))
- moment_head: float32 [256, 172], P(('section', 'dp'))
- moment_biases: float32 [684], replicated
- square_inner: float32 [256, 256], P(('section', 'dp'))
- square_outer: float32 [512, 256], P(('section', 'dp'))
- square_head: float32 [256, 172], P(('section', 'dp'))
- square_biases: float32 [684], replicated
- average_inner: float32 [256, 256], P(('section', 'dp'))
- average_outer: float32 [512, 256], P(('section', 'dp'))
- average_head: float32 [256, 172], P(('section', 'dp'))
- average_biases: float32 [684], replicated
Inputs may be any that keep to these rules, and one draw needn't show every extreme that they name: `owners`: the frontier of one micro-batch on one data index names each owner at most 7680 times, a bound that some block reaches. `label_mask`: the share of labelled seeds rises with the data index.
All inputs are finite; a program needn't handle non-finite values.
Results may differ from a plain program's by a relative error of at most 0.0042.
Values may be sent and summed in bfloat16 or wider, within the bound.
A program may use at most 192 MiB of HBM per device.

v0:
```python
import jax
import jax.numpy as jnp
from jax import lax
from jax.sharding import PartitionSpec as P

STEP = 5


BETA_ONE = 0.9
BETA_TWO = 0.999
EPSILON = 1e-06
DECAY = 0.01
RATE = 0.25
CLIP = 0.05
AVERAGE = 0.9


def passed_along(value, axis, steps):
    count = lax.axis_size(axis)
    first, last = (max(0, -steps), min(count, count - steps))
    return lax.ppermute(value, axis, [(source, source + steps) for source in range(first, last)])


def outer_product(left, right):
    return lax.dot_general(
        left, right, (((0,), (0,)), ((), ())), preferred_element_type=jnp.float32
    )


def against(left, right):
    return lax.dot_general(
        left, right, (((1,), (1,)), ((), ())), preferred_element_type=jnp.float32
    )


def joined_input(source, neighbours, counts):
    dest_rows, fanout = neighbours.shape
    keep_mask = jnp.arange(fanout)[None, :] < counts[:, None]
    summed = jnp.sum(
        jnp.where(keep_mask[:, :, None], source[neighbours], jnp.zeros((), source.dtype)),
        axis=1,
        dtype=jnp.float32,
    )
    average_in = (summed / counts[:, None].astype(jnp.float32)).astype(jnp.bfloat16)
    return (jnp.concatenate([source[:dest_rows], average_in], axis=1), keep_mask)


def layer_apply(joined, weight, bias):
    before = jnp.dot(joined, weight, preferred_element_type=jnp.float32) + bias
    return jax.nn.silu(before).astype(jnp.bfloat16)


def layer_back(joined, weight, bias, grad_out):
    before = jnp.dot(joined, weight, preferred_element_type=jnp.float32) + bias
    sigmoid = jax.nn.sigmoid(before)
    return (grad_out.astype(jnp.float32) * sigmoid * (1.0 + before * (1.0 - sigmoid))).astype(
        jnp.bfloat16
    )


def sage_backward(source, neighbours, counts, weight, bias, grad_out):
    joined, keep_mask = joined_input(source, neighbours, counts)
    grad_before = layer_back(joined, weight, bias, grad_out)
    grad_weight = outer_product(joined, grad_before)
    grad_bias = jnp.sum(grad_before.astype(jnp.float32), axis=0)
    dest_rows = neighbours.shape[0]
    feature_width = source.shape[1]
    grad_joined = against(grad_before, weight)
    share_part = grad_joined[:, feature_width:] / counts[:, None].astype(jnp.float32)
    spread = jnp.where(keep_mask[:, :, None], share_part[:, None, :], 0.0)
    grad_source = (
        jnp.zeros(source.shape, jnp.float32).at[:dest_rows].add(grad_joined[:, :feature_width])
    )
    grad_source = grad_source.at[neighbours.reshape(-1)].add(spread.reshape(-1, feature_width))
    return (grad_source.astype(jnp.bfloat16), grad_weight, grad_bias)


def head_pass(hidden_two, weight_head, bias_head, batch_labels, batch_mask, label_count):
    logits = jnp.dot(hidden_two, weight_head, preferred_element_type=jnp.float32) + bias_head
    highest = jnp.max(logits, axis=1, keepdims=True)
    shifted = logits - highest
    log_total = jnp.log(jnp.sum(jnp.exp(shifted), axis=1, keepdims=True))
    chosen = (jnp.arange(logits.shape[1])[None, :] == batch_labels[:, None]).astype(jnp.float32)
    row_weight = batch_mask.astype(jnp.float32)
    loss_part = jnp.sum((log_total[:, 0] - jnp.sum(shifted * chosen, axis=1)) * row_weight)
    grad_logits = (
        (jnp.exp(shifted - log_total) - chosen) * (row_weight / label_count)[:, None]
    ).astype(jnp.bfloat16)
    grad_weight = outer_product(hidden_two, grad_logits)
    grad_bias = jnp.sum(grad_logits.astype(jnp.float32), axis=0)
    grad_hidden = against(grad_logits, weight_head).astype(jnp.bfloat16)
    return (loss_part, grad_weight, grad_bias, grad_hidden)


def moments(weight, gradient, first, second):
    first = BETA_ONE * first + (1.0 - BETA_ONE) * gradient
    second = BETA_TWO * second + (1.0 - BETA_TWO) * gradient * gradient
    update = (
        first / (1.0 - BETA_ONE**STEP) / (jnp.sqrt(second / (1.0 - BETA_TWO**STEP)) + EPSILON)
        + DECAY * weight
    )
    return (first, second, update)


def bias_ratio(weight, update, hidden):
    bounds = ((0, hidden), (hidden, 2 * hidden), (2 * hidden, weight.shape[0]))
    pieces = []
    for start_at, stop_at in bounds:
        weight_norm = jnp.sqrt(jnp.sum(weight[start_at:stop_at] ** 2))
        update_norm = jnp.sqrt(jnp.sum(update[start_at:stop_at] ** 2))
        pieces.append(jnp.zeros((stop_at - start_at,), jnp.float32) + weight_norm / update_norm)
    return jnp.concatenate(pieces)


def hop_forward(values):
    return passed_along(values, "section", 1)


def hop_back(values):
    return passed_along(values, "section", -1)


def on_device(
    node_table,
    owners,
    local_rows,
    inner_neighbours,
    inner_counts,
    outer_neighbours,
    outer_counts,
    labels,
    label_mask,
    weight_inner,
    weight_outer,
    weight_head,
    biases,
    first_inner,
    first_outer,
    first_head,
    first_biases,
    second_inner,
    second_outer,
    second_head,
    second_biases,
    smooth_inner,
    smooth_outer,
    smooth_head,
    smooth_biases,
):
    phase_at = lax.axis_index("section")
    micro_count = inner_neighbours.shape[0]
    dest_count = inner_neighbours.shape[1]
    seed_count = outer_neighbours.shape[1]
    hidden = weight_inner.shape[1]
    classes = weight_head.shape[1]
    feature_width = node_table.shape[1]
    full_inner, full_outer, full_head = (
        lax.all_gather(weight_inner.astype(jnp.bfloat16), ("section", "dp"), axis=0, tiled=True),
        lax.all_gather(weight_outer.astype(jnp.bfloat16), ("section", "dp"), axis=0, tiled=True),
        lax.all_gather(weight_head.astype(jnp.bfloat16), ("section", "dp"), axis=0, tiled=True),
    )
    label_count = jnp.maximum(lax.psum(jnp.sum(label_mask.astype(jnp.float32)), "dp"), 1.0)
    owner_ids = owners.reshape(-1)
    row_ids = local_rows.reshape(-1)
    peer_count = lax.axis_size("dp")
    frontier_rows = owner_ids.shape[0]
    slot_count = max(2, 2 * frontier_rows // peer_count)
    owner_hot = (owner_ids[:, None] == jnp.arange(peer_count)[None, :]).astype(jnp.int32)
    ranking = jnp.sum((jnp.cumsum(owner_hot, axis=0) - 1) * owner_hot, axis=1)
    placed = owner_ids * slot_count + ranking
    request = (
        jnp.zeros((peer_count * slot_count,), jnp.int32)
        .at[placed]
        .set(row_ids)
        .reshape(peer_count, slot_count)
    )
    returned = lax.all_to_all(
        node_table[lax.all_to_all(request, "dp", split_axis=0, concat_axis=0, tiled=True)],
        "dp",
        split_axis=0,
        concat_axis=0,
        tiled=True,
    )
    features = returned.reshape(peer_count * slot_count, -1)[placed]
    bias_inner = biases[:hidden]
    bias_outer = biases[hidden : 2 * hidden]
    bias_head = biases[2 * hidden :]
    all_features = lax.all_gather(features[None], "section", axis=0, tiled=True)

    def expand_all():
        return jnp.stack(
            [
                joined_input(
                    all_features[batch_at], inner_neighbours[batch_at], inner_counts[batch_at]
                )[0]
                for batch_at in range(micro_count)
            ]
        )

    def expand_quiet():
        return jnp.zeros((micro_count, dest_count, 2 * feature_width), jnp.bfloat16)

    joined_all = lax.cond(phase_at == 0, expand_all, expand_quiet)
    arrived_joined = hop_forward(joined_all)

    def inner_forward():
        return jnp.stack(
            [
                layer_apply(arrived_joined[batch_at], full_inner, bias_inner)
                for batch_at in range(micro_count)
            ]
        )

    def inner_quiet():
        return jnp.zeros((micro_count, dest_count, hidden), jnp.bfloat16)

    arrived_one = hop_forward(lax.cond(phase_at == 1, inner_forward, inner_quiet))

    def outer_forward():
        return jnp.stack(
            [
                layer_apply(
                    joined_input(
                        arrived_one[batch_at], outer_neighbours[batch_at], outer_counts[batch_at]
                    )[0],
                    full_outer,
                    bias_outer,
                )
                for batch_at in range(micro_count)
            ]
        )

    def outer_quiet():
        return jnp.zeros((micro_count, seed_count, hidden), jnp.bfloat16)

    arrived_two = hop_forward(lax.cond(phase_at == 2, outer_forward, outer_quiet))

    def head_all():
        results = [
            head_pass(
                arrived_two[batch_at],
                full_head,
                bias_head,
                labels[batch_at],
                label_mask[batch_at],
                label_count,
            )
            for batch_at in range(micro_count)
        ]
        return (
            sum((item[0] for item in results)),
            sum((item[1] for item in results)),
            sum((item[2] for item in results)),
            jnp.stack([item[3] for item in results]),
        )

    def head_quiet():
        return (
            jnp.zeros((), jnp.float32),
            jnp.zeros((hidden, classes), jnp.float32),
            jnp.zeros((classes,), jnp.float32),
            jnp.zeros((micro_count, seed_count, hidden), jnp.bfloat16),
        )

    loss_part, grad_head, grad_bias_head, grad_two = lax.cond(phase_at == 3, head_all, head_quiet)
    back_two = hop_back(grad_two)

    def outer_backward():
        results = [
            sage_backward(
                arrived_one[batch_at],
                outer_neighbours[batch_at],
                outer_counts[batch_at],
                full_outer,
                bias_outer,
                back_two[batch_at],
            )
            for batch_at in range(micro_count)
        ]
        return (
            jnp.stack([item[0] for item in results]),
            sum((item[1] for item in results)),
            sum((item[2] for item in results)),
        )

    def outer_none():
        return (
            jnp.zeros((micro_count, dest_count, hidden), jnp.bfloat16),
            jnp.zeros((2 * hidden, hidden), jnp.float32),
            jnp.zeros((hidden,), jnp.float32),
        )

    grad_one, grad_outer, grad_bias_outer = lax.cond(phase_at == 2, outer_backward, outer_none)
    back_one = hop_back(grad_one)

    def inner_backward():
        pieces = [
            layer_back(arrived_joined[batch_at], full_inner, bias_inner, back_one[batch_at])
            for batch_at in range(micro_count)
        ]
        return (
            jnp.stack(pieces),
            sum((jnp.sum(piece.astype(jnp.float32), axis=0) for piece in pieces)),
        )

    def inner_none():
        return (
            jnp.zeros((micro_count, dest_count, hidden), jnp.bfloat16),
            jnp.zeros((hidden,), jnp.float32),
        )

    grad_pre_one, grad_bias_inner = lax.cond(phase_at == 1, inner_backward, inner_none)
    back_pre = hop_back(grad_pre_one)

    def inner_weight():
        return sum(
            (
                outer_product(joined_all[batch_at], back_pre[batch_at])
                for batch_at in range(micro_count)
            )
        )

    def inner_weight_none():
        return jnp.zeros((2 * feature_width, hidden), jnp.float32)

    grad_inner = lax.cond(phase_at == 0, inner_weight, inner_weight_none)
    shard_inner, shard_outer, shard_head = (
        lax.psum_scatter(grad_inner, ("section", "dp"), scatter_dimension=0, tiled=True),
        lax.psum_scatter(grad_outer, ("section", "dp"), scatter_dimension=0, tiled=True),
        lax.psum_scatter(grad_head, ("section", "dp"), scatter_dimension=0, tiled=True),
    )
    bias_grad, loss_sum = lax.psum(
        (jnp.concatenate([grad_bias_inner, grad_bias_outer, grad_bias_head]), loss_part),
        ("section", "dp"),
    )
    weights = (weight_inner, weight_outer, weight_head)
    shards = (shard_inner, shard_outer, shard_head)
    grad_partial = sum((jnp.sum(shard * shard) for shard in shards))
    weight_partial = jnp.stack([jnp.sum(weight * weight) for weight in weights])
    grad_square = lax.psum(grad_partial, ("section", "dp"))
    clip_norm = jnp.sqrt(grad_square + jnp.sum(bias_grad * bias_grad))
    factor = jnp.minimum(1.0, CLIP / clip_norm)
    firsts = (first_inner, first_outer, first_head)
    seconds = (second_inner, second_outer, second_head)
    smooths = (smooth_inner, smooth_outer, smooth_head)
    states = [
        moments(weights[slot_at], shards[slot_at] * factor, firsts[slot_at], seconds[slot_at])
        for slot_at in range(3)
    ]
    update_square = lax.psum(
        jnp.stack([jnp.sum(state[2] * state[2]) for state in states]), ("section", "dp")
    )
    weight_square = lax.psum(weight_partial, ("section", "dp"))
    weight_norms = jnp.sqrt(weight_square)
    update_norms = jnp.sqrt(update_square)
    news = [
        weights[slot_at]
        - RATE * (weight_norms[slot_at] / update_norms[slot_at]) * states[slot_at][2]
        for slot_at in range(3)
    ]
    averages = [
        AVERAGE * smooths[slot_at] + (1.0 - AVERAGE) * news[slot_at] for slot_at in range(3)
    ]
    bias_first, bias_second, bias_update = moments(
        biases, bias_grad * factor, first_biases, second_biases
    )
    bias_new = biases - RATE * bias_ratio(biases, bias_update, hidden) * bias_update
    bias_average = AVERAGE * smooth_biases + (1.0 - AVERAGE) * bias_new
    return (
        loss_sum,
        label_count,
        clip_norm,
        jnp.stack([weight_norms, update_norms], axis=1),
        news[0],
        news[1],
        news[2],
        bias_new,
        states[0][0],
        states[1][0],
        states[2][0],
        bias_first,
        states[0][1],
        states[1][1],
        states[2][1],
        bias_second,
        averages[0],
        averages[1],
        averages[2],
        bias_average,
    )


def solution(mesh):
    in_specs = (
        P("dp", None),
        P("section", "dp", None),
        P("section", "dp"),
        P(None, "dp", None),
        P(None, "dp"),
        P(None, "dp", None),
        P(None, "dp"),
        P(None, "dp"),
        P(None, "dp"),
        P(("section", "dp"), None),
        P(("section", "dp"), None),
        P(("section", "dp"), None),
        P(),
        P(("section", "dp"), None),
        P(("section", "dp"), None),
        P(("section", "dp"), None),
        P(),
        P(("section", "dp"), None),
        P(("section", "dp"), None),
        P(("section", "dp"), None),
        P(),
        P(("section", "dp"), None),
        P(("section", "dp"), None),
        P(("section", "dp"), None),
        P(),
    )
    out_specs = (
        P(),
        P(),
        P(),
        P(),
        P(("section", "dp"), None),
        P(("section", "dp"), None),
        P(("section", "dp"), None),
        P(),
        P(("section", "dp"), None),
        P(("section", "dp"), None),
        P(("section", "dp"), None),
        P(),
        P(("section", "dp"), None),
        P(("section", "dp"), None),
        P(("section", "dp"), None),
        P(),
        P(("section", "dp"), None),
        P(("section", "dp"), None),
        P(("section", "dp"), None),
        P(),
    )
    return jax.shard_map(
        on_device, mesh=mesh, in_specs=in_specs, out_specs=out_specs, check_vma=False
    )
```

profile of v0, /device:TPU:0, one launch (start us, length us, event | category | flops | bytes accessed | tf_op | source)
XLA Modules:
  0.0 2886.4 jit_solution(9822531091246742138)
XLA Ops:
  11.0 113.0 %scatter_custom_fusion.4 = s32[61440]{0:T(1024)S(1)} fusion(s32[30720]{0:T(1024)S(1)} %bitcast.398, s32[30720]{0:T(1024)} %bitcast.430, s32[]{:T(128)} %constant.231.clone.1), kind=kCustom, calls=%fused_computation.373 | custom fusion | bytes 246272 | tf_op jit(solution)/shard_map/scatter | solution.py:174
  139.8 206.8 %gather_fusion.12 = bf16[61440,128]{1,0:T(8,128)(2,1)} fusion(bf16[16384,128]{1,0:T(8,128)(2,1)} %param.47, s32[61440]{0:T(1024)S(1)} %broadcast_clamp_fusion), kind=kCustom, calls=%fused_computation.12 | custom fusion | bytes 31703040 | tf_op jit(solution)/shard_map/gather | solution.py:178
  352.3 341.1 %all-to-all-done.1 = bf16[8,7680,128]{2,1,0:T(8,128)(2,1)} async-done(((bf16[8,7680,128]{2,1,0:T(8,128)(2,1)}), bf16[8,7680,128]{2,1,0:T(8,128)(2,1)}, u32[]{:S(2)}, u32[]{:S(2)}) %all-to-all-start.1) | async-done | bytes 15728672 | tf_op jit(solution)/shard_map/all_to_all | solution.py:177
  693.4 110.0 %gather_fusion.13 = bf16[30720,128]{1,0:T(8,128)(2,1)} fusion(bf16[61440,128]{1,0:T(8,128)(2,1)} %bitcast.119, s32[30720]{0:T(1024)S(1)} %broadcast_clamp_fusion.1), kind=kCustom, calls=%fused_computation.13 | custom fusion | bytes 15851520 | tf_op jit(solution)/shard_map/gather | solution.py:184
  803.5 278.8 %all-gather.3.cloned.1.call-done = bf16[122880,128]{1,0:T(8,128)(2,1)} async-done(((bf16[30720,128]{1,0:T(8,128)(2,1)}), bf16[122880,128]{1,0:T(8,128)(2,1)}) %all-gather.3.cloned.1.call-update) | async-done | bytes 31457296 | tf_op jit(solution)/shard_map/all_gather | solution.py:188
  1082.2 520.7 %conditional.7 = (bf16[4,2816,256]{2,1,0:T(8,128)(2,1)}) conditional(s32[]{:T(128)} %convert_element_type.427, () %tuple.75, (bf16[4,30720,128]{2,1,0:T(8,128)(2,1)}, s32[4,2816]{1,0:T(4,128)S(1)}, s32[4,2816,15]{1,0,2:T(4,128)S(1)}) %tuple.230), branch_computations={%region_5.6_spmd, %region_6.11_spmd} | conditional | flops 87366656 | bytes 349325472 | solution.py:203
  1082.8 21.4 slice_bitcast_fusion.15
  1113.8 82.0 %gather_fusion.3 = bf16[42240,128]{1,0:T(8,128)(2,1)} fusion(bf16[30720,128]{1,0:T(8,128)(2,1)} %get-tuple-element.288, s32[43008]{0:T(1024)S(1)} %pad_clamp_fusion.4), kind=kCustom, calls=%fused_computation.3 | custom fusion | bytes 21795840 | tf_op jit(solution)/shard_map/cond/branch_1_fun/gather | solution.py:40
  1195.9 16.7 reshape.1215
  1214.4 17.2 convert_reduce_fusion.12
  1239.4 82.0 %gather_fusion.2 = bf16[42240,128]{1,0:T(8,128)(2,1)} fusion(bf16[30720,128]{1,0:T(8,128)(2,1)} %get-tuple-element.286, s32[43008]{0:T(1024)S(1)} %pad_clamp_fusion.5), kind=kCustom, calls=%fused_computation.2 | custom fusion | bytes 21795840 | tf_op jit(solution)/shard_map/cond/branch_1_fun/gather | solution.py:40
  1321.5 16.7 reshape.1207
  1338.2 17.5 convert_reduce_fusion.13
  1359.8 82.0 %gather_fusion.1 = bf16[42240,128]{1,0:T(8,128)(2,1)} fusion(bf16[30720,128]{1,0:T(8,128)(2,1)} %get-tuple-element.287, s32[43008]{0:T(1024)S(1)} %pad_clamp_fusion.6), kind=kCustom, calls=%fused_computation.1 | custom fusion | bytes 21795840 | tf_op jit(solution)/shard_map/cond/branch_1_fun/gather | solution.py:40
  1441.8 16.7 reshape.1199
  1460.2 17.3 convert_reduce_fusion.14
  1481.9 82.0 %gather_fusion = bf16[42240,128]{1,0:T(8,128)(2,1)} fusion(bf16[30720,128]{1,0:T(8,128)(2,1)} %get-tuple-element.285, s32[43008]{0:T(1024)S(1)} %pad_clamp_fusion.7), kind=kCustom, calls=%fused_computation | custom fusion | bytes 21795840 | tf_op jit(solution)/shard_map/cond/branch_1_fun/gather | solution.py:40
  1563.9 16.7 reshape.1191
  1580.6 17.3 convert_reduce_fusion.15
  1606.8 38.7 %all_gather.13 = bf16[256,256]{1,0:T(8,128)(2,1)S(1)} all-gather(bf16[8,256]{1,0:T(8,128)(2,1)S(1)} %convert_element_type.429), channel_id=1, replica_groups=mesh['section'=4,'dp'=8] {'section','dp'}, dimensions={0}, use_global_device_ids=true | all-gather | bytes 135168 | tf_op jit(solution)/shard_map/all_gather | solution.py:158
  1646.7 82.4 %collective-permute-done = bf16[4,2816,256]{2,1,0:T(8,128)(2,1)} collective-permute-done((bf16[4,2816,256]{2,1,0:T(8,128)(2,1)}, bf16[4,2816,256]{2,1,0:T(8,128)(2,1)}, u32[]{:S(2)}, u32[]{:S(2)}) %collective-permute-start) | collective-permute-done | bytes 5767200 | tf_op jit(solution)/shard_map/ppermute | solution.py:21
  1732.0 16.4 collective-permute-start.1
  1748.4 41.2 %all_gather.14 = bf16[512,256]{1,0:T(8,128)(2,1)} all-gather(bf16[16,256]{1,0:T(8,128)(2,1)S(1)} %convert_element_type.430), channel_id=1, replica_groups=mesh['section'=4,'dp'=8] {'section','dp'}, dimensions={0}, use_global_device_ids=true | all-gather | bytes 270336 | tf_op jit(solution)/shard_map/all_gather | solution.py:159
  1789.5 80.9 %collective-permute-done.1 = bf16[4,2816,256]{2,1,0:T(8,128)(2,1)} collective-permute-done((bf16[4,2816,256]{2,1,0:T(8,128)(2,1)}, bf16[4,2816,256]{2,1,0:T(8,128)(2,1)}, u32[]{:S(2)}, u32[]{:S(2)}) %collective-permute-start.1) | collective-permute-done | bytes 5767200 | tf_op jit(solution)/shard_map/ppermute | solution.py:21
  1892.8 103.8 %all_gather.15 = bf16[256,172]{1,0:T(8,128)(2,1)S(1)} all-gather(bf16[8,172]{1,0:T(8,128)(2,1)S(1)} %convert_element_type.431), channel_id=1, replica_groups=mesh['section'=4,'dp'=8] {'section','dp'}, dimensions={0}, use_global_device_ids=true | all-gather | bytes 90816 | tf_op jit(solution)/shard_map/all_gather | solution.py:160
  1999.1 16.1 collective-permute-done.3
  2026.2 129.8 %collective-permute-done.4 = bf16[4,2816,256]{2,1,0:T(8,128)(2,1)S(1)} collective-permute-done((bf16[4,2816,256]{2,1,0:T(8,128)(2,1)S(1)}, bf16[4,2816,256]{2,1,0:T(8,128)(2,1)S(1)}, u32[]{:S(2)}, u32[]{:S(2)}) %collective-permute-start.4) | collective-permute-done | bytes 5767200 | tf_op jit(solution)/shard_map/ppermute | solution.py:21
  2161.8 338.9 %collective-permute-done.5 = bf16[4,2816,256]{2,1,0:T(8,128)(2,1)} collective-permute-done((bf16[4,2816,256]{2,1,0:T(8,128)(2,1)}, bf16[4,2816,256]{2,1,0:T(8,128)(2,1)}, u32[]{:S(2)}, u32[]{:S(2)}) %collective-permute-start.5) | collective-permute-done | bytes 5767200 | tf_op jit(solution)/shard_map/ppermute | solution.py:21
  2513.2 126.7 %reduce-scatter.6.cloned.1.call-done = f32[16,256]{1,0:T(8,128)} async-done(((f32[512,256]{1,0:T(8,128)}), f32[16,256]{1,0:T(8,128)}) %reduce-scatter.6.cloned.1.call-update) | async-done | bytes 16400 | tf_op jit(solution)/shard_map/reduce_scatter | solution.py:329
  2641.3 130.5 %reduce-scatter.4.cloned.1.call-done = f32[8,256]{1,0:T(8,128)} async-done(((f32[256,256]{1,0:T(8,128)}), f32[8,256]{1,0:T(8,128)}) %reduce-scatter.4.cloned.1.call-update) | async-done | bytes 8208 | tf_op jit(solution)/shard_map/reduce_scatter | solution.py:328
  2775.7 37.0 %all-reduce.7 = (f32[]{:T(128)}, f32[684]{0:T(1024)S(1)}) all-reduce(f32[]{:T(128)S(6)} %add.622, f32[684]{0:T(1024)S(1)} %pad_maximum_fusion.18), channel_id=1, replica_groups=mesh['section'=4,'dp'=8] {'section','dp'}, use_global_device_ids=true, to_apply=%region_72.73 | all-reduce | flops 685 | bytes 5480 | tf_op jit(solution)/shard_map/psum | solution.py:340
  2824.7 42.3 %all-reduce.6 = (f32[]{:T(128)}, f32[3]{0:T(128)S(1)}, f32[3]{0:T(128)S(1)}) all-reduce(f32[]{:T(128)} %get-tuple-element.176, f32[3]{0:T(128)S(1)} %pad_maximum_fusion.21, f32[3]{0:T(128)S(1)} %pad_maximum_fusion.20), channel_id=1, replica_groups=mesh['section'=4,'dp'=8] {'section','dp'}, use_global_device_ids=true, to_apply=%region_43.44 | all-reduce | flops 7 | bytes 56 | tf_op jit(solution)/shard_map/psum | solution.py:332
  (207 shorter events, 152.5 us)
Async XLA Ops:
  346.6 346.8 %all-to-all-start.1 = ((bf16[8,7680,128]{2,1,0:T(8,128)(2,1)}), bf16[8,7680,128]{2,1,0:T(8,128)(2,1)}, u32[]{:S(2)}, u32[]{:S(2)}) async-start(bf16[8,7680,128]{2,1,0:T(8,128)(2,1)} %bitcast.387), calls=%async_computation.1 | async-start | bytes 31457280 | tf_op jit(solution)/shard_map/all_to_all | solution.py:177
  352.2 730.0 %all-gather.3.cloned.1.call-start = ((), (), s32[]{:S(2)}) async-start(), calls=%async_computation.8 | async-start | bytes 39321600 | tf_op jit(solution)/shard_map/all_gather | solution.py:188
  803.4 278.8 %copy-start.12 = (s32[4,2816,15]{1,0,2:T(4,128)S(1)}, s32[4,2816,15]{1,0,2:T(4,128)}, u32[]{:S(2)}) copy-start(s32[4,2816,15]{1,0,2:T(4,128)} %param.50) | copy-start | bytes 2027524
  803.4 278.8 %copy-start.58 = (s32[4,2816]{1,0:T(4,128)S(1)}, s32[4,2816]{1,0:T(4,128)}, u32[]{:S(2)}) copy-start(s32[4,2816]{1,0:T(4,128)} %param.51) | copy-start | bytes 135172
  803.4 1708.5 %reduce-scatter.8.cloned.1.call-start = ((), (), s32[]{:S(2)}) async-start(), calls=%async_computation.7 | async-start | bytes 270336 | tf_op jit(solution)/shard_map/reduce_scatter | solution.py:330
  1082.2 524.5 %copy-start.52 = (f32[8,256]{1,0:T(8,128)S(1)}, f32[8,256]{1,0:T(8,128)}, u32[]{:S(2)}) copy-start(f32[8,256]{1,0:T(8,128)} %param.56) | copy-start | bytes 24580
  1082.2 563.2 %copy-start.63 = (f32[684]{0:T(1024)S(1)}, f32[684]{0:T(1024)}, u32[]{:S(2)}) copy-start(f32[684]{0:T(1024)} %param.59) | copy-start | bytes 8212
  1603.0 126.1 %collective-permute-start = (bf16[4,2816,256]{2,1,0:T(8,128)(2,1)}, bf16[4,2816,256]{2,1,0:T(8,128)(2,1)}, u32[]{:S(2)}, u32[]{:S(2)}) collective-permute-start(bf16[4,2816,256]{2,1,0:T(8,128)(2,1)} %get-tuple-element.403), channel_id=1, source_target_pairs={{0,8},{8,16},{16,24},{1,9},{9,17},{17,25},{2,10},{10,18},{18,26},{... | collective-permute-start | bytes 17301512 | tf_op jit(solution)/shard_map/ppermute | solution.py:21
  1729.1 141.4 %copy-start.43 = (s32[4,256,10]{1,0,2:T(4,128)S(1)}, s32[4,256,10]{1,0,2:T(4,128)}, u32[]{:S(2)}) copy-start(s32[4,256,10]{1,0,2:T(4,128)} %param.52) | copy-start | bytes 122884
  1729.1 141.4 %copy-start.66 = (s32[4,256]{1,0:T(4,128)S(1)}, s32[4,256]{1,0:T(4,128)}, u32[]{:S(2)}) copy-start(s32[4,256]{1,0:T(4,128)} %param.53) | copy-start | bytes 12292
  1732.0 138.5 %collective-permute-start.1 = (bf16[4,2816,256]{2,1,0:T(8,128)(2,1)}, bf16[4,2816,256]{2,1,0:T(8,128)(2,1)}, u32[]{:S(2)}, u32[]{:S(2)}) collective-permute-start(bf16[4,2816,256]{2,1,0:T(8,128)(2,1)} %get-tuple-element.404), channel_id=1, source_target_pairs={{0,8},{8,16},{16,24},{1,9},{9,17},{17,25},{2,10},{10,18},{18,26},{... | collective-permute-start | bytes 17301512 | tf_op jit(solution)/shard_map/ppermute | solution.py:21
  1871.6 125.6 %collective-permute-start.2 = (bf16[4,256,256]{2,1,0:T(8,128)(2,1)}, bf16[4,256,256]{2,1,0:T(8,128)(2,1)S(1)}, u32[]{:S(2)}, u32[]{:S(2)}) collective-permute-start(bf16[4,256,256]{2,1,0:T(8,128)(2,1)} %copy-done.13), channel_id=1, source_target_pairs={{0,8},{8,16},{16,24},{1,9},{9,17},{17,25},{2,10},{10,18},{18,26},{... | collective-permute-start | bytes 1572872 | tf_op jit(solution)/shard_map/ppermute | solution.py:21
  1997.8 17.4 collective-permute-start.3
  2024.9 131.1 %collective-permute-start.4 = (bf16[4,2816,256]{2,1,0:T(8,128)(2,1)S(1)}, bf16[4,2816,256]{2,1,0:T(8,128)(2,1)S(1)}, u32[]{:S(2)}, u32[]{:S(2)}) collective-permute-start(bf16[4,2816,256]{2,1,0:T(8,128)(2,1)S(1)} %get-tuple-element.178), channel_id=1, source_target_pairs={{8,0},{16,8},{24,16},{9,1},{17,9},{25,17},{10,2},{18,10},{26,18},{... | collective-permute-start | bytes 17301512 | tf_op jit(solution)/shard_map/ppermute | solution.py:21
  2158.9 341.8 %collective-permute-start.5 = (bf16[4,2816,256]{2,1,0:T(8,128)(2,1)}, bf16[4,2816,256]{2,1,0:T(8,128)(2,1)}, u32[]{:S(2)}, u32[]{:S(2)}) collective-permute-start(bf16[4,2816,256]{2,1,0:T(8,128)(2,1)} %get-tuple-element.179), channel_id=1, source_target_pairs={{8,0},{16,8},{24,16},{9,1},{17,9},{25,17},{10,2},{18,10},{26,18},{... | collective-permute-start | bytes 17301512 | tf_op jit(solution)/shard_map/ppermute | solution.py:21
  2161.0 478.9 %reduce-scatter.6.cloned.1.call-start = ((), (), s32[]{:S(2)}) async-start(), calls=%async_computation.6 | async-start | bytes 540672 | tf_op jit(solution)/shard_map/reduce_scatter | solution.py:329
  2161.8 610.0 %reduce-scatter.4.cloned.1.call-start = ((), (), s32[]{:S(2)}) async-start(), calls=%async_computation.5 | async-start | bytes 270336 | tf_op jit(solution)/shard_map/reduce_scatter | solution.py:328
  2500.7 314.0 %copy-start.80 = (f32[684]{0:T(1024)S(1)}, f32[684]{0:T(1024)}, u32[]{:S(2)}) copy-start(f32[684]{0:T(1024)} %param.63) | copy-start | bytes 8212
  2500.7 314.0 %copy-start.81 = (f32[684]{0:T(1024)S(1)}, f32[684]{0:T(1024)}, u32[]{:S(2)}) copy-start(f32[684]{0:T(1024)} %param.67) | copy-start | bytes 8212
  2500.7 315.9 %copy-start.55 = (f32[8,172]{1,0:T(8,128)S(1)}, f32[8,172]{1,0:T(8,128)}, u32[]{:S(2)}) copy-start(f32[8,172]{1,0:T(8,128)} %param.58) | copy-start | bytes 16516
  2500.7 315.9 %copy-start.74 = (f32[8,172]{1,0:T(8,128)S(1)}, f32[8,172]{1,0:T(8,128)}, u32[]{:S(2)}) copy-start(f32[8,172]{1,0:T(8,128)} %param.62) | copy-start | bytes 16516
  2500.7 315.8 %copy-start.75 = (f32[8,172]{1,0:T(8,128)S(1)}, f32[8,172]{1,0:T(8,128)}, u32[]{:S(2)}) copy-start(f32[8,172]{1,0:T(8,128)} %param.66) | copy-start | bytes 16516
  2500.7 317.2 %copy-start.46 = (f32[16,256]{1,0:T(8,128)S(1)}, f32[16,256]{1,0:T(8,128)}, u32[]{:S(2)}) copy-start(f32[16,256]{1,0:T(8,128)} %param.57) | copy-start | bytes 49156
  2500.7 317.2 %copy-start.64 = (f32[16,256]{1,0:T(8,128)S(1)}, f32[16,256]{1,0:T(8,128)}, u32[]{:S(2)}) copy-start(f32[16,256]{1,0:T(8,128)} %param.61) | copy-start | bytes 49156
  2500.7 317.1 %copy-start.65 = (f32[16,256]{1,0:T(8,128)S(1)}, f32[16,256]{1,0:T(8,128)}, u32[]{:S(2)}) copy-start(f32[16,256]{1,0:T(8,128)} %param.65) | copy-start | bytes 49156
  2500.8 318.5 %copy-start.53 = (f32[8,256]{1,0:T(8,128)S(1)}, f32[8,256]{1,0:T(8,128)}, u32[]{:S(2)}) copy-start(f32[8,256]{1,0:T(8,128)} %param.56) | copy-start | bytes 24580
  2500.8 318.5 %copy-start.76 = (f32[8,256]{1,0:T(8,128)S(1)}, f32[8,256]{1,0:T(8,128)}, u32[]{:S(2)}) copy-start(f32[8,256]{1,0:T(8,128)} %param.60) | copy-start | bytes 24580
  2500.8 318.5 %copy-start.77 = (f32[8,256]{1,0:T(8,128)S(1)}, f32[8,256]{1,0:T(8,128)}, u32[]{:S(2)}) copy-start(f32[8,256]{1,0:T(8,128)} %param.64) | copy-start | bytes 24580
  2500.8 374.0 %copy-start.78 = (f32[8,256]{1,0:T(8,128)S(1)}, f32[8,256]{1,0:T(8,128)}, u32[]{:S(2)}) copy-start(f32[8,256]{1,0:T(8,128)} %param.68) | copy-start | bytes 24580
  2500.8 374.6 %copy-start.68 = (f32[16,256]{1,0:T(8,128)S(1)}, f32[16,256]{1,0:T(8,128)}, u32[]{:S(2)}) copy-start(f32[16,256]{1,0:T(8,128)} %param.69) | copy-start | bytes 49156
  2500.8 375.3 %copy-start.79 = (f32[8,172]{1,0:T(8,128)S(1)}, f32[8,172]{1,0:T(8,128)}, u32[]{:S(2)}) copy-start(f32[8,172]{1,0:T(8,128)} %param.70) | copy-start | bytes 16516
  2500.8 375.9 %copy-start.82 = (f32[684]{0:T(1024)S(1)}, f32[684]{0:T(1024)}, u32[]{:S(2)}) copy-start(f32[684]{0:T(1024)} %param.71) | copy-start | bytes 8212
  (26 other events, 1090.8 us)
Sparse Core Ops, SparseCore 0:
  803.5 278.6 all-gather.2
  2161.1 346.3 reduce-scatter.7
  2509.9 129.9 reduce-scatter.5
  2642.0 129.7 reduce-scatter.3
where the time goes:
time: 2900 us; the launch traced here: 2890 us
  waiting for transfers between devices  1530 us (53%)
  local copies, waits for them, and re-layouts  875 us (30%)
  blocking collectives  293 us (10%)
  other arithmetic  110 us (4%)
  starting transfers between devices  34.2 us (1%)
    ppermute x6, waiting for transfers between devices, passed_along(): lax.ppermute(value, axis, [(source, source + steps) for source in range(f...  648 us
    gather x8, local copies, waits for them, and re-layouts, joined_input(): source[neighbours]  395 us
    all_to_all x1, waiting for transfers between devices, on_device(): lax.all_to_all(node_table[lax.all_to_all(request, 'dp', split_axis=0, con...  341 us
    all_gather x1, waiting for transfers between devices, on_device(): all_features = lax.all_gather(features[None], 'section', axis=0, tiled=True)  279 us
    gather x1, local copies, waits for them, and re-layouts, on_device(): node_table[lax.all_to_all(request, 'dp', split_axis=0, concat_axis=0, til...  207 us
    reduce_scatter x1, waiting for transfers between devices, on_device(): lax.psum_scatter(grad_inner, ('section', 'dp'), scatter_dimension=0, tile...  130 us
    reduce_scatter x1, waiting for transfers between devices, on_device(): lax.psum_scatter(grad_outer, ('section', 'dp'), scatter_dimension=0, tile...  127 us
    scatter x1, local copies, waits for them, and re-layouts, on_device(): request = jnp.zeros((peer_count * slot_count,), jnp.int32).at[placed].set...  113 us
  transfers between devices with their start and end apart: 11, of which 9 were waited for; matrix products, arithmetic and copies ran while one was open for 1% of the time, Pallas kernels for 0%

commit v1 on v0

v1 whole, which is shorter than its diff:
```python
import jax
import jax.numpy as jnp
from jax import lax
from jax.sharding import PartitionSpec as P

STEP = 5


BETA_ONE = 0.9
BETA_TWO = 0.999
EPSILON = 1e-06
DECAY = 0.01
RATE = 0.25
CLIP = 0.05
AVERAGE = 0.9

WHOLE_TABLE_LIMIT = 64 * 2**20


def outer_product(left, right):
    return lax.dot_general(
        left, right, (((0,), (0,)), ((), ())), preferred_element_type=jnp.float32
    )


def against(left, right):
    return lax.dot_general(
        left, right, (((1,), (1,)), ((), ())), preferred_element_type=jnp.float32
    )


def silu_slope(before, grad_out):
    sigmoid = jax.nn.sigmoid(before)
    return (grad_out * sigmoid * (1.0 + before * (1.0 - sigmoid))).astype(jnp.bfloat16)


def moments(weight, gradient, first, second):
    first = BETA_ONE * first + (1.0 - BETA_ONE) * gradient
    second = BETA_TWO * second + (1.0 - BETA_TWO) * gradient * gradient
    update = (
        first / (1.0 - BETA_ONE**STEP) / (jnp.sqrt(second / (1.0 - BETA_TWO**STEP)) + EPSILON)
        + DECAY * weight
    )
    return (first, second, update)


def bias_ratio(weight, update, hidden):
    bounds = ((0, hidden), (hidden, 2 * hidden), (2 * hidden, weight.shape[0]))
    pieces = []
    for start_at, stop_at in bounds:
        weight_norm = jnp.sqrt(jnp.sum(weight[start_at:stop_at] ** 2))
        update_norm = jnp.sqrt(jnp.sum(update[start_at:stop_at] ** 2))
        pieces.append(jnp.zeros((stop_at - start_at,), jnp.float32) + weight_norm / update_norm)
    return jnp.concatenate(pieces)


def gathered_rows(node_table, owner_ids, row_ids):
    peer_count = lax.axis_size("dp")
    parts = lax.axis_size("section")
    table_rows = node_table.shape[0]
    if peer_count * node_table.size * 2 <= WHOLE_TABLE_LIMIT and table_rows % parts == 0:
        part_rows = table_rows // parts
        quarter = lax.dynamic_slice_in_dim(
            node_table, lax.axis_index("section") * part_rows, part_rows, 0
        )
        source = lax.all_gather(quarter, ("section", "dp"), axis=0, tiled=True)
        place = (row_ids // part_rows * peer_count + owner_ids) * part_rows + row_ids % part_rows
        return source, place
    frontier_rows = owner_ids.shape[0]
    slot_count = max(2, 2 * frontier_rows // peer_count)
    owner_hot = (owner_ids[:, None] == jnp.arange(peer_count)[None, :]).astype(jnp.int32)
    ranking = jnp.sum((jnp.cumsum(owner_hot, axis=0) - 1) * owner_hot, axis=1)
    placed = owner_ids * slot_count + ranking
    request = (
        jnp.zeros((peer_count * slot_count,), jnp.int32)
        .at[placed]
        .set(row_ids)
        .reshape(peer_count, slot_count)
    )
    returned = lax.all_to_all(
        node_table[lax.all_to_all(request, "dp", split_axis=0, concat_axis=0, tiled=True)],
        "dp",
        split_axis=0,
        concat_axis=0,
        tiled=True,
    )
    return returned.reshape(peer_count * slot_count, -1), placed


def on_device(
    node_table,
    owners,
    local_rows,
    inner_neighbours,
    inner_counts,
    outer_neighbours,
    outer_counts,
    labels,
    label_mask,
    weight_inner,
    weight_outer,
    weight_head,
    biases,
    first_inner,
    first_outer,
    first_head,
    first_biases,
    second_inner,
    second_outer,
    second_head,
    second_biases,
    smooth_inner,
    smooth_outer,
    smooth_head,
    smooth_biases,
):
    at = lax.axis_index("section")
    every = ("section", "dp")
    hidden = weight_inner.shape[1]
    dest_count, fan_inner = inner_neighbours.shape[1:]
    seed_count, fan_outer = outer_neighbours.shape[1:]
    classes = weight_head.shape[1]
    label_count = jnp.maximum(lax.psum(jnp.sum(label_mask.astype(jnp.float32)), "dp"), 1.0)

    def mine(array):
        return lax.dynamic_index_in_dim(array, at, 0, keepdims=False)

    inner_neighbours, inner_counts = mine(inner_neighbours), mine(inner_counts)
    outer_neighbours, outer_counts = mine(outer_neighbours), mine(outer_counts)
    labels, label_mask = mine(labels), mine(label_mask)
    sizes = [weight.shape[0] for weight in (weight_inner, weight_outer, weight_head)]
    full_inner, full_outer, full_head = (
        lax.all_gather(weight.astype(jnp.bfloat16), every, axis=0, tiled=True)
        for weight in (weight_inner, weight_outer, weight_head)
    )
    bias_inner = biases[:hidden]
    bias_outer = biases[hidden : 2 * hidden]
    bias_head = biases[2 * hidden :]

    source, place = gathered_rows(node_table, owners.reshape(-1), local_rows.reshape(-1))
    keep = jnp.arange(fan_inner)[None, :] < inner_counts[:, None]
    rows = source[place[inner_neighbours]]
    summed = jnp.sum(
        jnp.where(keep[:, :, None], rows, jnp.zeros((), rows.dtype)), axis=1, dtype=jnp.float32
    )
    mean_one = (summed / inner_counts[:, None].astype(jnp.float32)).astype(jnp.bfloat16)
    joined_one = jnp.concatenate([source[place[:dest_count]], mean_one], axis=1)
    pre_one = jnp.dot(joined_one, full_inner, preferred_element_type=jnp.float32) + bias_inner
    hidden_one = jax.nn.silu(pre_one).astype(jnp.bfloat16)

    keep_outer = jnp.arange(fan_outer)[None, :] < outer_counts[:, None]
    pick = jnp.sum(
        (
            jnp.where(keep_outer, outer_neighbours, -1)[:, :, None]
            == jnp.arange(dest_count)[None, None, :]
        ).astype(jnp.float32),
        axis=1,
    ).astype(jnp.bfloat16)
    count_two = outer_counts[:, None].astype(jnp.float32)
    mean_two = (jnp.dot(pick, hidden_one, preferred_element_type=jnp.float32) / count_two).astype(
        jnp.bfloat16
    )
    joined_two = jnp.concatenate([hidden_one[:seed_count], mean_two], axis=1)
    pre_two = jnp.dot(joined_two, full_outer, preferred_element_type=jnp.float32) + bias_outer
    hidden_two = jax.nn.silu(pre_two).astype(jnp.bfloat16)

    logits = jnp.dot(hidden_two, full_head, preferred_element_type=jnp.float32) + bias_head
    shifted = logits - jnp.max(logits, axis=1, keepdims=True)
    log_total = jnp.log(jnp.sum(jnp.exp(shifted), axis=1, keepdims=True))
    chosen = (jnp.arange(classes)[None, :] == labels[:, None]).astype(jnp.float32)
    row_weight = label_mask.astype(jnp.float32)
    loss_part = jnp.sum((log_total[:, 0] - jnp.sum(shifted * chosen, axis=1)) * row_weight)
    grad_logits = (
        (jnp.exp(shifted - log_total) - chosen) * (row_weight / label_count)[:, None]
    ).astype(jnp.bfloat16)
    grad_head = outer_product(hidden_two, grad_logits)
    grad_two = against(grad_logits, full_head).astype(jnp.bfloat16).astype(jnp.float32)
    grad_pre_two = silu_slope(pre_two, grad_two)
    grad_outer = outer_product(joined_two, grad_pre_two)
    grad_joined = against(grad_pre_two, full_outer)
    share = grad_joined[:, hidden:] / count_two
    share_high = share.astype(jnp.bfloat16)
    share_low = (share - share_high.astype(jnp.float32)).astype(jnp.bfloat16)
    grad_one = outer_product(pick, share_high) + outer_product(pick, share_low)
    grad_one = jnp.concatenate(
        [grad_one[:seed_count] + grad_joined[:, :hidden], grad_one[seed_count:]], axis=0
    )
    grad_one = grad_one.astype(jnp.bfloat16).astype(jnp.float32)
    grad_pre_one = silu_slope(pre_one, grad_one)
    grad_inner = outer_product(joined_one, grad_pre_one)
    bias_part = jnp.concatenate(
        [
            jnp.sum(part.astype(jnp.float32), axis=0)
            for part in (grad_pre_one, grad_pre_two, grad_logits)
        ]
    )

    devices = lax.axis_size(every)
    grads = jnp.concatenate(
        [grad.reshape(devices, -1) for grad in (grad_inner, grad_outer, grad_head)], axis=1
    )
    shard = lax.psum_scatter(grads, every, scatter_dimension=0, tiled=True).reshape(-1)
    weights = (weight_inner, weight_outer, weight_head)
    shards = []
    for weight in weights:
        shards.append(shard[: weight.size].reshape(weight.shape))
        shard = shard[weight.size :]
    packed = lax.psum(jnp.concatenate([bias_part, loss_part[None]]), every)
    bias_grad, loss_sum = packed[:-1], packed[-1]
    grad_partial = sum((jnp.sum(part * part) for part in shards))
    weight_partial = [jnp.sum(weight * weight) for weight in weights]
    squares = lax.psum(jnp.stack([grad_partial] + weight_partial), every)
    clip_norm = jnp.sqrt(squares[0] + jnp.sum(bias_grad * bias_grad))
    factor = jnp.minimum(1.0, CLIP / clip_norm)
    firsts = (first_inner, first_outer, first_head)
    seconds = (second_inner, second_outer, second_head)
    smooths = (smooth_inner, smooth_outer, smooth_head)
    states = [
        moments(weights[slot_at], shards[slot_at] * factor, firsts[slot_at], seconds[slot_at])
        for slot_at in range(3)
    ]
    update_square = lax.psum(jnp.stack([jnp.sum(state[2] * state[2]) for state in states]), every)
    weight_norms = jnp.sqrt(squares[1:])
    update_norms = jnp.sqrt(update_square)
    news = [
        weights[slot_at]
        - RATE * (weight_norms[slot_at] / update_norms[slot_at]) * states[slot_at][2]
        for slot_at in range(3)
    ]
    averages = [
        AVERAGE * smooths[slot_at] + (1.0 - AVERAGE) * news[slot_at] for slot_at in range(3)
    ]
    bias_first, bias_second, bias_update = moments(
        biases, bias_grad * factor, first_biases, second_biases
    )
    bias_new = biases - RATE * bias_ratio(biases, bias_update, hidden) * bias_update
    bias_average = AVERAGE * smooth_biases + (1.0 - AVERAGE) * bias_new
    return (
        loss_sum,
        label_count,
        clip_norm,
        jnp.stack([weight_norms, update_norms], axis=1),
        news[0],
        news[1],
        news[2],
        bias_new,
        states[0][0],
        states[1][0],
        states[2][0],
        bias_first,
        states[0][1],
        states[1][1],
        states[2][1],
        bias_second,
        averages[0],
        averages[1],
        averages[2],
        bias_average,
    )


def solution(mesh):
    in_specs = (
        P("dp", None),
        P("section", "dp", None),
        P("section", "dp"),
        P(None, "dp", None),
        P(None, "dp"),
        P(None, "dp", None),
        P(None, "dp"),
        P(None, "dp"),
        P(None, "dp"),
        P(("section", "dp"), None),
        P(("section", "dp"), None),
        P(("section", "dp"), None),
        P(),
        P(("section", "dp"), None),
        P(("section", "dp"), None),
        P(("section", "dp"), None),
        P(),
        P(("section", "dp"), None),
        P(("section", "dp"), None),
        P(("section", "dp"), None),
        P(),
        P(("section", "dp"), None),
        P(("section", "dp"), None),
        P(("section", "dp"), None),
        P(),
    )
    out_specs = (
        P(),
        P(),
        P(),
        P(),
        P(("section", "dp"), None),
        P(("section", "dp"), None),
        P(("section", "dp"), None),
        P(),
        P(("section", "dp"), None),
        P(("section", "dp"), None),
        P(("section", "dp"), None),
        P(),
        P(("section", "dp"), None),
        P(("section", "dp"), None),
        P(("section", "dp"), None),
        P(),
        P(("section", "dp"), None),
        P(("section", "dp"), None),
        P(("section", "dp"), None),
        P(),
    )
    return jax.shard_map(
        on_device, mesh=mesh, in_specs=in_specs, out_specs=out_specs, check_vma=False
    )
```

time: 2900 us -> 895 us (0.31)
  waiting for transfers between devices: 1530 us -> 124 us
  local copies, waits for them, and re-layouts: 875 us -> 464 us
  blocking collectives: 293 us -> 212 us
  other arithmetic: 110 us -> 56.1 us
  starting transfers between devices: 34.2 us -> 0.08 us
    ppermute x6 -> x0, waiting for transfers between devices: 648 us -> none  [passed_along(): lax.ppermute(value, axis, [(source, source + steps) for source in range(f...]
    all_to_all x1 -> x0, waiting for transfers between devices: 341 us -> none  [on_device(): lax.all_to_all(node_table[lax.all_to_all(request, 'dp', split_axis=0, con...]
    all_gather x1, waiting for transfers between devices: 279 us -> 0.02 us  [gathered_rows(): source = lax.all_gather(quarter, ('section', 'dp'), axis=0, tiled=True)]
    gather x10 -> x5, local copies, waits for them, and re-layouts: 712 us -> 450 us  [the longest x4 435 us: on_device(): rows = source[place[inner_neighbours]]]
    reduce_scatter x3 -> x0, waiting for transfers between devices: 257 us -> none  [the longest x1 130 us: on_device(): lax.psum_scatter(grad_inner, ('section', 'dp'), scatter_dimension=0, tile...]
    unnamed x4 -> x3, waiting for transfers between devices: 0.73 us -> 124 us
    scatter x1 -> x0, local copies, waits for them, and re-layouts: 113 us -> none  [on_device(): request = jnp.zeros((peer_count * slot_count,), jnp.int32).at[placed].set...]
    all_gather x3, blocking collectives: 184 us -> 113 us  [on_device(): lax.all_gather(weight.astype(jnp.bfloat16), every, axis=0, tiled=True)]
  transfers between devices with their start and end apart: 11 -> 2, of which waited for: 9 -> 1; matrix products, arithmetic and copies ran while one was open for 1% -> 27% of each run, Pallas kernels for 0% -> 0%
where the time goes in v1:
time: 895 us; the launch traced here: 893 us
  local copies, waits for them, and re-layouts  464 us (52%)
  blocking collectives  212 us (24%)
  waiting for transfers between devices  124 us (14%)
  other arithmetic  56.1 us (6%)
  between operations  28.5 us (3%)
    gather x4, local copies, waits for them, and re-layouts, on_device(): rows = source[place[inner_neighbours]]  435 us
    unnamed x3, waiting for transfers between devices  124 us
    all_gather x3, blocking collectives, on_device(): lax.all_gather(weight.astype(jnp.bfloat16), every, axis=0, tiled=True)  113 us
    psum x1, blocking collectives, on_device(): packed = lax.psum(jnp.concatenate([bias_part, loss_part[None]]), every)  40.5 us
    psum x1, blocking collectives, on_device(): lax.psum(jnp.stack([jnp.sum(state[2] * state[2]) for state in states]), e...  39.9 us
    psum x1, blocking collectives, on_device(): lax.psum(jnp.sum(label_mask.astype(jnp.float32)), 'dp')  18.8 us
  transfers between devices with their start and end apart: 2, of which 1 were waited for; matrix products, arithmetic and copies ran while one was open for 27% of the time, Pallas kernels for 0%

profile of v1, /device:TPU:0, one launch (start us, length us, event | category | flops | bytes accessed | tf_op | source)
XLA Modules:
  0.0 892.9 jit_solution(12380588611474835535)
XLA Ops:
  7.3 2.3 constant_dynamic-slice_fusion.3
  10.3 18.8 %psum.28 = f32[]{:T(128)} all-reduce(f32[]{:T(128)} %convert_reduce_fusion.5), channel_id=1, replica_groups=mesh['section'=4,'dp'=8] {'dp'}, use_global_device_ids=true, to_apply=%region_5.6 | all-reduce | flops 1 | bytes 8 | tf_op jit(solution)/shard_map/psum | solution.py:123
  30.9 0.8 dynamic-slice_reduce_fusion
  33.5 1.3 compare_select_fusion.1
  34.8 2.4 reshape.223
  37.4 216.3 %gather_fusion.1 = s32[42240]{0:T(1024)S(1)} fusion(s32[30720]{0:T(1024)S(1)} %fusion.11, s32[43008]{0:T(1024)S(1)} %pad_clamp_fusion.1), kind=kCustom, calls=%fused_computation.1 | custom fusion | bytes 506880 | tf_op jit(solution)/shard_map/gather | solution.py:142
  253.7 1.5 gather.13
  255.2 1.3 compare_select_fusion
  256.5 2.4 reshape.231
  260.2 36.8 %all_gather.15 = bf16[256,172]{1,0:T(8,128)(2,1)S(1)} all-gather(bf16[8,172]{1,0:T(8,128)(2,1)S(1)} %get-tuple-element.57), channel_id=1, replica_groups=mesh['section'=4,'dp'=8] {'section','dp'}, dimensions={0}, use_global_device_ids=true | all-gather | bytes 90816 | tf_op jit(solution)/shard_map/all_gather | solution.py:133
  297.6 38.8 %all_gather.13 = bf16[256,256]{1,0:T(8,128)(2,1)S(1)} all-gather(bf16[8,256]{1,0:T(8,128)(2,1)S(1)} %get-tuple-element.55), channel_id=1, replica_groups=mesh['section'=4,'dp'=8] {'section','dp'}, dimensions={0}, use_global_device_ids=true | all-gather | bytes 135168 | tf_op jit(solution)/shard_map/all_gather | solution.py:133
  339.2 37.7 %all_gather.14 = bf16[512,256]{1,0:T(8,128)(2,1)S(1)} all-gather(bf16[16,256]{1,0:T(8,128)(2,1)S(1)} %get-tuple-element.53), channel_id=1, replica_groups=mesh['section'=4,'dp'=8] {'section','dp'}, dimensions={0}, use_global_device_ids=true | all-gather | bytes 270336 | tf_op jit(solution)/shard_map/all_gather | solution.py:133
  378.1 4.2 convert_reduce_fusion
  382.4 1.5 iota_compare_fusion.1
  383.9 200.6 %gather_fusion.2 = bf16[42240,128]{1,0:T(8,128)(2,1)} fusion(bf16[131072,128]{1,0:T(8,128)(2,1)} %all-gather.2.cloned.1.call-done, s32[43008]{0:T(1024)S(1)} %pad_clamp_fusion), kind=kCustom, calls=%fused_computation.2 | custom fusion | bytes 21795840 | tf_op jit(solution)/shard_map/gather | solution.py:142
  584.5 16.7 %reshape.230 = bf16[2816,15,128]{2,1,0:T(8,128)(2,1)} reshape(bf16[42240,128]{1,0:T(8,128)(2,1)} %gather_fusion.2) | data formatting | bytes 21626880 | tf_op jit(solution)/shard_map/gather | solution.py:142
  601.2 17.2 %convert_reduce_fusion.1 = f32[2816,128]{1,0:T(8,128)S(1)} fusion(bf16[2816,15,128]{2,1,0:T(8,128)(2,1)} %reshape.230, pred[2816,15]{1,0:T(8,128)(4,1)S(1)} %iota_compare_fusion.1), kind=kLoop, calls=%fused_computation.5 | loop fusion | flops 15859712 | bytes 12297472 | tf_op jit(solution)/shard_map/reduce_sum | solution.py:143
  618.9 14.9 %gather_fusion = bf16[2816,128]{1,0:T(8,128)(2,1)} fusion(bf16[131072,128]{1,0:T(8,128)(2,1)} %all-gather.2.cloned.1.call-done, s32[3072]{0:T(1024)S(1)} %pad_clamp_fusion.2), kind=kCustom, calls=%fused_computation | custom fusion | bytes 1453056 | tf_op jit(solution)/shard_map/gather | solution.py:147
  633.8 3.6 multiply_convert_fusion.1
  642.2 3.1 convert_reduce_fusion.2
  646.1 1.0 pad_maximum_fusion.1
  649.9 124.4 %all-reduce.4.cloned.1.call-done = f32[32,7520]{1,0:T(8,128)} async-done(((f32[32,7520]{1,0:T(8,128)}), f32[32,7520]{1,0:T(8,128)}) %all-reduce.4.cloned.1.call-update) | async-done | bytes 962576
  774.3 1.5 multiply_reduce_fusion.9
  775.8 1.6 multiply_reduce_fusion.3
  778.7 1.5 multiply_reduce_fusion.11
  780.8 2.0 pad_maximum_fusion.9
  782.8 40.5 %all-reduce.1 = (f32[685]{0:T(1024)S(1)}, f32[4]{0:T(128)S(1)}) all-reduce(f32[685]{0:T(1024)S(1)} %pad_maximum_fusion.7, f32[4]{0:T(128)S(1)} %pad_maximum_fusion.9), channel_id=1, replica_groups=mesh['section'=4,'dp'=8] {'section','dp'}, use_global_device_ids=true, to_apply=%region_11.12 | all-reduce | flops 689 | bytes 5512 | tf_op jit(solution)/shard_map/psum | solution.py:208
  827.2 0.9 multiply_reduce_fusion.10
  828.2 1.0 multiply_reduce_fusion.1
  829.2 0.9 multiply_reduce_fusion.6
  833.4 2.0 pad_maximum_fusion.10
  836.1 39.9 %psum.31 = f32[3]{0:T(128)S(1)} all-reduce(f32[3]{0:T(128)S(1)} %pad_maximum_fusion.10), channel_id=1, replica_groups=mesh['section'=4,'dp'=8] {'section','dp'}, use_global_device_ids=true, to_apply=%region_24.25 | all-reduce | flops 3 | bytes 24 | tf_op jit(solution)/shard_map/psum | solution.py:222
  (140 shorter events, 25.1 us)
Async XLA Ops:
  7.2 25.7 %copy-start = (s32[4,2816,15]{1,0,2:T(4,128)S(1)}, s32[4,2816,15]{1,0,2:T(4,128)}, u32[]{:S(2)}) copy-start(s32[4,2816,15]{1,0,2:T(4,128)} %param.28) | copy-start | bytes 2027524
  7.2 376.7 %all-gather.2.cloned.1.call-start = ((), (), s32[]{:S(2)}) async-start(), calls=%async_computation | async-start | bytes 34603008 | tf_op jit(solution)/shard_map/all_gather | solution.py:66
  9.6 764.7 %all-reduce.4.cloned.1.call-start = ((), (), s32[]{:S(2)}) async-start(), calls=%async_computation.1 | async-start | bytes 1933312
  256.5 40.5 %copy-start.11 = (f32[8,256]{1,0:T(8,128)S(1)}, f32[8,256]{1,0:T(8,128)}, u32[]{:S(2)}) copy-start(f32[8,256]{1,0:T(8,128)} %param.34) | copy-start | bytes 24580
  256.5 82.1 %copy-start.5 = (f32[16,256]{1,0:T(8,128)S(1)}, f32[16,256]{1,0:T(8,128)}, u32[]{:S(2)}) copy-start(f32[16,256]{1,0:T(8,128)} %param.35) | copy-start | bytes 49156
  256.5 120.4 %copy-start.19 = (f32[684]{0:T(1024)S(1)}, f32[684]{0:T(1024)}, u32[]{:S(2)}) copy-start(f32[684]{0:T(1024)} %param.37) | copy-start | bytes 8212
  256.5 121.6 %copy-start.24 = (s32[1,256]{1,0:T(1,128)S(1)}, s32[1,256]{1,0:T(1,128)}, u32[]{:S(2)}) copy-start(s32[1,256]{1,0:T(1,128)} %copy-done.23) | copy-start | bytes 3076
  258.9 123.5 %copy-start.9 = (s32[2816]{0:T(1024)S(1)}, s32[2816]{0:T(1024)}, u32[]{:S(2)}) copy-start(s32[2816]{0:T(1024)} %copy-done.8) | copy-start | bytes 33796
  601.2 17.3 %copy-start.14 = (f32[2816]{0:T(1024)S(1)}, f32[2816]{0:T(1024)}, u32[]{:S(2)}) copy-start(f32[2816]{0:T(1024)} %convert_element_type.102) | copy-start | bytes 33796
  618.9 14.9 %copy-start.2 = (bf16[2816,128]{1,0:T(8,128)(2,1)}, bf16[2816,128]{1,0:T(8,128)(2,1)S(1)}, u32[]{:S(2)}) copy-start(bf16[2816,128]{1,0:T(8,128)(2,1)S(1)} %divide_convert_fusion) | copy-start | bytes 2162692
  633.8 3.6 copy-start.25
  642.1 3.2 copy-start.3
  642.1 3.1 copy-start.4
  645.9 237.9 %copy-start.1 = (s32[4,2816,15]{1,0,2:T(4,128)S(1)}, s32[4,2816,15]{1,0,2:T(4,128)}, u32[]{:S(2)}) copy-start(s32[4,2816,15]{1,0,2:T(4,128)} %param.28) | copy-start | bytes 2027524
  645.9 179.4 %copy-start.33 = (f32[684]{0:T(1024)S(1)}, f32[684]{0:T(1024)}, u32[]{:S(2)}) copy-start(f32[684]{0:T(1024)} %param.41) | copy-start | bytes 8212
  646.0 179.4 %copy-start.34 = (f32[684]{0:T(1024)S(1)}, f32[684]{0:T(1024)}, u32[]{:S(2)}) copy-start(f32[684]{0:T(1024)} %param.45) | copy-start | bytes 8212
  646.0 185.5 %copy-start.26 = (f32[8,256]{1,0:T(8,128)S(1)}, f32[8,256]{1,0:T(8,128)}, u32[]{:S(2)}) copy-start(f32[8,256]{1,0:T(8,128)} %param.38) | copy-start | bytes 24580
  646.0 185.5 %copy-start.27 = (f32[8,256]{1,0:T(8,128)S(1)}, f32[8,256]{1,0:T(8,128)}, u32[]{:S(2)}) copy-start(f32[8,256]{1,0:T(8,128)} %param.42) | copy-start | bytes 24580
  646.0 186.1 %copy-start.28 = (f32[8,172]{1,0:T(8,128)S(1)}, f32[8,172]{1,0:T(8,128)}, u32[]{:S(2)}) copy-start(f32[8,172]{1,0:T(8,128)} %param.40) | copy-start | bytes 16516
  646.0 186.1 %copy-start.29 = (f32[8,172]{1,0:T(8,128)S(1)}, f32[8,172]{1,0:T(8,128)}, u32[]{:S(2)}) copy-start(f32[8,172]{1,0:T(8,128)} %param.44) | copy-start | bytes 16516
  646.0 186.7 %copy-start.20 = (f32[16,256]{1,0:T(8,128)S(1)}, f32[16,256]{1,0:T(8,128)}, u32[]{:S(2)}) copy-start(f32[16,256]{1,0:T(8,128)} %param.39) | copy-start | bytes 49156
  646.0 186.7 %copy-start.21 = (f32[16,256]{1,0:T(8,128)S(1)}, f32[16,256]{1,0:T(8,128)}, u32[]{:S(2)}) copy-start(f32[16,256]{1,0:T(8,128)} %param.43) | copy-start | bytes 49156
  646.0 235.2 %copy-start.35 = (f32[684]{0:T(1024)S(1)}, f32[684]{0:T(1024)}, u32[]{:S(2)}) copy-start(f32[684]{0:T(1024)} %param.49) | copy-start | bytes 8212
  646.1 235.8 %copy-start.30 = (f32[8,172]{1,0:T(8,128)S(1)}, f32[8,172]{1,0:T(8,128)}, u32[]{:S(2)}) copy-start(f32[8,172]{1,0:T(8,128)} %param.48) | copy-start | bytes 16516
  646.1 236.4 %copy-start.31 = (f32[8,256]{1,0:T(8,128)S(1)}, f32[8,256]{1,0:T(8,128)}, u32[]{:S(2)}) copy-start(f32[8,256]{1,0:T(8,128)} %param.46) | copy-start | bytes 24580
  646.1 237.1 %copy-start.22 = (f32[16,256]{1,0:T(8,128)S(1)}, f32[16,256]{1,0:T(8,128)}, u32[]{:S(2)}) copy-start(f32[16,256]{1,0:T(8,128)} %param.47) | copy-start | bytes 49156
  832.1 51.7 %copy-start.15 = (f32[8,256]{1,0:T(8,128)}, f32[8,256]{1,0:T(8,128)S(1)}, u32[]{:S(2)}) copy-start(f32[8,256]{1,0:T(8,128)S(1)} %get-tuple-element.40) | copy-start | bytes 24580
  832.1 51.7 %copy-start.16 = (f32[8,256]{1,0:T(8,128)}, f32[8,256]{1,0:T(8,128)S(1)}, u32[]{:S(2)}) copy-start(f32[8,256]{1,0:T(8,128)S(1)} %get-tuple-element.41) | copy-start | bytes 24580
  832.8 51.0 %copy-start.17 = (f32[8,172]{1,0:T(8,128)}, f32[8,172]{1,0:T(8,128)S(1)}, u32[]{:S(2)}) copy-start(f32[8,172]{1,0:T(8,128)S(1)} %get-tuple-element.46) | copy-start | bytes 16516
  832.8 51.0 %copy-start.18 = (f32[8,172]{1,0:T(8,128)}, f32[8,172]{1,0:T(8,128)S(1)}, u32[]{:S(2)}) copy-start(f32[8,172]{1,0:T(8,128)S(1)} %get-tuple-element.47) | copy-start | bytes 16516
  833.4 50.4 %copy-start.12 = (f32[16,256]{1,0:T(8,128)}, f32[16,256]{1,0:T(8,128)S(1)}, u32[]{:S(2)}) copy-start(f32[16,256]{1,0:T(8,128)S(1)} %get-tuple-element.43) | copy-start | bytes 49156
  833.4 50.4 %copy-start.13 = (f32[16,256]{1,0:T(8,128)}, f32[16,256]{1,0:T(8,128)S(1)}, u32[]{:S(2)}) copy-start(f32[16,256]{1,0:T(8,128)S(1)} %get-tuple-element.44) | copy-start | bytes 49156
  (6 other events, 11.5 us)
Sparse Core Ops, SparseCore 0:
  11.0 197.5 all-gather.1
  647.3 126.9 all-reduce.3

commit v2 on v1

--- a/solution.py
+++ b/solution.py
@@ -1,6 +1,8 @@
 import jax
 import jax.numpy as jnp
 from jax import lax
+from jax.experimental import pallas as pl
+from jax.experimental.pallas import tpu as pltpu
 from jax.sharding import PartitionSpec as P
 
 STEP = 5
@@ -14,7 +16,360 @@
 CLIP = 0.05
 AVERAGE = 0.9
 
+
+VMEM_TABLE_LIMIT = 36 * 2**20
 WHOLE_TABLE_LIMIT = 64 * 2**20
+MESH = pl.DeviceIdType.MESH
+SLOT = 16
+BLOCK = 16
+CHUNKS = 4
+GROUP = 4
+SETS = 4
+
+
+def spread_kernel(
+    table_ref,
+    weight_ref,
+    place_ref,
+    near_ref,
+    live_ref,
+    full_ref,
+    weights_ref,
+    idx_ref,
+    mix_ref,
+    parts,
+    own_sem,
+    z_sem,
+    x_sem,
+    y_sem,
+    far_sem,
+    twin_sem,
+    twin_own_sem,
+    double_sem,
+    send_sem,
+    double_send_sem,
+):
+    section, at = lax.axis_index("section"), lax.axis_index("dp")
+    z, core = at // 2, at % 2
+    flipped = z // 2
+    height = z + flipped * (3 - 2 * z)
+    pairs = table_ref.shape[0]
+    quarter = pairs // 4
+    chunk = quarter // CHUNKS
+
+    def level(value):
+        return value + flipped * (3 - 2 * value)
+
+    here = (section, at)
+    twin = (section, z * 2 + 1 - core)
+    beside_x = (section + 1 - 2 * (section % 2), at)
+    beside_y = (section + 2 - 4 * (section // 2), at)
+    inner_z = (section, level(1 - height) * 2 + core)
+    across_z = (section, level(2) * 2 + core)
+    outer_z = (section, level(0) * 2 + core)
+    skip_z = (section, ((z + 2) % 4) * 2 + core)
+    sources = [level(1 - height), level(2), level(3)]
+    crosses = height == 1
+
+    barrier = pltpu.get_barrier_semaphore()
+    for partner in (twin, beside_x, beside_y, inner_z, skip_z):
+        pl.semaphore_signal(barrier, inc=1, device_id=partner, device_id_type=MESH)
+
+    @pl.when(crosses)
+    def greet_across():
+        pl.semaphore_signal(barrier, inc=1, device_id=across_z, device_id_type=MESH)
+
+    pl.semaphore_wait(barrier, 5 + height)
+
+    sent = []
+
+    def region(shard, part, piece):
+        start_at = shard * pairs + part * quarter + piece * chunk
+        return full_ref.at[pl.ds(pl.multiple_of(start_at, chunk), chunk)]
+
+    def send(source, target, recv, device, when=None):
+        number = len(sent)
+        copy = pltpu.make_async_remote_copy(
+            src_ref=source,
+            dst_ref=target,
+            send_sem=send_sem.at[number],
+            recv_sem=recv,
+            device_id=device,
+            device_id_type=MESH,
+        )
+        sent.append((copy, when))
+        if when is None:
+            copy.start()
+        else:
+            pl.when(when)(copy.start)
+        return copy
+
+    def arrived(target, recv):
+        pltpu.make_async_copy(target, target, recv).wait()
+
+    mine = section * (lax.axis_size("dp")) + at
+    pltpu.sync_copy(weight_ref, weights_ref.at[mine])
+    doubling = [(twin, 1), (inner_z, 2), (skip_z, 4), (beside_x, 8), (beside_y, 16)]
+    doubled = []
+
+    def double_start(number):
+        device, size = doubling[number]
+        start_at = (mine // size) * size
+        block = weights_ref.at[pl.ds(start_at, size)]
+        copy = pltpu.make_async_remote_copy(
+            src_ref=block,
+            dst_ref=block,
+            send_sem=double_send_sem.at[number],
+            recv_sem=double_sem.at[number],
+            device_id=device,
+            device_id_type=MESH,
+        )
+        copy.start()
+        doubled.append(copy)
+
+    double_start(0)
+    for piece in range(CHUNKS):
+        start_at = section * quarter + piece * chunk
+        block = table_ref.at[pl.ds(pl.multiple_of(start_at, chunk), chunk)]
+        goal = region(at, section, piece)
+        send(block, goal, z_sem.at[piece], inner_z)
+        send(block, goal, z_sem.at[CHUNKS + piece], across_z, crosses)
+    whole = full_ref.at[pl.ds(pl.multiple_of(at * pairs, pairs), pairs)]
+    own = pltpu.make_async_copy(table_ref, whole, own_sem)
+    own.start()
+    send(table_ref, whole, twin_own_sem, twin)
+
+    placed = place_ref[...]
+    pair_at = placed // 2
+    high = place_ref.shape[1]
+    parts[0:128, :] = (pair_at % 256).astype(jnp.float32).astype(jnp.bfloat16)
+    parts[128:256, :] = (pair_at // 256).astype(jnp.float32).astype(jnp.bfloat16)
+    parts[256:384, :] = (placed % 2).astype(jnp.float32).astype(jnp.bfloat16)
+    looked_rows = near_ref.shape[0]
+    steps = 3 * CHUNKS + 2
+    per_step = -(-looked_rows // (8 * steps)) * 8
+
+    def look_up(first, last):
+        def rows_of(block, carry):
+            start_at = pl.multiple_of(block * 8, 8)
+            sub = lax.broadcasted_iota(jnp.int32, (high, 256), 0)
+            low_at = lax.broadcasted_iota(jnp.int32, (128, 256), 0)
+            row = lax.broadcasted_iota(jnp.int32, (256, 512), 0)
+            column = lax.broadcasted_iota(jnp.int32, (256, 512), 1)
+            for k in range(8):
+                node = near_ref[pl.ds(start_at + k, 1), :]
+                hot = (sub == node // 128).astype(jnp.float32).astype(jnp.bfloat16)
+                got = jnp.dot(parts[...], hot, preferred_element_type=jnp.float32)
+                chosen = low_at == node % 128
+                found = jnp.where(chosen, got[0:128] + 256.0 * got[128:256], 0.0)
+                odd = jnp.where(chosen, got[256:384], 0.0)
+                idx_ref[pl.ds(start_at + k, 1), :] = jnp.sum(found, axis=0, keepdims=True).astype(
+                    jnp.int32
+                )
+                mix_ref[pl.ds(start_at + k, 1), 0:256] = jnp.sum(odd, axis=0, keepdims=True)
+            odd = mix_ref[pl.ds(start_at, 8), 0:256]
+            live = live_ref[pl.ds(start_at, 8), :]
+            mix_ref[pl.ds(start_at, 8), :] = jnp.dot(
+                (live * (1.0 - odd)).astype(jnp.bfloat16),
+                (column == 2 * row).astype(jnp.float32).astype(jnp.bfloat16),
+                preferred_element_type=jnp.float32,
+            ) + jnp.dot(
+                (live * odd).astype(jnp.bfloat16),
+                (column == 2 * row + 1).astype(jnp.float32).astype(jnp.bfloat16),
+                preferred_element_type=jnp.float32,
+            )
+            return carry
+
+        lax.fori_loop(first // 8, last // 8, rows_of, 0)
+
+    total = 3 * CHUNKS
+    twins = []
+
+    def to_twin(block, number):
+        send(block, block, twin_sem.at[number], twin)
+        twins.append(number)
+
+    for step in range(steps):
+        if step < total:
+            turn, piece = divmod(step, CHUNKS)
+            shard = sources[turn] * 2 + core
+            block = region(shard, section, piece)
+            arrived(block, z_sem.at[step])
+            if turn == 0:
+                send(block, block, z_sem.at[2 * CHUNKS + piece], across_z, crosses)
+            else:
+                send(block, block, z_sem.at[step], outer_z, crosses)
+            send(block, block, x_sem.at[step], beside_x)
+            send(block, block, y_sem.at[step], beside_y)
+            to_twin(block, step)
+        late = step - 1
+        if 0 <= late < total:
+            turn, piece = divmod(late, CHUNKS)
+            shard = sources[turn] * 2 + core
+            block = region(shard, beside_x[0], piece)
+            arrived(block, x_sem.at[late])
+            if piece % 2 == 0:
+                send(block, block, far_sem.at[late], beside_y)
+            to_twin(block, total + late)
+            block = region(shard, beside_y[0], piece)
+            arrived(block, y_sem.at[late])
+            if piece % 2 == 1:
+                send(block, block, far_sem.at[late], beside_x)
+            to_twin(block, 2 * total + late)
+        later = step - 2
+        if 0 <= later < total:
+            turn, piece = divmod(later, CHUNKS)
+            shard = sources[turn] * 2 + core
+            block = region(shard, 3 - section, piece)
+            arrived(block, far_sem.at[later])
+            to_twin(block, 3 * total + later)
+        if step % 2 == 0 and step // 2 < len(doubling):
+            doubled[step // 2].wait()
+            if step // 2 + 1 < len(doubling):
+                double_start(step // 2 + 1)
+        first = min(step * per_step, looked_rows)
+        last = min(first + per_step, looked_rows)
+        if last > first:
+            look_up(first, last)
+
+    for number in range(len(twins)):
+        kind, step = divmod(number, total)
+        turn, piece = divmod(step, CHUNKS)
+        part = (section, beside_x[0], beside_y[0], 3 - section)[kind]
+        arrived(region(sources[turn] * 2 + 1 - core, part, piece), twin_sem.at[number])
+    other = full_ref.at[pl.ds(pl.multiple_of((z * 2 + 1 - core) * pairs, pairs), pairs)]
+    arrived(other, twin_own_sem)
+    own.wait()
+    for copy, when in sent:
+        if when is None:
+            copy.wait_send()
+        else:
+            pl.when(when)(copy.wait_send)
+
+
+def spread(node_table, packed, place, near, live):
+    devices = lax.axis_size(("section", "dp"))
+    table_rows = node_table.shape[0]
+    frontier_high = place.shape[1]
+    looked = near.shape[0]
+    total = 3 * CHUNKS
+    sends = 2 * CHUNKS + 1 + 3 * total + total + 4 * total
+    vmem = pl.BlockSpec(memory_space=pltpu.VMEM)
+    return pl.pallas_call(
+        spread_kernel,
+        out_shape=(
+            pltpu.VMEM((lax.axis_size("dp") * table_rows // 2, 2, node_table.shape[1]), jnp.bfloat16),
+            jax.ShapeDtypeStruct((devices,) + packed.shape, packed.dtype),
+            jax.ShapeDtypeStruct((looked, 256), jnp.int32),
+            jax.ShapeDtypeStruct((looked, 512), jnp.float32),
+        ),
+        in_specs=[pl.BlockSpec(memory_space=pl.ANY), vmem, vmem, vmem, vmem],
+        out_specs=(vmem, vmem, vmem, vmem),
+        scratch_shapes=[
+            pltpu.VMEM((384, frontier_high), jnp.bfloat16),
+            pltpu.SemaphoreType.DMA(()),
+            pltpu.SemaphoreType.DMA((total,)),
+            pltpu.SemaphoreType.DMA((total,)),
+            pltpu.SemaphoreType.DMA((total,)),
+            pltpu.SemaphoreType.DMA((total,)),
+            pltpu.SemaphoreType.DMA((4 * total,)),
+            pltpu.SemaphoreType.DMA(()),
+            pltpu.SemaphoreType.DMA((5,)),
+            pltpu.SemaphoreType.DMA((sends,)),
+            pltpu.SemaphoreType.DMA((5,)),
+        ],
+        compiler_params=pltpu.CompilerParams(
+            collective_id=0, has_side_effects=True, vmem_limit_bytes=12 * 2**20
+        ),
+    )(node_table.reshape(table_rows // 2, 2, -1), packed, place, near, live)
+
+
+def pick_kernel(idx_ref, mix_ref, table_ref, sum_ref, self_ref, *scratch):
+    blocks = mix_ref.shape[0]
+    stages = (scratch[:GROUP], scratch[GROUP : 2 * GROUP])
+    lists = scratch[2 * GROUP : 2 * GROUP + SETS]
+    sems = scratch[2 * GROUP + SETS]
+    words = GROUP * BLOCK * SLOT
+    lane = lax.broadcasted_iota(jnp.int32, (BLOCK, 2 * BLOCK * SLOT), 1)
+    same = lane // (2 * SLOT) == lax.broadcasted_iota(jnp.int32, lane.shape, 0)
+    near_part = jnp.logical_and(same, lane % (2 * SLOT) < 2 * SLOT - 2).astype(jnp.float32)
+    self_part = jnp.logical_and(same, lane % (2 * SLOT) >= 2 * SLOT - 2).astype(jnp.float32)
+    last = blocks // GROUP - 1
+
+    def fetch(turn, slot):
+        start_at = pl.multiple_of(jnp.minimum(turn, last) * words, words)
+        return pltpu.make_async_copy(idx_ref.at[pl.ds(start_at, words)], lists[slot], sems.at[slot])
+
+    def pick(member, slot, stage):
+        for unit in range(BLOCK * SLOT):
+            entry = table_ref[lists[slot][member * BLOCK * SLOT + unit]]
+            stage[pl.ds(2 * unit, 2), :] = entry.astype(jnp.float32)
+
+    def reduce(block, stage):
+        mix = mix_ref[pl.ds(block, 1), :]
+        left = jnp.concatenate([mix * near_part, mix * self_part], axis=0).astype(jnp.bfloat16)
+        out = jnp.dot(left, stage[...].astype(jnp.bfloat16), preferred_element_type=jnp.float32)
+        start_at = pl.multiple_of(block * BLOCK, BLOCK)
+        sum_ref[pl.ds(start_at, BLOCK), :] = out[:BLOCK]
+        self_ref[pl.ds(start_at, BLOCK), :] = out[BLOCK:].astype(jnp.bfloat16)
+
+    for slot in range(SETS):
+        fetch(slot, slot).start()
+    for member in range(GROUP):
+        stages[1][member][...] = jnp.zeros(stages[1][member].shape, jnp.float32)
+
+    def round_of(number, carry):
+        for slot in range(SETS):
+            turn = number * SETS + slot
+            fetch(turn, slot).wait()
+            for member in range(GROUP):
+                pick(member, slot, stages[slot % 2][member])
+                reduce(
+                    jnp.maximum((turn - 1) * GROUP + member, 0), stages[1 - slot % 2][member]
+                )
+            fetch(turn + SETS, slot).start()
+        return carry
+
+    lax.fori_loop(0, blocks // (GROUP * SETS), round_of, 0)
+    for slot in range(SETS):
+        fetch(0, slot).wait()
+    for member in range(GROUP):
+        reduce(blocks - GROUP + member, stages[(SETS - 1) % 2][member])
+
+
+def picked(idx, mix, table):
+    rows = mix.shape[0] * BLOCK
+    width = table.shape[2]
+    vmem = pl.BlockSpec(memory_space=pltpu.VMEM)
+    return pl.pallas_call(
+        pick_kernel,
+        out_shape=(
+            jax.ShapeDtypeStruct((rows, width), jnp.float32),
+            jax.ShapeDtypeStruct((rows, width), jnp.bfloat16),
+        ),
+        in_specs=[pl.BlockSpec(memory_space=pl.ANY), vmem, vmem],
+        out_specs=(vmem, vmem),
+        scratch_shapes=[pltpu.VMEM((2 * BLOCK * SLOT, width), jnp.float32)] * (2 * GROUP)
+        + [pltpu.SMEM((GROUP * BLOCK * SLOT,), jnp.int32)] * SETS
+        + [pltpu.SemaphoreType.DMA((SETS,))],
+        compiler_params=pltpu.CompilerParams(vmem_limit_bytes=16 * 2**20),
+    )(idx.reshape(-1), mix, table)
+
+
+def on_slice_kernels(node_table, owner_ids, dest_count, fan_inner):
+    parts, peers = lax.axis_size("section"), lax.axis_size("dp")
+    return (
+        parts == 4
+        and peers == 8
+        and peers * node_table.size * 2 <= VMEM_TABLE_LIMIT
+        and node_table.shape[1] == 128
+        and node_table.shape[0] % (64 * CHUNKS) == 0
+        and peers * node_table.shape[0] <= 131072
+        and owner_ids.shape[0] % 1024 == 0
+        and owner_ids.shape[0] <= 32768
+        and fan_inner == SLOT - 1
+        and dest_count % (BLOCK * GROUP * SETS) == 0
+    )
 
 
 def outer_product(left, right):
@@ -120,7 +475,7 @@
     dest_count, fan_inner = inner_neighbours.shape[1:]
     seed_count, fan_outer = outer_neighbours.shape[1:]
     classes = weight_head.shape[1]
-    label_count = jnp.maximum(lax.psum(jnp.sum(label_mask.astype(jnp.float32)), "dp"), 1.0)
+    label_part = jnp.sum(label_mask.astype(jnp.float32))
 
     def mine(array):
         return lax.dynamic_index_in_dim(array, at, 0, keepdims=False)
@@ -128,23 +483,47 @@
     inner_neighbours, inner_counts = mine(inner_neighbours), mine(inner_counts)
     outer_neighbours, outer_counts = mine(outer_neighbours), mine(outer_counts)
     labels, label_mask = mine(labels), mine(label_mask)
-    sizes = [weight.shape[0] for weight in (weight_inner, weight_outer, weight_head)]
-    full_inner, full_outer, full_head = (
-        lax.all_gather(weight.astype(jnp.bfloat16), every, axis=0, tiled=True)
-        for weight in (weight_inner, weight_outer, weight_head)
-    )
     bias_inner = biases[:hidden]
     bias_outer = biases[hidden : 2 * hidden]
     bias_head = biases[2 * hidden :]
 
-    source, place = gathered_rows(node_table, owners.reshape(-1), local_rows.reshape(-1))
+    owner_ids, row_ids = owners.reshape(-1), local_rows.reshape(-1)
+    weights = (weight_inner, weight_outer, weight_head)
     keep = jnp.arange(fan_inner)[None, :] < inner_counts[:, None]
-    rows = source[place[inner_neighbours]]
-    summed = jnp.sum(
-        jnp.where(keep[:, :, None], rows, jnp.zeros((), rows.dtype)), axis=1, dtype=jnp.float32
-    )
+    if on_slice_kernels(node_table, owner_ids, dest_count, fan_inner):
+        devices, peers = lax.axis_size(every), lax.axis_size("dp")
+        place = (owner_ids * node_table.shape[0] + row_ids).reshape(-1, 128).T
+        own = jnp.arange(dest_count, dtype=jnp.int32)[:, None]
+        near = jnp.concatenate([inner_neighbours, own], axis=1).reshape(-1, BLOCK * SLOT)
+        live = jnp.concatenate([keep.astype(jnp.float32), jnp.ones(own.shape, jnp.float32)], axis=1)
+        live = live.reshape(near.shape)
+        tail = jnp.stack([label_part // 256, label_part % 256])
+        tail = jnp.pad(tail[None], ((0, weight_head.shape[0] - 1), (0, hidden - classes - 2)))
+        packed = jnp.concatenate(
+            [weight_inner, weight_outer, jnp.concatenate([weight_head, tail], axis=1)], axis=0
+        ).astype(jnp.bfloat16)
+        table, everyone, idx, mix = spread(node_table, packed, place, near, live)
+        row_inner, row_outer = weight_inner.shape[0], weight_outer.shape[0]
+        full_inner = everyone[:, :row_inner].reshape(-1, hidden)
+        full_outer = everyone[:, row_inner : row_inner + row_outer].reshape(-1, hidden)
+        full_head = everyone[:, row_inner + row_outer :].reshape(-1, hidden)[:, :classes]
+        counts = everyone[:peers, row_inner + row_outer, classes : classes + 2].astype(jnp.float32)
+        label_count = jnp.maximum(jnp.sum(counts[:, 0] * 256 + counts[:, 1]), 1.0)
+        summed, self_rows = picked(idx, mix, table)
+    else:
+        label_count = jnp.maximum(lax.psum(label_part, "dp"), 1.0)
+        full_inner, full_outer, full_head = (
+            lax.all_gather(weight.astype(jnp.bfloat16), every, axis=0, tiled=True)
+            for weight in weights
+        )
+        source, place = gathered_rows(node_table, owner_ids, row_ids)
+        rows = source[place[inner_neighbours]]
+        summed = jnp.sum(
+            jnp.where(keep[:, :, None], rows, jnp.zeros((), rows.dtype)), axis=1, dtype=jnp.float32
+        )
+        self_rows = source[place[:dest_count]]
     mean_one = (summed / inner_counts[:, None].astype(jnp.float32)).astype(jnp.bfloat16)
-    joined_one = jnp.concatenate([source[place[:dest_count]], mean_one], axis=1)
+    joined_one = jnp.concatenate([self_rows, mean_one], axis=1)
     pre_one = jnp.dot(joined_one, full_inner, preferred_element_type=jnp.float32) + bias_inner
     hidden_one = jax.nn.silu(pre_one).astype(jnp.bfloat16)
 
@@ -200,7 +579,6 @@
         [grad.reshape(devices, -1) for grad in (grad_inner, grad_outer, grad_head)], axis=1
     )
     shard = lax.psum_scatter(grads, every, scatter_dimension=0, tiled=True).reshape(-1)
-    weights = (weight_inner, weight_outer, weight_head)
     shards = []
     for weight in weights:
         shards.append(shard[: weight.size].reshape(weight.shape))

time: 895 us -> 476 us (0.53)
  local copies, waits for them, and re-layouts: 464 us -> 32.8 us
  Pallas kernels: 0 us -> 160 us
  blocking collectives: 212 us -> 80.4 us
  other arithmetic: 56.1 us -> 37.2 us
    gather x5 -> x0, local copies, waits for them, and re-layouts: 450 us -> none  [the longest x4 435 us: on_device(): rows = source[place[inner_neighbours]]]
    pallas_call x0 -> x2, Pallas kernels: none -> 160 us  [the longest x1 128 us: spread(): pl.pallas_call(spread_kernel, out_shape=(pltpu.VMEM((lax.axis_size('dp')...]
    all_gather x3 -> x0, blocking collectives: 113 us -> none  [on_device(): lax.all_gather(weight.astype(jnp.bfloat16), every, axis=0, tiled=True)]
    unnamed x72 -> x66, local copies, waits for them, and re-layouts: 1.33 us -> 25.1 us
    psum x1 -> x0, blocking collectives: 18.8 us -> none  [on_device(): lax.psum(jnp.sum(label_mask.astype(jnp.float32)), 'dp')]
    reduce_sum x2, other arithmetic: 17.8 us -> 1.96 us  [the longest x1 1.35 us: on_device(): label_part = jnp.sum(label_mask.astype(jnp.float32))]
    unnamed x3 -> x2, waiting for transfers between devices: 124 us -> 127 us
  transfers between devices with their start and end apart: 2 -> 1, of which waited for: 1 -> 1; matrix products, arithmetic and copies ran while one was open for 27% -> 0% of each run, Pallas kernels for 0% -> 0%
where the time goes in v2:
time: 476 us; the launch traced here: 475 us
  Pallas kernels  160 us (34%)
  waiting for transfers between devices  127 us (27%)
  blocking collectives  80.4 us (17%)
  other arithmetic  37.2 us (8%)
  local copies, waits for them, and re-layouts  32.8 us (7%)
  between operations  29.9 us (6%)
  matrix products  8.21 us (2%)
    pallas_call x1, Pallas kernels, spread(): pl.pallas_call(spread_kernel, out_shape=(pltpu.VMEM((lax.axis_size('dp')...  128 us
    unnamed x2, waiting for transfers between devices  127 us
    psum x1, blocking collectives, on_device(): packed = lax.psum(jnp.concatenate([bias_part, loss_part[None]]), every)  40.5 us
    psum x1, blocking collectives, on_device(): lax.psum(jnp.stack([jnp.sum(state[2] * state[2]) for state in states]), e...  39.9 us
    pallas_call x1, Pallas kernels, picked(): pl.pallas_call(pick_kernel, out_shape=(jax.ShapeDtypeStruct((rows, width)...  31.7 us
    unnamed x66, local copies, waits for them, and re-layouts  25.1 us
  transfers between devices with their start and end apart: 1, of which 1 were waited for; matrix products, arithmetic and copies ran while one was open for 0% of the time, Pallas kernels for 0%

profile of v2, /device:TPU:0, one launch (start us, length us, event | category | flops | bytes accessed | tf_op | source)
XLA Modules:
  0.0 474.8 jit_solution(11575380038216968623)
XLA Ops:
  7.3 1.4 convert_reduce_fusion.4
  10.0 0.8 dynamic-slice_reduce_fusion
  10.8 1.3 iota_compare_fusion.1
  12.1 1.4 multiply_reduce_fusion.2
  13.5 1.4 multiply_reduce_fusion.8
  14.9 1.4 multiply_reduce_fusion.7
  18.8 2.2 copy-done.4
  21.0 128.1 %shard_map.392 = (bf16[65536,2,128]{2,1,0:T(2,128)(2,1)S(1)}, bf16[32,32,256]{2,1,0:T(8,128)(2,1)S(1)}, s32[176,256]{1,0:T(8,128)S(1)}, f32[176,512]{1,0:T(8,128)S(1)}) custom-call(bf16[8192,2,128]{2,1,0:T(2,128)(2,1)S(1)} %bitcast.58, bf16[32,256]{1,0:T(8,128)(2,1)S(1)} %fusion.20.weight_ref, s32[128,240]{1,0:T(8,128)S(1)} %bitcast.60, ...), custom_call_target="tpu_custom_call" | custom-call | tf_op jit(solution)/shard_map/pallas_call | solution.py:258
  149.1 11.1 %copy-done.2 = bf16[65536,2,128]{2,1,0:T(2,128)(2,1)} copy-done((bf16[65536,2,128]{2,1,0:T(2,128)(2,1)}, bf16[65536,2,128]{2,1,0:T(2,128)(2,1)S(1)}, u32[]{:S(2)}) %copy-start.2) | copy-done | bytes 33554456
  162.3 0.8 constant_dynamic-slice_fusion.3
  163.1 0.7 constant_dynamic-slice_fusion.1
  163.8 4.2 convert_reduce_fusion
  168.0 10.5 %copy-done.3 = bf16[65536,2,128]{2,1,0:T(2,128)(2,1)S(1)} copy-done((bf16[65536,2,128]{2,1,0:T(2,128)(2,1)S(1)}, bf16[65536,2,128]{2,1,0:T(2,128)(2,1)}, u32[]{:S(2)}) %copy-start.3) | copy-done | bytes 33554456
  178.6 31.7 %shard_map.393 = (f32[2816,128]{1,0:T(8,128)S(1)}, bf16[2816,128]{1,0:T(8,128)(2,1)S(1)}) custom-call(s32[45056]{0:T(1024)S(1)} %bitcast.59, f32[176,512]{1,0:T(8,128)S(1)} %get-tuple-element.27.mix_ref, bf16[65536,2,128]{2,1,0:T(2,128)(2,1)S(1)} %copy-done.3), custom_call_target="tpu_custom_call" | custom-call | tf_op jit(solution)/shard_map/pallas_call | solution.py:344
  210.7 2.8 multiply_convert_fusion.1
  213.6 0.9 slice.135
  215.8 1.9 fusion
  221.7 1.1 copy-done.5
  222.8 1.3 convert_reduce_fusion.1
  225.1 1.0 pad_maximum_fusion.1
  228.3 0.7 pad_maximum_fusion.7
  229.0 126.6 %all-reduce.6.cloned.1.call-done = f32[32,7520]{1,0:T(8,128)} async-done(((f32[32,7520]{1,0:T(8,128)}), f32[32,7520]{1,0:T(8,128)}) %all-reduce.6.cloned.1.call-update) | async-done | bytes 962576
  355.6 1.5 multiply_reduce_fusion.9
  357.1 1.6 multiply_reduce_fusion.3
  360.0 1.5 multiply_reduce_fusion.11
  362.1 2.0 pad_maximum_fusion.9
  364.2 40.5 %all-reduce.3 = (f32[685]{0:T(1024)S(1)}, f32[4]{0:T(128)S(1)}) all-reduce(f32[685]{0:T(1024)S(1)} %pad_maximum_fusion.7, f32[4]{0:T(128)S(1)} %pad_maximum_fusion.9), channel_id=1, replica_groups=mesh['section'=4,'dp'=8] {'section','dp'}, use_global_device_ids=true, to_apply=%region_10.11 | all-reduce | flops 689 | bytes 5512 | tf_op jit(solution)/shard_map/psum | solution.py:586
  409.9 0.9 multiply_reduce_fusion.6
  410.7 1.0 multiply_reduce_fusion.1
  411.8 0.9 multiply_reduce_fusion.10
  414.8 2.0 pad_maximum_fusion.10
  417.5 39.9 %psum.23 = f32[3]{0:T(128)S(1)} all-reduce(f32[3]{0:T(128)S(1)} %pad_maximum_fusion.10), channel_id=1, replica_groups=mesh['section'=4,'dp'=8] {'section','dp'}, use_global_device_ids=true, to_apply=%region_23.24 | all-reduce | flops 3 | bytes 24 | tf_op jit(solution)/shard_map/psum | solution.py:600
  (128 shorter events, 19.9 us)
Async XLA Ops:
  7.2 9.9 %copy-start = (s32[4,2816,15]{1,0,2:T(4,128)S(1)}, s32[4,2816,15]{1,0,2:T(4,128)}, u32[]{:S(2)}) copy-start(s32[4,2816,15]{1,0,2:T(4,128)} %param.28) | copy-start | bytes 2027524
  7.2 348.4 %all-reduce.6.cloned.1.call-start = ((), (), s32[]{:S(2)}) async-start(), calls=%async_computation | async-start | bytes 1933312
  16.4 1.9 copy-start.9
  16.5 2.0 copy-start.10
  18.5 141.7 %copy-start.19 = (f32[684]{0:T(1024)S(1)}, f32[684]{0:T(1024)}, u32[]{:S(2)}) copy-start(f32[684]{0:T(1024)} %param.37) | copy-start | bytes 8212
  18.8 2.2 copy-start.4
  149.1 11.1 %copy-start.2 = (bf16[65536,2,128]{2,1,0:T(2,128)(2,1)}, bf16[65536,2,128]{2,1,0:T(2,128)(2,1)S(1)}, u32[]{:S(2)}) copy-start(bf16[65536,2,128]{2,1,0:T(2,128)(2,1)S(1)} %get-tuple-element.28.table_ref) | copy-start | bytes 100663296
  168.0 10.5 %copy-start.3 = (bf16[65536,2,128]{2,1,0:T(2,128)(2,1)S(1)}, bf16[65536,2,128]{2,1,0:T(2,128)(2,1)}, u32[]{:S(2)}) copy-start(bf16[65536,2,128]{2,1,0:T(2,128)(2,1)} %copy-done.2) | copy-start | bytes 100663296
  210.7 2.9 copy-start.6
  220.9 1.8 copy-start.5
  224.1 241.7 %copy-start.1 = (s32[4,2816,15]{1,0,2:T(4,128)S(1)}, s32[4,2816,15]{1,0,2:T(4,128)}, u32[]{:S(2)}) copy-start(s32[4,2816,15]{1,0,2:T(4,128)} %param.28) | copy-start | bytes 2027524
  224.6 181.4 %copy-start.29 = (f32[684]{0:T(1024)S(1)}, f32[684]{0:T(1024)}, u32[]{:S(2)}) copy-start(f32[684]{0:T(1024)} %param.41) | copy-start | bytes 8212
  224.7 181.3 %copy-start.30 = (f32[684]{0:T(1024)S(1)}, f32[684]{0:T(1024)}, u32[]{:S(2)}) copy-start(f32[684]{0:T(1024)} %param.45) | copy-start | bytes 8212
  224.7 188.1 %copy-start.12 = (f32[8,256]{1,0:T(8,128)S(1)}, f32[8,256]{1,0:T(8,128)}, u32[]{:S(2)}) copy-start(f32[8,256]{1,0:T(8,128)} %param.34) | copy-start | bytes 24580
  224.7 188.1 %copy-start.23 = (f32[8,256]{1,0:T(8,128)S(1)}, f32[8,256]{1,0:T(8,128)}, u32[]{:S(2)}) copy-start(f32[8,256]{1,0:T(8,128)} %param.38) | copy-start | bytes 24580
  224.7 188.1 %copy-start.24 = (f32[8,256]{1,0:T(8,128)S(1)}, f32[8,256]{1,0:T(8,128)}, u32[]{:S(2)}) copy-start(f32[8,256]{1,0:T(8,128)} %param.42) | copy-start | bytes 24580
  224.7 188.7 %copy-start.8 = (f32[16,256]{1,0:T(8,128)S(1)}, f32[16,256]{1,0:T(8,128)}, u32[]{:S(2)}) copy-start(f32[16,256]{1,0:T(8,128)} %param.35) | copy-start | bytes 49156
  224.7 188.7 %copy-start.20 = (f32[16,256]{1,0:T(8,128)S(1)}, f32[16,256]{1,0:T(8,128)}, u32[]{:S(2)}) copy-start(f32[16,256]{1,0:T(8,128)} %param.39) | copy-start | bytes 49156
  224.7 188.7 %copy-start.21 = (f32[16,256]{1,0:T(8,128)S(1)}, f32[16,256]{1,0:T(8,128)}, u32[]{:S(2)}) copy-start(f32[16,256]{1,0:T(8,128)} %param.43) | copy-start | bytes 49156
  224.7 189.4 %copy-start.11 = (f32[8,172]{1,0:T(8,128)S(1)}, f32[8,172]{1,0:T(8,128)}, u32[]{:S(2)}) copy-start(f32[8,172]{1,0:T(8,128)} %param.36) | copy-start | bytes 16516
  224.8 189.3 %copy-start.25 = (f32[8,172]{1,0:T(8,128)S(1)}, f32[8,172]{1,0:T(8,128)}, u32[]{:S(2)}) copy-start(f32[8,172]{1,0:T(8,128)} %param.40) | copy-start | bytes 16516
  224.8 189.3 %copy-start.26 = (f32[8,172]{1,0:T(8,128)S(1)}, f32[8,172]{1,0:T(8,128)}, u32[]{:S(2)}) copy-start(f32[8,172]{1,0:T(8,128)} %param.44) | copy-start | bytes 16516
  224.8 238.4 %copy-start.31 = (f32[684]{0:T(1024)S(1)}, f32[684]{0:T(1024)}, u32[]{:S(2)}) copy-start(f32[684]{0:T(1024)} %param.49) | copy-start | bytes 8212
  224.8 239.0 %copy-start.27 = (f32[8,172]{1,0:T(8,128)S(1)}, f32[8,172]{1,0:T(8,128)}, u32[]{:S(2)}) copy-start(f32[8,172]{1,0:T(8,128)} %param.48) | copy-start | bytes 16516
  224.8 239.6 %copy-start.22 = (f32[16,256]{1,0:T(8,128)S(1)}, f32[16,256]{1,0:T(8,128)}, u32[]{:S(2)}) copy-start(f32[16,256]{1,0:T(8,128)} %param.47) | copy-start | bytes 49156
  224.8 240.3 %copy-start.28 = (f32[8,256]{1,0:T(8,128)S(1)}, f32[8,256]{1,0:T(8,128)}, u32[]{:S(2)}) copy-start(f32[8,256]{1,0:T(8,128)} %param.46) | copy-start | bytes 24580
  413.4 52.2 %copy-start.15 = (f32[8,256]{1,0:T(8,128)}, f32[8,256]{1,0:T(8,128)S(1)}, u32[]{:S(2)}) copy-start(f32[8,256]{1,0:T(8,128)S(1)} %get-tuple-element.52) | copy-start | bytes 24580
  413.5 52.2 %copy-start.16 = (f32[8,256]{1,0:T(8,128)}, f32[8,256]{1,0:T(8,128)S(1)}, u32[]{:S(2)}) copy-start(f32[8,256]{1,0:T(8,128)S(1)} %get-tuple-element.53) | copy-start | bytes 24580
  414.1 51.6 %copy-start.13 = (f32[16,256]{1,0:T(8,128)}, f32[16,256]{1,0:T(8,128)S(1)}, u32[]{:S(2)}) copy-start(f32[16,256]{1,0:T(8,128)S(1)} %get-tuple-element.55) | copy-start | bytes 49156
  414.1 51.6 %copy-start.14 = (f32[16,256]{1,0:T(8,128)}, f32[16,256]{1,0:T(8,128)S(1)}, u32[]{:S(2)}) copy-start(f32[16,256]{1,0:T(8,128)S(1)} %get-tuple-element.56) | copy-start | bytes 49156
  414.7 51.0 %copy-start.17 = (f32[8,172]{1,0:T(8,128)}, f32[8,172]{1,0:T(8,128)S(1)}, u32[]{:S(2)}) copy-start(f32[8,172]{1,0:T(8,128)S(1)} %get-tuple-element.58) | copy-start | bytes 16516
  414.7 51.0 %copy-start.18 = (f32[8,172]{1,0:T(8,128)}, f32[8,172]{1,0:T(8,128)S(1)}, u32[]{:S(2)}) copy-start(f32[8,172]{1,0:T(8,128)S(1)} %get-tuple-element.59) | copy-start | bytes 16516
  (1 other events, 1.3 us)
Sparse Core Ops, SparseCore 0:
  226.3 129.2 all-reduce.5

commit v3 on v2

--- a/solution.py
+++ b/solution.py
@@ -1,3 +1,5 @@
+import functools
+
 import jax
 import jax.numpy as jnp
 from jax import lax
@@ -107,9 +109,9 @@
     def arrived(target, recv):
         pltpu.make_async_copy(target, target, recv).wait()
 
-    mine = section * (lax.axis_size("dp")) + at
+    mine = (core * 4 + section) * 4 + z
     pltpu.sync_copy(weight_ref, weights_ref.at[mine])
-    doubling = [(twin, 1), (inner_z, 2), (skip_z, 4), (beside_x, 8), (beside_y, 16)]
+    doubling = [(inner_z, 1), (skip_z, 2), (beside_x, 4), (beside_y, 8), (twin, 16)]
     doubled = []
 
     def double_start(number):
@@ -284,7 +286,7 @@
     )(node_table.reshape(table_rows // 2, 2, -1), packed, place, near, live)
 
 
-def pick_kernel(idx_ref, mix_ref, table_ref, sum_ref, self_ref, *scratch):
+def pick_kernel(idx_ref, mix_ref, table_ref, joined_ref, *scratch):
     blocks = mix_ref.shape[0]
     stages = (scratch[:GROUP], scratch[GROUP : 2 * GROUP])
     lists = scratch[2 * GROUP : 2 * GROUP + SETS]
@@ -307,11 +309,13 @@
 
     def reduce(block, stage):
         mix = mix_ref[pl.ds(block, 1), :]
-        left = jnp.concatenate([mix * near_part, mix * self_part], axis=0).astype(jnp.bfloat16)
+        near = mix * near_part
+        left = jnp.concatenate([near, mix * self_part], axis=0).astype(jnp.bfloat16)
         out = jnp.dot(left, stage[...].astype(jnp.bfloat16), preferred_element_type=jnp.float32)
+        count = jnp.maximum(jnp.sum(near, axis=1, keepdims=True), 1.0)
+        both = jnp.concatenate([out[BLOCK:], out[:BLOCK] / count], axis=1)
         start_at = pl.multiple_of(block * BLOCK, BLOCK)
-        sum_ref[pl.ds(start_at, BLOCK), :] = out[:BLOCK]
-        self_ref[pl.ds(start_at, BLOCK), :] = out[BLOCK:].astype(jnp.bfloat16)
+        joined_ref[pl.ds(start_at, BLOCK), :] = both.astype(jnp.bfloat16)
 
     for slot in range(SETS):
         fetch(slot, slot).start()
@@ -343,12 +347,9 @@
     vmem = pl.BlockSpec(memory_space=pltpu.VMEM)
     return pl.pallas_call(
         pick_kernel,
-        out_shape=(
-            jax.ShapeDtypeStruct((rows, width), jnp.float32),
-            jax.ShapeDtypeStruct((rows, width), jnp.bfloat16),
-        ),
+        out_shape=jax.ShapeDtypeStruct((rows, 2 * width), jnp.bfloat16),
         in_specs=[pl.BlockSpec(memory_space=pl.ANY), vmem, vmem],
-        out_specs=(vmem, vmem),
+        out_specs=vmem,
         scratch_shapes=[pltpu.VMEM((2 * BLOCK * SLOT, width), jnp.float32)] * (2 * GROUP)
         + [pltpu.SMEM((GROUP * BLOCK * SLOT,), jnp.int32)] * SETS
         + [pltpu.SemaphoreType.DMA((SETS,))],
@@ -356,7 +357,411 @@
     )(idx.reshape(-1), mix, table)
 
 
-def on_slice_kernels(node_table, owner_ids, dest_count, fan_inner):
+TILE = 256
+
+
+def block_order():
+    return [(e % 2) * 16 + (e // 8) * 4 + (e % 8) // 2 for e in range(32)]
+
+
+def dense_kernel(
+    sizes,
+    joined_ref,
+    everyone_ref,
+    bias_ref,
+    seed_ref,
+    seed_across_ref,
+    grads_ref,
+    extra_ref,
+    first_pre,
+    first_hidden,
+    wide,
+    mean_sum,
+    pick_back,
+    inner_sum,
+):
+    classes, fan_outer, row_inner, row_outer, row_head = sizes
+    dest_count, hidden = joined_ref.shape
+    tiles = dest_count // TILE
+    order = block_order()
+    weights = everyone_ref[...].astype(jnp.float32)
+    split = (0, row_inner, row_inner + row_outer, row_inner + row_outer + row_head)
+    full_inner, full_outer, full_head = (
+        jnp.concatenate([weights[place, split[k] : split[k + 1]] for place in order], axis=0)
+        for k in range(3)
+    )
+    lane = lax.broadcasted_iota(jnp.int32, (1, hidden), 1)
+    tails = weights[0:4, split[2] : split[2] + 1] + weights[16:20, split[2] : split[2] + 1]
+    tails = jnp.sum(tails.reshape(4, hidden), axis=0, keepdims=True)
+    scale = jnp.where(lane == classes, 256.0, jnp.where(lane == classes + 1, 1.0, 0.0))
+    label_count = jnp.maximum(jnp.sum(tails * scale), 1.0)
+    full_inner = full_inner.astype(jnp.bfloat16)
+    full_outer = full_outer.astype(jnp.bfloat16)
+    full_head = jnp.where(lane < classes, full_head, 0.0).astype(jnp.bfloat16)
+    bias_inner, bias_outer, bias_head = (bias_ref[k : k + 1, :] for k in range(3))
+    seeds = seed_ref.shape[0]
+    kept = seed_ref[:, 0:fan_outer]
+    count_two = jnp.sum((kept >= 0).astype(jnp.float32), axis=1, keepdims=True)
+    for j in range(fan_outer):
+        wide[j] = jnp.broadcast_to(seed_ref[:, j : j + 1], (seeds, TILE))
+    mean_sum[...] = jnp.zeros(mean_sum.shape, jnp.float32)
+
+    def forward(tile, carry):
+        start_at = pl.multiple_of(tile * TILE, TILE)
+        rows = pl.ds(start_at, TILE)
+        before = (
+            jnp.dot(joined_ref[rows, :], full_inner, preferred_element_type=jnp.float32) + bias_inner
+        )
+        first_pre[rows, :] = before
+        out = (before * lax.logistic(before)).astype(jnp.bfloat16)
+        first_hidden[rows, :] = out
+        dest = lax.broadcasted_iota(jnp.int32, (seeds, TILE), 1) + start_at
+        hits = jnp.zeros((seeds, TILE), jnp.float32)
+        for j in range(fan_outer):
+            hits = hits + (wide[j] == dest).astype(jnp.float32)
+        mean_sum[...] += jnp.dot(
+            hits.astype(jnp.bfloat16), out, preferred_element_type=jnp.float32
+        )
+        return carry
+
+    lax.fori_loop(0, tiles, forward, 0)
+    mean_two = (mean_sum[...] / count_two).astype(jnp.bfloat16)
+    joined_two = jnp.concatenate([first_hidden[0:seeds, :], mean_two], axis=1)
+    pre_two = jnp.dot(joined_two, full_outer, preferred_element_type=jnp.float32) + bias_outer
+    gate_two = lax.logistic(pre_two)
+    hidden_two = (pre_two * gate_two).astype(jnp.bfloat16)
+    logits = jnp.dot(hidden_two, full_head, preferred_element_type=jnp.float32) + bias_head
+    inside = lane < classes
+    highest = jnp.max(jnp.where(inside, logits, -jnp.inf), axis=1, keepdims=True)
+    shifted = jnp.where(inside, logits - highest, 0.0)
+    total = jnp.sum(jnp.where(inside, jnp.exp(shifted), 0.0), axis=1, keepdims=True)
+    log_total = jnp.log(total)
+    chosen = (lane == seed_ref[:, fan_outer : fan_outer + 1]).astype(jnp.float32)
+    row_weight = seed_ref[:, fan_outer + 1 : fan_outer + 2].astype(jnp.float32)
+    loss = jnp.sum((log_total - jnp.sum(shifted * chosen, axis=1, keepdims=True)) * row_weight)
+    grad_logits = (jnp.exp(shifted - log_total) - chosen) * (row_weight / label_count)
+    grad_logits = jnp.where(inside, grad_logits, 0.0).astype(jnp.bfloat16)
+    grad_head = outer_product(hidden_two, grad_logits)
+    grad_two = against(grad_logits, full_head).astype(jnp.bfloat16).astype(jnp.float32)
+    grad_pre_two = (grad_two * gate_two * (1.0 + pre_two * (1.0 - gate_two))).astype(jnp.bfloat16)
+    grad_outer = outer_product(joined_two, grad_pre_two)
+    grad_joined = against(grad_pre_two, full_outer)
+    share = grad_joined[:, hidden:] / count_two
+    share_high = share.astype(jnp.bfloat16)
+    share_low = (share - share_high.astype(jnp.float32)).astype(jnp.bfloat16)
+    for number, place in enumerate(order):
+        grads_ref[place, split[1] : split[2], :] = grad_outer[
+            number * row_outer : (number + 1) * row_outer
+        ]
+        grads_ref[place, split[2] : split[3], :] = grad_head[
+            number * row_head : (number + 1) * row_head
+        ]
+    inner_sum[...] = jnp.zeros(inner_sum.shape, jnp.float32)
+    share_parts = jnp.concatenate([share_high, share_low], axis=0)
+
+    def backward(tile, bias_sum, own=None):
+        start_at = pl.multiple_of(jnp.int32(tile) * TILE, TILE)
+        rows = pl.ds(start_at, TILE)
+        dest = lax.broadcasted_iota(jnp.int32, (TILE, seeds), 0) + start_at
+        hits = jnp.zeros((TILE, seeds), jnp.float32)
+        for j in range(fan_outer):
+            hits = hits + (seed_across_ref[j : j + 1, :] == dest).astype(jnp.float32)
+        hits = hits.astype(jnp.bfloat16)
+        both_hits = jnp.concatenate([hits, hits], axis=1)
+        grad_one = jnp.dot(both_hits, share_parts, preferred_element_type=jnp.float32)
+        if own is not None:
+            grad_one = grad_one + own
+        grad_one = grad_one.astype(jnp.bfloat16).astype(jnp.float32)
+        before = first_pre[rows, :]
+        gate = lax.logistic(before)
+        grad_pre = (grad_one * gate * (1.0 + before * (1.0 - gate))).astype(jnp.bfloat16)
+        inner_sum[...] += outer_product(joined_ref[rows, :], grad_pre)
+        return bias_sum + jnp.sum(grad_pre.astype(jnp.float32), axis=0, keepdims=True)
+
+    pick_back[...] = jnp.zeros(pick_back.shape, jnp.float32)
+    pick_back[0:seeds, :] = grad_joined[:, 0:hidden]
+    bias_sum = backward(0, jnp.zeros((1, hidden), jnp.float32), pick_back[...])
+    bias_sum = lax.fori_loop(1, tiles, backward, bias_sum)
+    grad_inner = inner_sum[...]
+    for number, place in enumerate(order):
+        grads_ref[place, split[0] : split[1], :] = grad_inner[
+            number * row_inner : (number + 1) * row_inner
+        ]
+    extra_ref[0:1, :] = bias_sum
+    extra_ref[1:2, :] = jnp.sum(grad_pre_two.astype(jnp.float32), axis=0, keepdims=True)
+    extra_ref[2:3, :] = jnp.sum(grad_logits.astype(jnp.float32), axis=0, keepdims=True)
+    extra_ref[3:4, :] = jnp.where(lane == 0, loss, jnp.where(lane == 1, label_count, 0.0))
+    extra_ref[4:8, :] = jnp.zeros((4, hidden), jnp.float32)
+
+
+def dense(sizes, joined, everyone, bias_rows, seed_table):
+    dest_count, hidden = joined.shape
+    seeds = seed_table.shape[0]
+    vmem = pl.BlockSpec(memory_space=pltpu.VMEM)
+    return pl.pallas_call(
+        functools.partial(dense_kernel, sizes),
+        out_shape=(
+            jax.ShapeDtypeStruct(everyone.shape, jnp.float32),
+            jax.ShapeDtypeStruct((8, hidden), jnp.float32),
+        ),
+        in_specs=[vmem] * 5,
+        out_specs=(vmem, vmem),
+        scratch_shapes=[
+            pltpu.VMEM((dest_count, hidden), jnp.float32),
+            pltpu.VMEM((dest_count, hidden), jnp.bfloat16),
+            pltpu.VMEM((sizes[1], seeds, TILE), jnp.int32),
+            pltpu.VMEM((seeds, hidden), jnp.float32),
+            pltpu.VMEM((TILE, hidden), jnp.float32),
+            pltpu.VMEM((hidden, hidden), jnp.float32),
+        ],
+        compiler_params=pltpu.CompilerParams(vmem_limit_bytes=32 * 2**20),
+    )(joined, everyone, bias_rows, seed_table, seed_table.T)
+
+
+def reduce_kernel(
+    sizes,
+    grads_ref,
+    extra_ref,
+    weight_refs,
+    first_refs,
+    second_refs,
+    out_ref,
+    half,
+    half_in,
+    fourth,
+    plane_in,
+    line_in,
+    extra_twin,
+    extra_plane,
+    extra_line,
+    sums_twin,
+    sums_plane,
+    sums_line,
+    recv_sem,
+    send_sem,
+):
+    section, at = lax.axis_index("section"), lax.axis_index("dp")
+    z, core = at // 2, at % 2
+    rows, hidden = grads_ref.shape[1], grads_ref.shape[2]
+    twin = (section, z * 2 + 1 - core)
+    plane = [((section + k) % 4, at) for k in range(1, 4)]
+    line = [(section, ((z + k) % 4) * 2 + core) for k in range(1, 4)]
+    barrier = pltpu.get_barrier_semaphore()
+    for partner in [twin] + plane + line:
+        pl.semaphore_signal(barrier, inc=1, device_id=partner, device_id_type=MESH)
+    pl.semaphore_wait(barrier, 7)
+    copies = []
+
+    def send(source, target, number, device):
+        copy = pltpu.make_async_remote_copy(
+            src_ref=source,
+            dst_ref=target,
+            send_sem=send_sem.at[len(copies)],
+            recv_sem=recv_sem.at[number],
+            device_id=device,
+            device_id_type=MESH,
+        )
+        copies.append(copy)
+        copy.start()
+
+    def arrived(target, number):
+        pltpu.make_async_copy(target, target, recv_sem.at[number]).wait()
+
+    def over_twin(value, slots, base):
+        slots[core] = value
+        send(slots.at[core], slots.at[core], base, twin)
+        arrived(slots.at[1 - core], base)
+        return slots[0] + slots[1]
+
+    def over_four(value, slots, base, me, partners):
+        slots[me] = value
+        for partner in partners:
+            send(slots.at[me], slots.at[me], base + me, partner)
+        for k in range(1, 4):
+            other = (me + k) % 4
+            arrived(slots.at[other], base + other)
+        return (slots[0] + slots[1]) + (slots[2] + slots[3])
+
+    send(grads_ref.at[pl.ds((1 - core) * 16, 16)], half_in, 0, twin)
+    extra = over_twin(extra_ref[...], extra_twin, 1)
+    arrived(half_in, 0)
+    half[...] = grads_ref[pl.ds(core * 16, 16)] + half_in[...]
+    for k, partner in enumerate(plane):
+        send(half.at[pl.ds(partner[0] * 4, 4)], plane_in.at[section], 2 + section, partner)
+    extra = over_four(extra, extra_plane, 6, section, plane)
+    plane_in[section] = half[pl.ds(section * 4, 4)]
+    for k in range(1, 4):
+        other = (section + k) % 4
+        arrived(plane_in.at[other], 2 + other)
+    quarter = (plane_in[0] + plane_in[1]) + (plane_in[2] + plane_in[3])
+    fourth[...] = quarter
+    for k, partner in enumerate(line):
+        send(fourth.at[pl.ds((z + k + 1) % 4, 1)], line_in.at[pl.ds(z, 1)], 10 + z, partner)
+    extra = over_four(extra, extra_line, 14, z, line)
+    line_in[z] = fourth[z]
+    for k in range(1, 4):
+        other = (z + k) % 4
+        arrived(line_in.at[pl.ds(other, 1)], 10 + other)
+    shard = (line_in[0] + line_in[1]) + (line_in[2] + line_in[3])
+
+    lane = lax.broadcasted_iota(jnp.int32, (8, 128), 1)
+
+    def packed(values):
+        found = jnp.zeros((8, 128), jnp.float32)
+        for k, value in enumerate(values):
+            found = jnp.where(lane == k, value, found)
+        return found
+
+    def unpacked(found, k):
+        return jnp.sum(jnp.where(lane[0:1] == k, found[0:1], 0.0))
+
+    classes, row_inner, row_outer, row_head = sizes
+    split = (0, row_inner, row_inner + row_outer, rows)
+    widths = (hidden, hidden, classes)
+    pieces = [shard[split[k] : split[k + 1], : widths[k]] for k in range(3)]
+    weights = [ref[...] for ref in weight_refs]
+    values = packed(
+        [jnp.sum(shard * shard)] + [jnp.sum(weight * weight) for weight in weights]
+    )
+    values = over_twin(values, sums_twin.at[0], 18)
+    values = over_four(values, sums_plane.at[0], 19, section, plane)
+    values = over_four(values, sums_line.at[0], 23, z, line)
+    bias_square = jnp.sum(extra[0:3] * extra[0:3])
+    clip_norm = jnp.sqrt(jnp.full((1, 1), unpacked(values, 0) + bias_square, jnp.float32))
+    factor = jnp.minimum(1.0, CLIP / clip_norm)
+    parts = []
+    for k in range(3):
+        update = moments(weights[k], pieces[k] * factor, first_refs[k][...], second_refs[k][...])[2]
+        parts.append(jnp.sum(update * update))
+    updates = packed(parts)
+    updates = over_twin(updates, sums_twin.at[1], 27)
+    updates = over_four(updates, sums_plane.at[1], 28, section, plane)
+    updates = over_four(updates, sums_line.at[1], 32, z, line)
+    out_ref[0:rows, :] = shard
+    out_ref[rows : rows + 8, :] = extra
+    out_ref[rows + 8 : rows + 16, 0:128] = values
+    out_ref[rows + 8 : rows + 16, 128:256] = updates
+    for copy in copies:
+        copy.wait_send()
+
+
+def reduced(sizes, grads, extra, weights, firsts, seconds):
+    blocks, rows, hidden = grads.shape
+    vmem = pl.BlockSpec(memory_space=pltpu.VMEM)
+    return pl.pallas_call(
+        functools.partial(reduce_kernel, sizes),
+        out_shape=jax.ShapeDtypeStruct((rows + 16, hidden), jnp.float32),
+        in_specs=[vmem, vmem, (vmem,) * 3, (vmem,) * 3, (vmem,) * 3],
+        out_specs=vmem,
+        scratch_shapes=[
+            pltpu.VMEM((16, rows, hidden), jnp.float32),
+            pltpu.VMEM((16, rows, hidden), jnp.float32),
+            pltpu.VMEM((4, rows, hidden), jnp.float32),
+            pltpu.VMEM((4, 4, rows, hidden), jnp.float32),
+            pltpu.VMEM((4, rows, hidden), jnp.float32),
+            pltpu.VMEM((2, 8, hidden), jnp.float32),
+            pltpu.VMEM((4, 8, hidden), jnp.float32),
+            pltpu.VMEM((4, 8, hidden), jnp.float32),
+            pltpu.VMEM((2, 2, 8, 128), jnp.float32),
+            pltpu.VMEM((2, 4, 8, 128), jnp.float32),
+            pltpu.VMEM((2, 4, 8, 128), jnp.float32),
+            pltpu.SemaphoreType.DMA((36,)),
+            pltpu.SemaphoreType.DMA((28,)),
+        ],
+        compiler_params=pltpu.CompilerParams(
+            collective_id=1, has_side_effects=True, vmem_limit_bytes=16 * 2**20
+        ),
+    )(grads, extra, weights, firsts, seconds)
+
+
+def final_kernel(
+    sizes,
+    sums_ref,
+    weight_refs,
+    first_refs,
+    second_refs,
+    smooth_refs,
+    bias_ref,
+    scalar_ref,
+    norms_ref,
+    new_refs,
+    moment_refs,
+    square_refs,
+    average_refs,
+    bias_out_ref,
+):
+    classes, row_inner, row_outer, row_head = sizes
+    hidden = sums_ref.shape[1]
+    rows = row_inner + row_outer + row_head
+    split = (0, row_inner, row_inner + row_outer, rows)
+    widths = (hidden, hidden, classes)
+    lane = lax.broadcasted_iota(jnp.int32, (1, 128), 1)
+
+    def number(k, start_at):
+        found = sums_ref[rows + 8 : rows + 9, start_at : start_at + 128]
+        return jnp.sum(jnp.where(lane == k, found, 0.0), keepdims=True)
+
+    bias_grad = sums_ref[rows : rows + 3, :]
+    bias_square = jnp.sum(jnp.sum(bias_grad * bias_grad, axis=1, keepdims=True), axis=0, keepdims=True)
+    clip_norm = jnp.sqrt(number(0, 0) + bias_square)
+    factor = jnp.minimum(1.0, CLIP / clip_norm)
+    wide = lax.broadcasted_iota(jnp.int32, (8, 128), 1)
+    deep = lax.broadcasted_iota(jnp.int32, (8, 128), 0)
+    norms = jnp.zeros((8, 128), jnp.float32)
+    for k in range(3):
+        weight = weight_refs[k][...]
+        gradient = sums_ref[split[k] : split[k + 1], 0 : widths[k]] * factor
+        first, second, update = moments(weight, gradient, first_refs[k][...], second_refs[k][...])
+        weight_norm, update_norm = jnp.sqrt(number(1 + k, 0)), jnp.sqrt(number(k, 128))
+        fresh = weight - RATE * (weight_norm / update_norm) * update
+        new_refs[k][...] = fresh
+        moment_refs[k][...] = first
+        square_refs[k][...] = second
+        average_refs[k][...] = AVERAGE * smooth_refs[k][...] + (1.0 - AVERAGE) * fresh
+        norms = jnp.where(jnp.logical_and(deep == k, wide == 0), weight_norm, norms)
+        norms = jnp.where(jnp.logical_and(deep == k, wide == 1), update_norm, norms)
+    norms_ref[...] = norms[0:3, 0:2]
+    weight = bias_ref[0:3, :]
+    first, second, update = moments(
+        weight, bias_grad * factor, bias_ref[3:6, :], bias_ref[6:9, :]
+    )
+    column = lax.broadcasted_iota(jnp.int32, weight.shape, 1)
+    row = lax.broadcasted_iota(jnp.int32, weight.shape, 0)
+    update = jnp.where(jnp.logical_or(row < 2, column < classes), update, 0.0)
+    ratio = jnp.sqrt(jnp.sum(weight * weight, axis=1, keepdims=True)) / jnp.sqrt(
+        jnp.sum(update * update, axis=1, keepdims=True)
+    )
+    fresh = weight - RATE * ratio * update
+    average = AVERAGE * bias_ref[9:12, :] + (1.0 - AVERAGE) * fresh
+    for k, value in enumerate((fresh, first, second, average)):
+        bias_out_ref[4 * k : 4 * k + 3, :] = value
+    tail = sums_ref[rows + 3 : rows + 4, 0:128]
+    scalar_ref[...] = jnp.where(wide == 0, tail, jnp.where(wide == 1, clip_norm, 0.0))
+
+
+def finished(sizes, sums, weights, firsts, seconds, smooths, bias_rows):
+    hidden = sums.shape[1]
+    vmem = pl.BlockSpec(memory_space=pltpu.VMEM)
+    like = [jax.ShapeDtypeStruct(weight.shape, jnp.float32) for weight in weights]
+    return pl.pallas_call(
+        functools.partial(final_kernel, sizes),
+        out_shape=(
+            jax.ShapeDtypeStruct((8, 128), jnp.float32),
+            jax.ShapeDtypeStruct((3, 2), jnp.float32),
+            like,
+            like,
+            like,
+            like,
+            jax.ShapeDtypeStruct((16, hidden), jnp.float32),
+        ),
+        in_specs=[vmem] + [(vmem,) * 3] * 4 + [vmem],
+        out_specs=(vmem, vmem, [vmem] * 3, [vmem] * 3, [vmem] * 3, [vmem] * 3, vmem),
+    )(sums, weights, firsts, seconds, smooths, bias_rows)
+
+
+def on_slice_kernels(
+    node_table, owner_ids, dest_count, fan_inner, hidden, classes, seed_count, fan_outer, mask_sizes, weight_rows
+):
     parts, peers = lax.axis_size("section"), lax.axis_size("dp")
     return (
         parts == 4
@@ -369,6 +774,16 @@
         and owner_ids.shape[0] <= 32768
         and fan_inner == SLOT - 1
         and dest_count % (BLOCK * GROUP * SETS) == 0
+        and dest_count % TILE == 0
+        and hidden == 256
+        and classes + 2 <= hidden
+        and seed_count <= TILE
+        and seed_count % 16 == 0
+        and fan_outer + 2 <= SLOT
+        and len(mask_sizes) == 2
+        and mask_sizes[0] * mask_sizes[1] <= 65536
+        and all(rows % 8 == 0 for rows in weight_rows)
+        and sum(weight_rows) % 32 == 0
     )
 
 
@@ -475,6 +890,7 @@
     dest_count, fan_inner = inner_neighbours.shape[1:]
     seed_count, fan_outer = outer_neighbours.shape[1:]
     classes = weight_head.shape[1]
+    mask_sizes = label_mask.shape
     label_part = jnp.sum(label_mask.astype(jnp.float32))
 
     def mine(array):
@@ -490,7 +906,18 @@
     owner_ids, row_ids = owners.reshape(-1), local_rows.reshape(-1)
     weights = (weight_inner, weight_outer, weight_head)
     keep = jnp.arange(fan_inner)[None, :] < inner_counts[:, None]
-    if on_slice_kernels(node_table, owner_ids, dest_count, fan_inner):
+    if on_slice_kernels(
+        node_table,
+        owner_ids,
+        dest_count,
+        fan_inner,
+        hidden,
+        classes,
+        seed_count,
+        fan_outer,
+        mask_sizes,
+        [weight.shape[0] for weight in weights],
+    ):
         devices, peers = lax.axis_size(every), lax.axis_size("dp")
         place = (owner_ids * node_table.shape[0] + row_ids).reshape(-1, 128).T
         own = jnp.arange(dest_count, dtype=jnp.int32)[:, None]
@@ -503,25 +930,64 @@
             [weight_inner, weight_outer, jnp.concatenate([weight_head, tail], axis=1)], axis=0
         ).astype(jnp.bfloat16)
         table, everyone, idx, mix = spread(node_table, packed, place, near, live)
-        row_inner, row_outer = weight_inner.shape[0], weight_outer.shape[0]
-        full_inner = everyone[:, :row_inner].reshape(-1, hidden)
-        full_outer = everyone[:, row_inner : row_inner + row_outer].reshape(-1, hidden)
-        full_head = everyone[:, row_inner + row_outer :].reshape(-1, hidden)[:, :classes]
-        counts = everyone[:peers, row_inner + row_outer, classes : classes + 2].astype(jnp.float32)
-        label_count = jnp.maximum(jnp.sum(counts[:, 0] * 256 + counts[:, 1]), 1.0)
-        summed, self_rows = picked(idx, mix, table)
-    else:
-        label_count = jnp.maximum(lax.psum(label_part, "dp"), 1.0)
-        full_inner, full_outer, full_head = (
-            lax.all_gather(weight.astype(jnp.bfloat16), every, axis=0, tiled=True)
-            for weight in weights
+        firsts = (first_inner, first_outer, first_head)
+        seconds = (second_inner, second_outer, second_head)
+        smooths = (smooth_inner, smooth_outer, smooth_head)
+        rows = [weight.shape[0] for weight in weights]
+
+        def in_rows(*arrays):
+            return jnp.concatenate(
+                [jnp.pad(a, (0, 3 * hidden - a.shape[0])).reshape(3, hidden) for a in arrays]
+            )
+
+        bias_rows = in_rows(biases, first_biases, second_biases, smooth_biases)
+        keep_outer = jnp.arange(fan_outer)[None, :] < outer_counts[:, None]
+        seed_table = jnp.concatenate(
+            [
+                jnp.where(keep_outer, outer_neighbours, -1),
+                labels[:, None],
+                label_mask[:, None],
+                jnp.zeros((seed_count, SLOT - fan_outer - 2), jnp.int32),
+            ],
+            axis=1,
         )
-        source, place = gathered_rows(node_table, owner_ids, row_ids)
-        rows = source[place[inner_neighbours]]
-        summed = jnp.sum(
-            jnp.where(keep[:, :, None], rows, jnp.zeros((), rows.dtype)), axis=1, dtype=jnp.float32
+        joined_one = picked(idx, mix, table)
+        grads, extra = dense(
+            (classes, fan_outer, *rows), joined_one, everyone, bias_rows, seed_table
         )
-        self_rows = source[place[:dest_count]]
+        sums = reduced((classes, *rows), grads, extra, weights, firsts, seconds)
+        scalars, norms, news, moment, square, average, bias_out = finished(
+            (classes, *rows), sums, weights, firsts, seconds, smooths, bias_rows
+        )
+        bias_outs = [
+            bias_out[4 * k : 4 * k + 3].reshape(-1)[: biases.shape[0]] for k in range(4)
+        ]
+        return (
+            scalars[0, 0],
+            extra[3, 1],
+            scalars[1, 1],
+            norms,
+            *news,
+            bias_outs[0],
+            *moment,
+            bias_outs[1],
+            *square,
+            bias_outs[2],
+            *average,
+            bias_outs[3],
+        )
+
+    label_count = jnp.maximum(lax.psum(label_part, "dp"), 1.0)
+    full_inner, full_outer, full_head = (
+        lax.all_gather(weight.astype(jnp.bfloat16), every, axis=0, tiled=True)
+        for weight in weights
+    )
+    source, place = gathered_rows(node_table, owner_ids, row_ids)
+    rows = source[place[inner_neighbours]]
+    summed = jnp.sum(
+        jnp.where(keep[:, :, None], rows, jnp.zeros((), rows.dtype)), axis=1, dtype=jnp.float32
+    )
+    self_rows = source[place[:dest_count]]
     mean_one = (summed / inner_counts[:, None].astype(jnp.float32)).astype(jnp.bfloat16)
     joined_one = jnp.concatenate([self_rows, mean_one], axis=1)
     pre_one = jnp.dot(joined_one, full_inner, preferred_element_type=jnp.float32) + bias_inner

time: 476 us -> 253 us (0.53)
  waiting for transfers between devices: 127 us -> 0 us
  blocking collectives: 80.4 us -> 0 us
  Pallas kernels: 160 us -> 208 us
  other arithmetic: 37.2 us -> 5.38 us
  between operations: 29.9 us -> 2.45 us
  matrix products: 8.21 us -> 0 us
    unnamed x2 -> x0, waiting for transfers between devices: 127 us -> none
    psum x2 -> x0, blocking collectives: 80.4 us -> none  [the longest x1 40.5 us: on_device(): packed = lax.psum(jnp.concatenate([bias_part, loss_part[None]]), every)]
    pallas_call x1 -> x4, Pallas kernels: 31.7 us -> 80.4 us  [the longest x1 32.9 us: reduced(): pl.pallas_call(functools.partial(reduce_kernel, sizes), out_shape=jax.Sha...]
    reduce_sum x19 -> x0, other arithmetic: 20 us -> none  [the longest x3 4.57 us: on_device(): grad_partial = sum((jnp.sum(part * part) for part in shards))]
    dot_general x11 -> x0, matrix products: 8.21 us -> none  [the longest x1 2.85 us: on_device(): jnp.dot(joined_one, full_inner, preferred_element_type=jnp.float32)]
    unnamed x66 -> x45, local copies, waits for them, and re-layouts: 25.1 us -> 26 us
  transfers between devices with their start and end apart: 1 -> 0, of which waited for: 1 -> 0; matrix products, arithmetic and copies ran while one was open for 0% -> 0% of each run, Pallas kernels for 0% -> 0%
where the time goes in v3:
time: 253 us; the launch traced here: 252 us
  Pallas kernels  208 us (82%)
  local copies, waits for them, and re-layouts  36.3 us (14%)
  other arithmetic  5.38 us (2%)
    pallas_call x1, Pallas kernels, spread(): pl.pallas_call(spread_kernel, out_shape=(pltpu.VMEM((lax.axis_size('dp')...  128 us
    pallas_call x1, Pallas kernels, reduced(): pl.pallas_call(functools.partial(reduce_kernel, sizes), out_shape=jax.Sha...  32.9 us
    pallas_call x1, Pallas kernels, picked(): pl.pallas_call(pick_kernel, out_shape=jax.ShapeDtypeStruct((rows, 2 * wid...  31.6 us
    unnamed x45, local copies, waits for them, and re-layouts  26 us
    pallas_call x1, Pallas kernels, dense(): pl.pallas_call(functools.partial(dense_kernel, sizes), out_shape=(jax.Sha...  14.1 us

profile of v3, /device:TPU:0, one launch (start us, length us, event | category | flops | bytes accessed | tf_op | source)
XLA Modules:
  0.0 252.3 jit_solution(613132143124508587)
XLA Ops:
  0.7 1.4 convert_reduce_fusion
  3.5 0.7 convert.26
  4.2 0.7 convert.25
  4.9 0.7 convert.27
  5.7 0.1 constant_dynamic-slice_fusion.4
  5.9 0.4 copy.56
  6.3 0.6 reshape.95.near_ref
  7.0 0.8 dynamic-slice_reduce_fusion
  7.8 1.3 iota_compare_fusion
  9.1 0.1 pad_convert_fusion
  9.3 0.6 reshape.108.live_ref
  9.9 0.1 copy-done.15
  10.2 2.2 copy-done.3
  12.4 127.7 %shard_map.392 = (bf16[65536,2,128]{2,1,0:T(2,128)(2,1)S(1)}, bf16[32,32,256]{2,1,0:T(8,128)(2,1)S(1)}, s32[176,256]{1,0:T(8,128)S(1)}, f32[176,512]{1,0:T(8,128)S(1)}) custom-call(bf16[8192,2,128]{2,1,0:T(2,128)(2,1)S(1)} %bitcast.31, bf16[32,256]{1,0:T(8,128)(2,1)S(1)} %fusion.4.weight_ref, s32[128,240]{1,0:T(8,128)S(1)} %bitcast.33, ...), custom_call_target="tpu_custom_call" | custom-call | tf_op jit(solution)/shard_map/pallas_call | solution.py:260
  140.2 11.1 %copy-done.1 = bf16[65536,2,128]{2,1,0:T(2,128)(2,1)} copy-done((bf16[65536,2,128]{2,1,0:T(2,128)(2,1)}, bf16[65536,2,128]{2,1,0:T(2,128)(2,1)S(1)}, u32[]{:S(2)}) %copy-start.1) | copy-done | bytes 33554456
  151.4 10.5 %copy-done.2 = bf16[65536,2,128]{2,1,0:T(2,128)(2,1)S(1)} copy-done((bf16[65536,2,128]{2,1,0:T(2,128)(2,1)S(1)}, bf16[65536,2,128]{2,1,0:T(2,128)(2,1)}, u32[]{:S(2)}) %copy-start.2) | copy-done | bytes 33554456
  161.9 31.6 %shard_map.393.joined_ref = bf16[2816,256]{1,0:T(8,128)(2,1)S(1)} custom-call(s32[45056]{0:T(1024)S(1)} %bitcast.32, f32[176,512]{1,0:T(8,128)S(1)} %get-tuple-element.42.mix_ref, bf16[65536,2,128]{2,1,0:T(2,128)(2,1)S(1)} %copy-done.2), custom_call_target="tpu_custom_call" | custom-call | tf_op jit(solution)/shard_map/pallas_call | solution.py:348
  193.7 0.7 constant_dynamic-slice_fusion.3
  194.4 0.8 constant_dynamic-slice_fusion.2
  195.2 0.7 fusion.7
  196.4 14.1 %shard_map.394 = (f32[32,32,256]{2,1,0:T(8,128)S(1)}, f32[8,256]{1,0:T(8,128)S(1)}) custom-call(bf16[2816,256]{1,0:T(8,128)(2,1)S(1)} %shard_map.393.joined_ref, bf16[32,32,256]{2,1,0:T(8,128)(2,1)S(1)} %get-tuple-element.44.everyone_ref, f32[12,256]{1,0:T(8,128)S(1)} %pad_maximum_fusion.bias_ref, s32[256,16]{1,0:T(8,128)S(1)} %copy.58.seed_ref, ...), custom_call_target="tpu_custom_call" | custom-call | tf_op jit(solution)/shard_map/pallas_call | solution.py:501
  210.6 32.9 %shard_map.395.sums_ref = f32[48,256]{1,0:T(8,128)S(1)} custom-call(f32[32,32,256]{2,1,0:T(8,128)S(1)} %get-tuple-element.45.grads_ref, f32[8,256]{1,0:T(8,128)S(1)} %get-tuple-element.46.extra_ref, f32[8,256]{1,0:T(8,128)S(1)} %copy-done.8, f32[16,256]{1,0:T(8,128)S(1)} %copy-done.5, f32[8,172]{1,0:T(8,128)S(1)} %copy-done.7, f32[8,256]{1,0:T(8,128)S(1)} %copy-done.11, ...), custom_call_target="tpu_custom_call" | custom-call | tf_op jit(solution)/shard_map/pallas_call | solution.py:651
  243.5 0.6 copy-done.4
  244.1 1.8 shard_map.396
  245.9 0.8 fusion.8
  246.7 0.6 reshape.103
  247.3 0.6 reshape.104
  247.9 0.6 reshape.105
  248.5 0.6 reshape.106
  249.1 1.3 fusion.9
  250.4 1.3 copy.59
  251.7 0.6 slice.34
  (61 shorter events, 1.0 us)
Async XLA Ops:
  0.7 5.0 %copy-start = (s32[4,2816,15]{1,0,2:T(4,128)S(1)}, s32[4,2816,15]{1,0,2:T(4,128)}, u32[]{:S(2)}) copy-start(s32[4,2816,15]{1,0,2:T(4,128)} %param.28) | copy-start | bytes 2027524
  9.1 0.9 copy-start.15
  9.1 1.0 copy-start.16
  10.2 2.2 copy-start.3
  140.2 11.1 %copy-start.1 = (bf16[65536,2,128]{2,1,0:T(2,128)(2,1)}, bf16[65536,2,128]{2,1,0:T(2,128)(2,1)S(1)}, u32[]{:S(2)}) copy-start(bf16[65536,2,128]{2,1,0:T(2,128)(2,1)S(1)} %get-tuple-element.43.table_ref) | copy-start | bytes 100663296
  151.3 10.5 %copy-start.2 = (bf16[65536,2,128]{2,1,0:T(2,128)(2,1)S(1)}, bf16[65536,2,128]{2,1,0:T(2,128)(2,1)}, u32[]{:S(2)}) copy-start(bf16[65536,2,128]{2,1,0:T(2,128)(2,1)} %copy-done.1) | copy-start | bytes 100663296
  161.9 34.3 %copy-start.17 = (f32[684]{0:T(1024)S(1)}, f32[684]{0:T(1024)}, u32[]{:S(2)}) copy-start(f32[684]{0:T(1024)} %param.41) | copy-start | bytes 8212
  161.9 34.4 %copy-start.18 = (f32[684]{0:T(1024)S(1)}, f32[684]{0:T(1024)}, u32[]{:S(2)}) copy-start(f32[684]{0:T(1024)} %param.45) | copy-start | bytes 8212
  161.9 34.4 %copy-start.19 = (f32[684]{0:T(1024)S(1)}, f32[684]{0:T(1024)}, u32[]{:S(2)}) copy-start(f32[684]{0:T(1024)} %param.49) | copy-start | bytes 8212
  161.9 34.4 %copy-start.20 = (f32[684]{0:T(1024)S(1)}, f32[684]{0:T(1024)}, u32[]{:S(2)}) copy-start(f32[684]{0:T(1024)} %param.37) | copy-start | bytes 8212
  193.5 17.0 %copy-start.5 = (f32[16,256]{1,0:T(8,128)S(1)}, f32[16,256]{1,0:T(8,128)}, u32[]{:S(2)}) copy-start(f32[16,256]{1,0:T(8,128)} %weight_refs_1_.3) | copy-start | bytes 49156
  193.6 17.0 %copy-start.7 = (f32[8,172]{1,0:T(8,128)S(1)}, f32[8,172]{1,0:T(8,128)}, u32[]{:S(2)}) copy-start(f32[8,172]{1,0:T(8,128)} %weight_refs_2_.3) | copy-start | bytes 16516
  193.6 17.0 %copy-start.8 = (f32[8,256]{1,0:T(8,128)S(1)}, f32[8,256]{1,0:T(8,128)}, u32[]{:S(2)}) copy-start(f32[8,256]{1,0:T(8,128)} %weight_refs_0_.3) | copy-start | bytes 24580
  193.6 17.0 %copy-start.9 = (f32[16,256]{1,0:T(8,128)S(1)}, f32[16,256]{1,0:T(8,128)}, u32[]{:S(2)}) copy-start(f32[16,256]{1,0:T(8,128)} %first_refs_1_.3) | copy-start | bytes 49156
  193.6 17.0 %copy-start.10 = (f32[16,256]{1,0:T(8,128)S(1)}, f32[16,256]{1,0:T(8,128)}, u32[]{:S(2)}) copy-start(f32[16,256]{1,0:T(8,128)} %second_refs_1_.3) | copy-start | bytes 49156
  193.6 17.0 %copy-start.11 = (f32[8,256]{1,0:T(8,128)S(1)}, f32[8,256]{1,0:T(8,128)}, u32[]{:S(2)}) copy-start(f32[8,256]{1,0:T(8,128)} %first_refs_0_.3) | copy-start | bytes 24580
  193.6 17.0 %copy-start.12 = (f32[8,172]{1,0:T(8,128)S(1)}, f32[8,172]{1,0:T(8,128)}, u32[]{:S(2)}) copy-start(f32[8,172]{1,0:T(8,128)} %first_refs_2_.3) | copy-start | bytes 16516
  193.6 17.0 %copy-start.13 = (f32[8,256]{1,0:T(8,128)S(1)}, f32[8,256]{1,0:T(8,128)}, u32[]{:S(2)}) copy-start(f32[8,256]{1,0:T(8,128)} %second_refs_0_.3) | copy-start | bytes 24580
  193.6 17.0 %copy-start.14 = (f32[8,172]{1,0:T(8,128)S(1)}, f32[8,172]{1,0:T(8,128)}, u32[]{:S(2)}) copy-start(f32[8,172]{1,0:T(8,128)} %second_refs_2_.3) | copy-start | bytes 16516
  196.4 47.1 %copy-start.6 = (f32[12,256]{1,0:T(8,128)}, f32[12,256]{1,0:T(8,128)S(1)}, u32[]{:S(2)}) copy-start(f32[12,256]{1,0:T(8,128)S(1)} %pad_maximum_fusion.bias_ref) | copy-start | bytes 36868
  243.5 0.6 copy-start.4

commit v4 on v3

--- a/solution.py
+++ b/solution.py
@@ -27,21 +27,36 @@
 CHUNKS = 4
 GROUP = 4
 SETS = 4
-
-
-def spread_kernel(
+SPARE = 8
+SPARE_EARLY = False
+TILE = 256
+
+
+def gather_kernel(
+    classes,
+    fan_outer,
     table_ref,
-    weight_ref,
+    weight_refs,
+    mask_ref,
     place_ref,
     near_ref,
-    live_ref,
+    seed_ref,
+    seed_across_ref,
+    joined_ref,
+    weights_ref,
+    hits_ref,
+    hits_back_ref,
     full_ref,
-    weights_ref,
+    packed,
+    parts,
     idx_ref,
     mix_ref,
-    parts,
+    wide,
+    stages,
+    lists,
     own_sem,
     z_sem,
+    spare_sem,
     x_sem,
     y_sem,
     far_sem,
@@ -50,19 +65,21 @@
     double_sem,
     send_sem,
     double_send_sem,
+    list_sem,
 ):
     section, at = lax.axis_index("section"), lax.axis_index("dp")
     z, core = at // 2, at % 2
     flipped = z // 2
     height = z + flipped * (3 - 2 * z)
     pairs = table_ref.shape[0]
-    quarter = pairs // 4
+    spare = pairs // SPARE
+    quarter = (pairs - spare) // 4
     chunk = quarter // CHUNKS
+    spare_chunk = spare // CHUNKS
 
     def level(value):
         return value + flipped * (3 - 2 * value)
 
-    here = (section, at)
     twin = (section, z * 2 + 1 - core)
     beside_x = (section + 1 - 2 * (section % 2), at)
     beside_y = (section + 2 - 4 * (section // 2), at)
@@ -86,8 +103,10 @@
     sent = []
 
     def region(shard, part, piece):
-        start_at = shard * pairs + part * quarter + piece * chunk
-        return full_ref.at[pl.ds(pl.multiple_of(start_at, chunk), chunk)]
+        return full_ref.at[pl.ds(shard * pairs + part * quarter + piece * chunk, chunk)]
+
+    def spare_region(shard, piece):
+        return full_ref.at[pl.ds(shard * pairs + 4 * quarter + piece * spare_chunk, spare_chunk)]
 
     def send(source, target, recv, device, when=None):
         number = len(sent)
@@ -109,15 +128,43 @@
     def arrived(target, recv):
         pltpu.make_async_copy(target, target, recv).wait()
 
+    for piece in range(CHUNKS):
+        block = table_ref.at[pl.ds(section * quarter + piece * chunk, chunk)]
+        goal = region(at, section, piece)
+        send(block, goal, z_sem.at[piece], inner_z)
+        send(block, goal, z_sem.at[CHUNKS + piece], across_z, crosses)
+        if SPARE_EARLY:
+            block = table_ref.at[pl.ds(4 * quarter + piece * spare_chunk, spare_chunk)]
+            goal = spare_region(at, piece)
+            send(block, goal, spare_sem.at[piece], inner_z)
+            send(block, goal, spare_sem.at[CHUNKS + piece], across_z, crosses)
+    whole = full_ref.at[pl.ds(at * pairs, pairs)]
+    own = pltpu.make_async_copy(table_ref, whole, own_sem)
+    own.start()
+    send(table_ref, whole, twin_own_sem, twin)
+
+    inner_ref, outer_ref, head_ref = weight_refs
+    row_inner, row_outer, row_head = (ref.shape[0] for ref in weight_refs)
+    hidden = inner_ref.shape[1]
+    head_at = row_inner + row_outer
+    packed[0:row_inner, :] = inner_ref[...]
+    packed[row_inner:head_at, :] = outer_ref[...]
+    packed[head_at:, :] = jnp.zeros((row_head, hidden), jnp.float32)
+    packed[head_at:, 0:classes] = head_ref[...]
+    labelled = jnp.sum(mask_ref[...].astype(jnp.float32)).astype(jnp.int32)
+    lane = lax.broadcasted_iota(jnp.int32, (1, hidden), 1)
+    high_part = (labelled // 256).astype(jnp.float32)
+    low_part = (labelled % 256).astype(jnp.float32)
+    tail = jnp.where(lane == classes, high_part, jnp.where(lane == classes + 1, low_part, 0.0))
+    packed[head_at : head_at + 1, :] += tail
     mine = (core * 4 + section) * 4 + z
-    pltpu.sync_copy(weight_ref, weights_ref.at[mine])
+    weights_ref[mine] = packed[...].astype(jnp.bfloat16)
     doubling = [(inner_z, 1), (skip_z, 2), (beside_x, 4), (beside_y, 8), (twin, 16)]
     doubled = []
 
     def double_start(number):
         device, size = doubling[number]
-        start_at = (mine // size) * size
-        block = weights_ref.at[pl.ds(start_at, size)]
+        block = weights_ref.at[pl.ds((mine // size) * size, size)]
         copy = pltpu.make_async_remote_copy(
             src_ref=block,
             dst_ref=block,
@@ -130,16 +177,6 @@
         doubled.append(copy)
 
     double_start(0)
-    for piece in range(CHUNKS):
-        start_at = section * quarter + piece * chunk
-        block = table_ref.at[pl.ds(pl.multiple_of(start_at, chunk), chunk)]
-        goal = region(at, section, piece)
-        send(block, goal, z_sem.at[piece], inner_z)
-        send(block, goal, z_sem.at[CHUNKS + piece], across_z, crosses)
-    whole = full_ref.at[pl.ds(pl.multiple_of(at * pairs, pairs), pairs)]
-    own = pltpu.make_async_copy(table_ref, whole, own_sem)
-    own.start()
-    send(table_ref, whole, twin_own_sem, twin)
 
     placed = place_ref[...]
     pair_at = placed // 2
@@ -148,8 +185,13 @@
     parts[128:256, :] = (pair_at // 256).astype(jnp.float32).astype(jnp.bfloat16)
     parts[256:384, :] = (placed % 2).astype(jnp.float32).astype(jnp.bfloat16)
     looked_rows = near_ref.shape[0]
-    steps = 3 * CHUNKS + 2
+    seeds = seed_ref.shape[0]
+    tiles = hits_ref.shape[1] // TILE
+    total = 3 * CHUNKS
+    steps = total + 2
     per_step = -(-looked_rows // (8 * steps)) * 8
+    for j in range(fan_outer):
+        wide[j] = jnp.broadcast_to(seed_ref[:, j : j + 1], (seeds, TILE))
 
     def look_up(first, last):
         def rows_of(block, carry):
@@ -165,12 +207,13 @@
                 chosen = low_at == node % 128
                 found = jnp.where(chosen, got[0:128] + 256.0 * got[128:256], 0.0)
                 odd = jnp.where(chosen, got[256:384], 0.0)
-                idx_ref[pl.ds(start_at + k, 1), :] = jnp.sum(found, axis=0, keepdims=True).astype(
-                    jnp.int32
+                entry_at = jnp.sum(found, axis=0, keepdims=True).astype(jnp.int32)
+                idx_ref[block * 2 + k // 4, k % 4 : k % 4 + 1, :] = jnp.clip(
+                    entry_at, 0, full_ref.shape[0] - 1
                 )
                 mix_ref[pl.ds(start_at + k, 1), 0:256] = jnp.sum(odd, axis=0, keepdims=True)
             odd = mix_ref[pl.ds(start_at, 8), 0:256]
-            live = live_ref[pl.ds(start_at, 8), :]
+            live = (near_ref[pl.ds(start_at, 8), :] >= 0).astype(jnp.float32)
             mix_ref[pl.ds(start_at, 8), :] = jnp.dot(
                 (live * (1.0 - odd)).astype(jnp.bfloat16),
                 (column == 2 * row).astype(jnp.float32).astype(jnp.bfloat16),
@@ -184,7 +227,19 @@
 
         lax.fori_loop(first // 8, last // 8, rows_of, 0)
 
-    total = 3 * CHUNKS
+    def mark(tile):
+        start_at = tile * TILE
+        dest = lax.broadcasted_iota(jnp.int32, (seeds, TILE), 1) + start_at
+        hits = jnp.zeros((seeds, TILE), jnp.float32)
+        for j in range(fan_outer):
+            hits = hits + (wide[j] == dest).astype(jnp.float32)
+        hits_ref[:, start_at : start_at + TILE] = hits.astype(jnp.bfloat16)
+        dest = lax.broadcasted_iota(jnp.int32, (TILE, seeds), 0) + start_at
+        hits = jnp.zeros((TILE, seeds), jnp.float32)
+        for j in range(fan_outer):
+            hits = hits + (seed_across_ref[j : j + 1, :] == dest).astype(jnp.float32)
+        hits_back_ref[start_at : start_at + TILE, :] = hits.astype(jnp.bfloat16)
+
     twins = []
 
     def to_twin(block, number):
@@ -195,19 +250,27 @@
         if step < total:
             turn, piece = divmod(step, CHUNKS)
             shard = sources[turn] * 2 + core
+            goes, number = (across_z, 2 * CHUNKS + piece) if turn == 0 else (outer_z, step)
             block = region(shard, section, piece)
             arrived(block, z_sem.at[step])
-            if turn == 0:
-                send(block, block, z_sem.at[2 * CHUNKS + piece], across_z, crosses)
-            else:
-                send(block, block, z_sem.at[step], outer_z, crosses)
+            send(block, block, z_sem.at[number], goes, crosses)
             send(block, block, x_sem.at[step], beside_x)
             send(block, block, y_sem.at[step], beside_y)
             to_twin(block, step)
+            if not SPARE_EARLY and turn == 0:
+                block = table_ref.at[pl.ds(4 * quarter + piece * spare_chunk, spare_chunk)]
+                goal = spare_region(at, piece)
+                send(block, goal, spare_sem.at[piece], inner_z)
+                send(block, goal, spare_sem.at[CHUNKS + piece], across_z, crosses)
         late = step - 1
         if 0 <= late < total:
             turn, piece = divmod(late, CHUNKS)
             shard = sources[turn] * 2 + core
+            goes, number = (across_z, 2 * CHUNKS + piece) if turn == 0 else (outer_z, late)
+            block = spare_region(shard, piece)
+            arrived(block, spare_sem.at[late])
+            send(block, block, spare_sem.at[number], goes, crosses)
+            to_twin(block, 4 * total + late)
             block = region(shard, beside_x[0], piece)
             arrived(block, x_sem.at[late])
             if piece % 2 == 0:
@@ -233,79 +296,40 @@
         last = min(first + per_step, looked_rows)
         if last > first:
             look_up(first, last)
-
-    for number in range(len(twins)):
+        for tile in range(step * tiles // steps, (step + 1) * tiles // steps):
+            mark(tile)
+
+    for number in sorted(twins):
         kind, step = divmod(number, total)
         turn, piece = divmod(step, CHUNKS)
-        part = (section, beside_x[0], beside_y[0], 3 - section)[kind]
-        arrived(region(sources[turn] * 2 + 1 - core, part, piece), twin_sem.at[number])
-    other = full_ref.at[pl.ds(pl.multiple_of((z * 2 + 1 - core) * pairs, pairs), pairs)]
-    arrived(other, twin_own_sem)
+        shard = sources[turn] * 2 + 1 - core
+        if kind == 4:
+            block = spare_region(shard, piece)
+        else:
+            block = region(shard, (section, beside_x[0], beside_y[0], 3 - section)[kind], piece)
+        arrived(block, twin_sem.at[number])
+    arrived(full_ref.at[pl.ds((z * 2 + 1 - core) * pairs, pairs)], twin_own_sem)
     own.wait()
-    for copy, when in sent:
-        if when is None:
-            copy.wait_send()
-        else:
-            pl.when(when)(copy.wait_send)
-
-
-def spread(node_table, packed, place, near, live):
-    devices = lax.axis_size(("section", "dp"))
-    table_rows = node_table.shape[0]
-    frontier_high = place.shape[1]
-    looked = near.shape[0]
-    total = 3 * CHUNKS
-    sends = 2 * CHUNKS + 1 + 3 * total + total + 4 * total
-    vmem = pl.BlockSpec(memory_space=pltpu.VMEM)
-    return pl.pallas_call(
-        spread_kernel,
-        out_shape=(
-            pltpu.VMEM((lax.axis_size("dp") * table_rows // 2, 2, node_table.shape[1]), jnp.bfloat16),
-            jax.ShapeDtypeStruct((devices,) + packed.shape, packed.dtype),
-            jax.ShapeDtypeStruct((looked, 256), jnp.int32),
-            jax.ShapeDtypeStruct((looked, 512), jnp.float32),
-        ),
-        in_specs=[pl.BlockSpec(memory_space=pl.ANY), vmem, vmem, vmem, vmem],
-        out_specs=(vmem, vmem, vmem, vmem),
-        scratch_shapes=[
-            pltpu.VMEM((384, frontier_high), jnp.bfloat16),
-            pltpu.SemaphoreType.DMA(()),
-            pltpu.SemaphoreType.DMA((total,)),
-            pltpu.SemaphoreType.DMA((total,)),
-            pltpu.SemaphoreType.DMA((total,)),
-            pltpu.SemaphoreType.DMA((total,)),
-            pltpu.SemaphoreType.DMA((4 * total,)),
-            pltpu.SemaphoreType.DMA(()),
-            pltpu.SemaphoreType.DMA((5,)),
-            pltpu.SemaphoreType.DMA((sends,)),
-            pltpu.SemaphoreType.DMA((5,)),
-        ],
-        compiler_params=pltpu.CompilerParams(
-            collective_id=0, has_side_effects=True, vmem_limit_bytes=12 * 2**20
-        ),
-    )(node_table.reshape(table_rows // 2, 2, -1), packed, place, near, live)
-
-
-def pick_kernel(idx_ref, mix_ref, table_ref, joined_ref, *scratch):
-    blocks = mix_ref.shape[0]
-    stages = (scratch[:GROUP], scratch[GROUP : 2 * GROUP])
-    lists = scratch[2 * GROUP : 2 * GROUP + SETS]
-    sems = scratch[2 * GROUP + SETS]
-    words = GROUP * BLOCK * SLOT
+
+    blocks = looked_rows
     lane = lax.broadcasted_iota(jnp.int32, (BLOCK, 2 * BLOCK * SLOT), 1)
     same = lane // (2 * SLOT) == lax.broadcasted_iota(jnp.int32, lane.shape, 0)
     near_part = jnp.logical_and(same, lane % (2 * SLOT) < 2 * SLOT - 2).astype(jnp.float32)
     self_part = jnp.logical_and(same, lane % (2 * SLOT) >= 2 * SLOT - 2).astype(jnp.float32)
-    last = blocks // GROUP - 1
+    turns = blocks // GROUP
 
     def fetch(turn, slot):
-        start_at = pl.multiple_of(jnp.minimum(turn, last) * words, words)
-        return pltpu.make_async_copy(idx_ref.at[pl.ds(start_at, words)], lists[slot], sems.at[slot])
+        return pltpu.make_async_copy(
+            idx_ref.at[jnp.minimum(turn, turns - 1)], lists[slot], list_sem.at[slot]
+        )
 
     def pick(member, slot, stage):
-        for unit in range(BLOCK * SLOT):
-            entry = table_ref[lists[slot][member * BLOCK * SLOT + unit]]
-            stage[pl.ds(2 * unit, 2), :] = entry.astype(jnp.float32)
+        def unit(number, carry):
+            entry = full_ref[lists[slot][member, number]]
+            stage[pl.ds(2 * number, 2), :] = entry.astype(jnp.float32)
+            return carry
+
+        lax.fori_loop(0, BLOCK * SLOT, unit, 0, unroll=BLOCK * SLOT)
 
     def reduce(block, stage):
         mix = mix_ref[pl.ds(block, 1), :]
@@ -317,10 +341,11 @@
         start_at = pl.multiple_of(block * BLOCK, BLOCK)
         joined_ref[pl.ds(start_at, BLOCK), :] = both.astype(jnp.bfloat16)
 
+    near_stages, far_stages = stages
     for slot in range(SETS):
         fetch(slot, slot).start()
     for member in range(GROUP):
-        stages[1][member][...] = jnp.zeros(stages[1][member].shape, jnp.float32)
+        far_stages[member][...] = jnp.zeros(far_stages[member].shape, jnp.float32)
 
     def round_of(number, carry):
         for slot in range(SETS):
@@ -339,25 +364,72 @@
         fetch(0, slot).wait()
     for member in range(GROUP):
         reduce(blocks - GROUP + member, stages[(SETS - 1) % 2][member])
-
-
-def picked(idx, mix, table):
-    rows = mix.shape[0] * BLOCK
-    width = table.shape[2]
+    for copy, when in sent:
+        if when is None:
+            copy.wait_send()
+        else:
+            pl.when(when)(copy.wait_send)
+
+
+def gathered(classes, fan_outer, node_table, weights, label_mask, place, near, seed_table):
+    devices = lax.axis_size(("section", "dp"))
+    table_rows, width = node_table.shape
+    frontier_high = place.shape[1]
+    looked = near.shape[0]
+    dest_count = looked * BLOCK
+    seeds = seed_table.shape[0]
+    hidden = weights[0].shape[1]
+    rows = sum(weight.shape[0] for weight in weights)
+    total = 3 * CHUNKS
+    sends = 4 * CHUNKS + 1 + 3 * total + total + total + 5 * total
     vmem = pl.BlockSpec(memory_space=pltpu.VMEM)
+    stage = (pltpu.VMEM((2 * BLOCK * SLOT, width), jnp.float32),) * GROUP
     return pl.pallas_call(
-        pick_kernel,
-        out_shape=jax.ShapeDtypeStruct((rows, 2 * width), jnp.bfloat16),
-        in_specs=[pl.BlockSpec(memory_space=pl.ANY), vmem, vmem],
-        out_specs=vmem,
-        scratch_shapes=[pltpu.VMEM((2 * BLOCK * SLOT, width), jnp.float32)] * (2 * GROUP)
-        + [pltpu.SMEM((GROUP * BLOCK * SLOT,), jnp.int32)] * SETS
-        + [pltpu.SemaphoreType.DMA((SETS,))],
-        compiler_params=pltpu.CompilerParams(vmem_limit_bytes=16 * 2**20),
-    )(idx.reshape(-1), mix, table)
-
-
-TILE = 256
+        functools.partial(gather_kernel, classes, fan_outer),
+        out_shape=(
+            jax.ShapeDtypeStruct((dest_count, 2 * width), jnp.bfloat16),
+            jax.ShapeDtypeStruct((devices, rows, hidden), jnp.bfloat16),
+            jax.ShapeDtypeStruct((seeds, dest_count), jnp.bfloat16),
+            jax.ShapeDtypeStruct((dest_count, seeds), jnp.bfloat16),
+        ),
+        in_specs=[pl.BlockSpec(memory_space=pl.ANY), (vmem,) * 3] + [vmem] * 5,
+        out_specs=(vmem,) * 4,
+        scratch_shapes=[
+            pltpu.VMEM((lax.axis_size("dp") * table_rows // 2, 2, width), jnp.bfloat16),
+            pltpu.VMEM((rows, hidden), jnp.float32),
+            pltpu.VMEM((384, frontier_high), jnp.bfloat16),
+            pltpu.VMEM((looked // GROUP, GROUP, 256), jnp.int32),
+            pltpu.VMEM((looked, 512), jnp.float32),
+            pltpu.VMEM((fan_outer, seeds, TILE), jnp.int32),
+            (stage, stage),
+            (pltpu.SMEM((GROUP, BLOCK * SLOT), jnp.int32),) * SETS,
+            pltpu.SemaphoreType.DMA(()),
+            pltpu.SemaphoreType.DMA((total,)),
+            pltpu.SemaphoreType.DMA((total,)),
+            pltpu.SemaphoreType.DMA((total,)),
+            pltpu.SemaphoreType.DMA((total,)),
+            pltpu.SemaphoreType.DMA((total,)),
+            pltpu.SemaphoreType.DMA((5 * total,)),
+            pltpu.SemaphoreType.DMA(()),
+            pltpu.SemaphoreType.DMA((5,)),
+            pltpu.SemaphoreType.DMA((sends,)),
+            pltpu.SemaphoreType.DMA((5,)),
+            pltpu.SemaphoreType.DMA((SETS,)),
+        ],
+        compiler_params=pltpu.CompilerParams(
+            collective_id=0, has_side_effects=True, vmem_limit_bytes=52 * 2**20
+        ),
+    )(
+        pltpu.with_memory_space_constraint(
+            node_table.reshape(table_rows // 2, 2, width), pltpu.HBM
+        ),
+        weights,
+        label_mask,
+        place,
+        near,
+        seed_table,
+        seed_table.T,
+    )
 
 
 def block_order():
@@ -368,16 +440,15 @@
     sizes,
     joined_ref,
     everyone_ref,
+    hits_ref,
+    hits_back_ref,
     bias_ref,
     seed_ref,
-    seed_across_ref,
     grads_ref,
     extra_ref,
     first_pre,
     first_hidden,
-    wide,
-    mean_sum,
-    pick_back,
+    own_part,
     inner_sum,
 ):
     classes, fan_outer, row_inner, row_outer, row_head = sizes
@@ -398,13 +469,10 @@
     full_inner = full_inner.astype(jnp.bfloat16)
     full_outer = full_outer.astype(jnp.bfloat16)
     full_head = jnp.where(lane < classes, full_head, 0.0).astype(jnp.bfloat16)
-    bias_inner, bias_outer, bias_head = (bias_ref[k : k + 1, :] for k in range(3))
+    bias_inner, bias_outer, bias_head = bias_rows_of(bias_ref, hidden)
     seeds = seed_ref.shape[0]
     kept = seed_ref[:, 0:fan_outer]
     count_two = jnp.sum((kept >= 0).astype(jnp.float32), axis=1, keepdims=True)
-    for j in range(fan_outer):
-        wide[j] = jnp.broadcast_to(seed_ref[:, j : j + 1], (seeds, TILE))
-    mean_sum[...] = jnp.zeros(mean_sum.shape, jnp.float32)
 
     def forward(tile, carry):
         start_at = pl.multiple_of(tile * TILE, TILE)
@@ -415,17 +483,11 @@
         first_pre[rows, :] = before
         out = (before * lax.logistic(before)).astype(jnp.bfloat16)
         first_hidden[rows, :] = out
-        dest = lax.broadcasted_iota(jnp.int32, (seeds, TILE), 1) + start_at
-        hits = jnp.zeros((seeds, TILE), jnp.float32)
-        for j in range(fan_outer):
-            hits = hits + (wide[j] == dest).astype(jnp.float32)
-        mean_sum[...] += jnp.dot(
-            hits.astype(jnp.bfloat16), out, preferred_element_type=jnp.float32
-        )
         return carry
 
     lax.fori_loop(0, tiles, forward, 0)
-    mean_two = (mean_sum[...] / count_two).astype(jnp.bfloat16)
+    mean_sum = jnp.dot(hits_ref[...], first_hidden[...], preferred_element_type=jnp.float32)
+    mean_two = (mean_sum / count_two).astype(jnp.bfloat16)
     joined_two = jnp.concatenate([first_hidden[0:seeds, :], mean_two], axis=1)
     pre_two = jnp.dot(joined_two, full_outer, preferred_element_type=jnp.float32) + bias_outer
     gate_two = lax.logistic(pre_two)
@@ -462,11 +524,7 @@
     def backward(tile, bias_sum, own=None):
         start_at = pl.multiple_of(jnp.int32(tile) * TILE, TILE)
         rows = pl.ds(start_at, TILE)
-        dest = lax.broadcasted_iota(jnp.int32, (TILE, seeds), 0) + start_at
-        hits = jnp.zeros((TILE, seeds), jnp.float32)
-        for j in range(fan_outer):
-            hits = hits + (seed_across_ref[j : j + 1, :] == dest).astype(jnp.float32)
-        hits = hits.astype(jnp.bfloat16)
+        hits = hits_back_ref[rows, :]
         both_hits = jnp.concatenate([hits, hits], axis=1)
         grad_one = jnp.dot(both_hits, share_parts, preferred_element_type=jnp.float32)
         if own is not None:
@@ -478,9 +536,9 @@
         inner_sum[...] += outer_product(joined_ref[rows, :], grad_pre)
         return bias_sum + jnp.sum(grad_pre.astype(jnp.float32), axis=0, keepdims=True)
 
-    pick_back[...] = jnp.zeros(pick_back.shape, jnp.float32)
-    pick_back[0:seeds, :] = grad_joined[:, 0:hidden]
-    bias_sum = backward(0, jnp.zeros((1, hidden), jnp.float32), pick_back[...])
+    own_part[...] = jnp.zeros(own_part.shape, jnp.float32)
+    own_part[0:seeds, :] = grad_joined[:, 0:hidden]
+    bias_sum = backward(0, jnp.zeros((1, hidden), jnp.float32), own_part[...])
     bias_sum = lax.fori_loop(1, tiles, backward, bias_sum)
     grad_inner = inner_sum[...]
     for number, place in enumerate(order):
@@ -494,9 +552,18 @@
     extra_ref[4:8, :] = jnp.zeros((4, hidden), jnp.float32)
 
 
-def dense(sizes, joined, everyone, bias_rows, seed_table):
+def bias_rows_of(ref, hidden):
+    width = ref.shape[0] - 2 * hidden
+    last = ref[pl.ds(2 * hidden, width)].reshape(1, width)
+    return (
+        ref[pl.ds(0, hidden)].reshape(1, hidden),
+        ref[pl.ds(hidden, hidden)].reshape(1, hidden),
+        jnp.concatenate([last, jnp.zeros((1, hidden - width), jnp.float32)], axis=1),
+    )
+
+
+def dense(sizes, joined, everyone, hits, hits_back, biases, seed_table):
     dest_count, hidden = joined.shape
-    seeds = seed_table.shape[0]
     vmem = pl.BlockSpec(memory_space=pltpu.VMEM)
     return pl.pallas_call(
         functools.partial(dense_kernel, sizes),
@@ -504,18 +571,16 @@
             jax.ShapeDtypeStruct(everyone.shape, jnp.float32),
             jax.ShapeDtypeStruct((8, hidden), jnp.float32),
         ),
-        in_specs=[vmem] * 5,
+        in_specs=[vmem] * 6,
         out_specs=(vmem, vmem),
         scratch_shapes=[
             pltpu.VMEM((dest_count, hidden), jnp.float32),
             pltpu.VMEM((dest_count, hidden), jnp.bfloat16),
-            pltpu.VMEM((sizes[1], seeds, TILE), jnp.int32),
-            pltpu.VMEM((seeds, hidden), jnp.float32),
             pltpu.VMEM((TILE, hidden), jnp.float32),
             pltpu.VMEM((hidden, hidden), jnp.float32),
         ],
         compiler_params=pltpu.CompilerParams(vmem_limit_bytes=32 * 2**20),
-    )(joined, everyone, bias_rows, seed_table, seed_table.T)
+    )(joined, everyone, hits, hits_back, biases, seed_table)
 
 
 def reduce_kernel(
@@ -531,10 +596,8 @@
     fourth,
     plane_in,
     line_in,
-    extra_twin,
     extra_plane,
     extra_line,
-    sums_twin,
     sums_plane,
     sums_line,
     recv_sem,
@@ -545,11 +608,12 @@
     rows, hidden = grads_ref.shape[1], grads_ref.shape[2]
     twin = (section, z * 2 + 1 - core)
     plane = [((section + k) % 4, at) for k in range(1, 4)]
+    beyond = [((section + k) % 4, z * 2 + 1 - core) for k in range(1, 4)]
     line = [(section, ((z + k) % 4) * 2 + core) for k in range(1, 4)]
     barrier = pltpu.get_barrier_semaphore()
-    for partner in [twin] + plane + line:
+    for partner in [twin] + plane + beyond + line:
         pl.semaphore_signal(barrier, inc=1, device_id=partner, device_id_type=MESH)
-    pl.semaphore_wait(barrier, 7)
+    pl.semaphore_wait(barrier, 10)
     copies = []
 
     def send(source, target, number, device):
@@ -567,41 +631,43 @@
     def arrived(target, number):
         pltpu.make_async_copy(target, target, recv_sem.at[number]).wait()
 
-    def over_twin(value, slots, base):
-        slots[core] = value
-        send(slots.at[core], slots.at[core], base, twin)
-        arrived(slots.at[1 - core], base)
-        return slots[0] + slots[1]
-
-    def over_four(value, slots, base, me, partners):
+    def share(value, slots, base, me, partners):
         slots[me] = value
         for partner in partners:
             send(slots.at[me], slots.at[me], base + me, partner)
-        for k in range(1, 4):
-            other = (me + k) % 4
+
+    def collect(slots, base, me):
+        count = slots.shape[0]
+        for k in range(1, count):
+            other = (me + k) % count
             arrived(slots.at[other], base + other)
-        return (slots[0] + slots[1]) + (slots[2] + slots[3])
+        values = [slots[k] for k in range(count)]
+        while len(values) > 1:
+            values = [values[k] + values[k + 1] for k in range(0, len(values), 2)]
+        return values[0]
+
+    place = section * 2 + core
+    neighbours = [twin] + plane + beyond
 
     send(grads_ref.at[pl.ds((1 - core) * 16, 16)], half_in, 0, twin)
-    extra = over_twin(extra_ref[...], extra_twin, 1)
+    share(extra_ref[...], extra_plane, 9, place, neighbours)
     arrived(half_in, 0)
     half[...] = grads_ref[pl.ds(core * 16, 16)] + half_in[...]
-    for k, partner in enumerate(plane):
-        send(half.at[pl.ds(partner[0] * 4, 4)], plane_in.at[section], 2 + section, partner)
-    extra = over_four(extra, extra_plane, 6, section, plane)
+    for partner in plane:
+        send(half.at[pl.ds(partner[0] * 4, 4)], plane_in.at[section], 1 + section, partner)
+    share(collect(extra_plane, 9, place), extra_line, 17, z, line)
     plane_in[section] = half[pl.ds(section * 4, 4)]
     for k in range(1, 4):
         other = (section + k) % 4
-        arrived(plane_in.at[other], 2 + other)
-    quarter = (plane_in[0] + plane_in[1]) + (plane_in[2] + plane_in[3])
-    fourth[...] = quarter
+        arrived(plane_in.at[other], 1 + other)
+    fourth[...] = (plane_in[0] + plane_in[1]) + (plane_in[2] + plane_in[3])
     for k, partner in enumerate(line):
-        send(fourth.at[pl.ds((z + k + 1) % 4, 1)], line_in.at[pl.ds(z, 1)], 10 + z, partner)
-    extra = over_four(extra, extra_line, 14, z, line)
+        send(fourth.at[pl.ds((z + k + 1) % 4, 1)], line_in.at[pl.ds(z, 1)], 5 + z, partner)
     line_in[z] = fourth[z]
+    extra = collect(extra_line, 17, z)
     for k in range(1, 4):
         other = (z + k) % 4
-        arrived(line_in.at[pl.ds(other, 1)], 10 + other)
+        arrived(line_in.at[pl.ds(other, 1)], 5 + other)
     shard = (line_in[0] + line_in[1]) + (line_in[2] + line_in[3])
 
     lane = lax.broadcasted_iota(jnp.int32, (8, 128), 1)
@@ -623,9 +689,9 @@
     values = packed(
         [jnp.sum(shard * shard)] + [jnp.sum(weight * weight) for weight in weights]
     )
-    values = over_twin(values, sums_twin.at[0], 18)
-    values = over_four(values, sums_plane.at[0], 19, section, plane)
-    values = over_four(values, sums_line.at[0], 23, z, line)
+    share(values, sums_plane.at[0], 21, place, neighbours)
+    share(collect(sums_plane.at[0], 21, place), sums_line.at[0], 29, z, line)
+    values = collect(sums_line.at[0], 29, z)
     bias_square = jnp.sum(extra[0:3] * extra[0:3])
     clip_norm = jnp.sqrt(jnp.full((1, 1), unpacked(values, 0) + bias_square, jnp.float32))
     factor = jnp.minimum(1.0, CLIP / clip_norm)
@@ -634,9 +700,9 @@
         update = moments(weights[k], pieces[k] * factor, first_refs[k][...], second_refs[k][...])[2]
         parts.append(jnp.sum(update * update))
     updates = packed(parts)
-    updates = over_twin(updates, sums_twin.at[1], 27)
-    updates = over_four(updates, sums_plane.at[1], 28, section, plane)
-    updates = over_four(updates, sums_line.at[1], 32, z, line)
+    share(updates, sums_plane.at[1], 33, place, neighbours)
+    share(collect(sums_plane.at[1], 33, place), sums_line.at[1], 41, z, line)
+    updates = collect(sums_line.at[1], 41, z)
     out_ref[0:rows, :] = shard
     out_ref[rows : rows + 8, :] = extra
     out_ref[rows + 8 : rows + 16, 0:128] = values
@@ -659,14 +725,12 @@
             pltpu.VMEM((4, rows, hidden), jnp.float32),
             pltpu.VMEM((4, 4, rows, hidden), jnp.float32),
             pltpu.VMEM((4, rows, hidden), jnp.float32),
-            pltpu.VMEM((2, 8, hidden), jnp.float32),
+            pltpu.VMEM((8, 8, hidden), jnp.float32),
             pltpu.VMEM((4, 8, hidden), jnp.float32),
-            pltpu.VMEM((4, 8, hidden), jnp.float32),
-            pltpu.VMEM((2, 2, 8, 128), jnp.float32),
+            pltpu.VMEM((2, 8, 8, 128), jnp.float32),
             pltpu.VMEM((2, 4, 8, 128), jnp.float32),
-            pltpu.VMEM((2, 4, 8, 128), jnp.float32),
-            pltpu.SemaphoreType.DMA((36,)),
-            pltpu.SemaphoreType.DMA((28,)),
+            pltpu.SemaphoreType.DMA((45,)),
+            pltpu.SemaphoreType.DMA((37,)),
         ],
         compiler_params=pltpu.CompilerParams(
             collective_id=1, has_side_effects=True, vmem_limit_bytes=16 * 2**20
@@ -676,19 +740,22 @@
 
 def final_kernel(
     sizes,
+    devices,
     sums_ref,
     weight_refs,
     first_refs,
     second_refs,
     smooth_refs,
-    bias_ref,
-    scalar_ref,
+    bias_refs,
+    loss_ref,
+    count_ref,
+    clip_ref,
     norms_ref,
     new_refs,
     moment_refs,
     square_refs,
     average_refs,
-    bias_out_ref,
+    bias_out_refs,
 ):
     classes, row_inner, row_outer, row_head = sizes
     hidden = sums_ref.shape[1]
@@ -699,7 +766,7 @@
 
     def number(k, start_at):
         found = sums_ref[rows + 8 : rows + 9, start_at : start_at + 128]
-        return jnp.sum(jnp.where(lane == k, found, 0.0), keepdims=True)
+        return jnp.sum(jnp.where(lane == k, found, 0.0), axis=1, keepdims=True)
 
     bias_grad = sums_ref[rows : rows + 3, :]
     bias_square = jnp.sum(jnp.sum(bias_grad * bias_grad, axis=1, keepdims=True), axis=0, keepdims=True)
@@ -721,10 +788,10 @@
         norms = jnp.where(jnp.logical_and(deep == k, wide == 0), weight_norm, norms)
         norms = jnp.where(jnp.logical_and(deep == k, wide == 1), update_norm, norms)
     norms_ref[...] = norms[0:3, 0:2]
-    weight = bias_ref[0:3, :]
-    first, second, update = moments(
-        weight, bias_grad * factor, bias_ref[3:6, :], bias_ref[6:9, :]
-    )
+    weight, first, second, smooth = (
+        jnp.concatenate(bias_rows_of(ref, hidden), axis=0) for ref in bias_refs
+    )
+    first, second, update = moments(weight, bias_grad * factor, first, second)
     column = lax.broadcasted_iota(jnp.int32, weight.shape, 1)
     row = lax.broadcasted_iota(jnp.int32, weight.shape, 0)
     update = jnp.where(jnp.logical_or(row < 2, column < classes), update, 0.0)
@@ -732,31 +799,38 @@
         jnp.sum(update * update, axis=1, keepdims=True)
     )
     fresh = weight - RATE * ratio * update
-    average = AVERAGE * bias_ref[9:12, :] + (1.0 - AVERAGE) * fresh
-    for k, value in enumerate((fresh, first, second, average)):
-        bias_out_ref[4 * k : 4 * k + 3, :] = value
+    average = AVERAGE * smooth + (1.0 - AVERAGE) * fresh
+    for ref, value in zip(bias_out_refs, (fresh, first, second, average)):
+        ref[pl.ds(0, hidden)] = value[0:1].reshape(hidden)
+        ref[pl.ds(hidden, hidden)] = value[1:2].reshape(hidden)
+        ref[pl.ds(2 * hidden, classes)] = value[2:3, 0:classes].reshape(classes)
     tail = sums_ref[rows + 3 : rows + 4, 0:128]
-    scalar_ref[...] = jnp.where(wide == 0, tail, jnp.where(wide == 1, clip_norm, 0.0))
-
-
-def finished(sizes, sums, weights, firsts, seconds, smooths, bias_rows):
-    hidden = sums.shape[1]
+    loss_ref[...] = jnp.sum(jnp.where(lane == 0, tail, 0.0), axis=1, keepdims=True)
+    count = jnp.sum(jnp.where(lane == 1, tail, 0.0), axis=1, keepdims=True)
+    count_ref[...] = count / devices
+    clip_ref[...] = clip_norm
+
+
+def finished(sizes, sums, weights, firsts, seconds, smooths, biases):
     vmem = pl.BlockSpec(memory_space=pltpu.VMEM)
     like = [jax.ShapeDtypeStruct(weight.shape, jnp.float32) for weight in weights]
+    scalar = jax.ShapeDtypeStruct((1, 1), jnp.float32)
     return pl.pallas_call(
-        functools.partial(final_kernel, sizes),
+        functools.partial(final_kernel, sizes, float(lax.axis_size(("section", "dp")))),
         out_shape=(
-            jax.ShapeDtypeStruct((8, 128), jnp.float32),
+            scalar,
+            scalar,
+            scalar,
             jax.ShapeDtypeStruct((3, 2), jnp.float32),
             like,
             like,
             like,
             like,
-            jax.ShapeDtypeStruct((16, hidden), jnp.float32),
+            [jax.ShapeDtypeStruct(biases[0].shape, jnp.float32)] * 4,
         ),
-        in_specs=[vmem] + [(vmem,) * 3] * 4 + [vmem],
-        out_specs=(vmem, vmem, [vmem] * 3, [vmem] * 3, [vmem] * 3, [vmem] * 3, vmem),
-    )(sums, weights, firsts, seconds, smooths, bias_rows)
+        in_specs=[vmem] + [(vmem,) * 3] * 4 + [(vmem,) * 4],
+        out_specs=(vmem,) * 4 + ([vmem] * 3,) * 4 + ([vmem] * 4,),
+    )(sums, weights, firsts, seconds, smooths, biases)
 
 
 def on_slice_kernels(
@@ -768,7 +842,8 @@
         and peers == 8
         and peers * node_table.size * 2 <= VMEM_TABLE_LIMIT
         and node_table.shape[1] == 128
-        and node_table.shape[0] % (64 * CHUNKS) == 0
+        and node_table.shape[0] % (2 * SPARE * CHUNKS) == 0
+        and (node_table.shape[0] // 2 - node_table.shape[0] // 2 // SPARE) % (4 * CHUNKS) == 0
         and peers * node_table.shape[0] <= 131072
         and owner_ids.shape[0] % 1024 == 0
         and owner_ids.shape[0] <= 32768
@@ -890,8 +965,8 @@
     dest_count, fan_inner = inner_neighbours.shape[1:]
     seed_count, fan_outer = outer_neighbours.shape[1:]
     classes = weight_head.shape[1]
+    whole_mask = label_mask
     mask_sizes = label_mask.shape
-    label_part = jnp.sum(label_mask.astype(jnp.float32))
 
     def mine(array):
         return lax.dynamic_index_in_dim(array, at, 0, keepdims=False)
@@ -918,29 +993,14 @@
         mask_sizes,
         [weight.shape[0] for weight in weights],
     ):
-        devices, peers = lax.axis_size(every), lax.axis_size("dp")
         place = (owner_ids * node_table.shape[0] + row_ids).reshape(-1, 128).T
         own = jnp.arange(dest_count, dtype=jnp.int32)[:, None]
-        near = jnp.concatenate([inner_neighbours, own], axis=1).reshape(-1, BLOCK * SLOT)
-        live = jnp.concatenate([keep.astype(jnp.float32), jnp.ones(own.shape, jnp.float32)], axis=1)
-        live = live.reshape(near.shape)
-        tail = jnp.stack([label_part // 256, label_part % 256])
-        tail = jnp.pad(tail[None], ((0, weight_head.shape[0] - 1), (0, hidden - classes - 2)))
-        packed = jnp.concatenate(
-            [weight_inner, weight_outer, jnp.concatenate([weight_head, tail], axis=1)], axis=0
-        ).astype(jnp.bfloat16)
-        table, everyone, idx, mix = spread(node_table, packed, place, near, live)
+        near = jnp.concatenate([jnp.where(keep, inner_neighbours, -1), own], axis=1)
+        near = near.reshape(-1, BLOCK * SLOT)
         firsts = (first_inner, first_outer, first_head)
         seconds = (second_inner, second_outer, second_head)
         smooths = (smooth_inner, smooth_outer, smooth_head)
         rows = [weight.shape[0] for weight in weights]
-
-        def in_rows(*arrays):
-            return jnp.concatenate(
-                [jnp.pad(a, (0, 3 * hidden - a.shape[0])).reshape(3, hidden) for a in arrays]
-            )
-
-        bias_rows = in_rows(biases, first_biases, second_biases, smooth_biases)
         keep_outer = jnp.arange(fan_outer)[None, :] < outer_counts[:, None]
         seed_table = jnp.concatenate(
             [
@@ -951,21 +1011,26 @@
             ],
             axis=1,
         )
-        joined_one = picked(idx, mix, table)
+        joined_one, everyone, hits, hits_back = gathered(
+            classes, fan_outer, node_table, weights, whole_mask, place, near, seed_table
+        )
         grads, extra = dense(
-            (classes, fan_outer, *rows), joined_one, everyone, bias_rows, seed_table
+            (classes, fan_outer, *rows), joined_one, everyone, hits, hits_back, biases, seed_table
         )
         sums = reduced((classes, *rows), grads, extra, weights, firsts, seconds)
-        scalars, norms, news, moment, square, average, bias_out = finished(
-            (classes, *rows), sums, weights, firsts, seconds, smooths, bias_rows
+        loss, count, clip, norms, news, moment, square, average, bias_outs = finished(
+            (classes, *rows),
+            sums,
+            weights,
+            firsts,
+            seconds,
+            smooths,
+            (biases, first_biases, second_biases, smooth_biases),
         )
-        bias_outs = [
-            bias_out[4 * k : 4 * k + 3].reshape(-1)[: biases.shape[0]] for k in range(4)
-        ]
         return (
-            scalars[0, 0],
-            extra[3, 1],
-            scalars[1, 1],
+            loss.reshape(()),
+            count.reshape(()),
+            clip.reshape(()),
             norms,
             *news,
             bias_outs[0],
@@ -977,6 +1042,7 @@
             bias_outs[3],
         )
 
+    label_part = jnp.sum(whole_mask.astype(jnp.float32))
     label_count = jnp.maximum(lax.psum(label_part, "dp"), 1.0)
     full_inner, full_outer, full_head = (
         lax.all_gather(weight.astype(jnp.bfloat16), every, axis=0, tiled=True)

time: 253 us -> 218 us (0.86)
  local copies, waits for them, and re-layouts: 36.3 us -> 10.6 us
  Pallas kernels: 208 us -> 204 us
  other arithmetic: 5.38 us -> 2.14 us
    unnamed x45 -> x33, local copies, waits for them, and re-layouts: 26 us -> 6.08 us
    pallas_call x1, Pallas kernels: 14.1 us -> 9.65 us  [dense(): pl.pallas_call(functools.partial(dense_kernel, sizes), out_shape=(jax.Sha...]
    reshape x10 -> x1, local copies, waits for them, and re-layouts: 3.65 us -> 0.61 us  [on_device(): near = near.reshape(-1, BLOCK * SLOT)]
    slice x3 -> x0, local copies, waits for them, and re-layouts: 2.7 us -> none  [the longest x1 1.34 us: on_device(): scalars[1, 1]]
    pallas_call x3 -> x2, Pallas kernels: 161 us -> 162 us  [the longest x1 160 us: gathered(): pl.pallas_call(functools.partial(gather_kernel, classes, fan_outer), out_...]
where the time goes in v4:
time: 218 us
  Pallas kernels  204 us (94%)
  local copies, waits for them, and re-layouts  10.6 us (5%)
    pallas_call x1, Pallas kernels, gathered(): pl.pallas_call(functools.partial(gather_kernel, classes, fan_outer), out_...  160 us
    pallas_call x1, Pallas kernels, reduced(): pl.pallas_call(functools.partial(reduce_kernel, sizes), out_shape=jax.Sha...  32.6 us
    pallas_call x1, Pallas kernels, dense(): pl.pallas_call(functools.partial(dense_kernel, sizes), out_shape=(jax.Sha...  9.65 us
    unnamed x33, local copies, waits for them, and re-layouts  6.08 us

profile of v4, /device:TPU:0, one launch (start us, length us, event | category | flops | bytes accessed | tf_op | source)
XLA Modules:
  0.0 217.8 jit_solution(7325692335589694369)
XLA Ops:
  0.7 0.0 copy-start
  0.7 0.1 pad.3.clone
  0.8 0.7 fusion.3
  1.5 0.7 constant_dynamic-slice_fusion.3
  2.2 0.8 constant_dynamic-slice_fusion.2
  3.0 0.8 dynamic-slice_reduce_fusion
  3.9 0.1 fusion.4.seed_across_ref
  3.9 0.1 add_add_fusion
  4.0 0.1 copy.76.seed_ref
  4.1 1.0 broadcast_multiply_fusion
  5.1 0.9 add.16
  6.1 0.1 copy.72
  6.2 0.2 constant_dynamic-slice_fusion.4
  6.4 0.0 copy-start.5
  6.4 0.0 copy-start.6
  6.4 0.0 copy-start.7
  6.4 0.0 copy-start.15
  6.4 0.4 copy.74
  6.9 0.6 reshape.72.near_ref
  7.5 0.0 copy-done.6
  7.5 0.0 copy-start.14
  7.5 160.1 %shard_map.392 = (bf16[2816,256]{1,0:T(8,128)(2,1)}, bf16[32,32,256]{2,1,0:T(8,128)(2,1)S(1)}, bf16[256,2816]{1,0:T(8,128)(2,1)}, bf16[2816,256]{1,0:T(8,128)(2,1)}) custom-call(bf16[8192,2,128]{2,1,0:T(2,128)(2,1)} %bitcast.23, f32[8,256]{1,0:T(8,128)S(1)} %copy-done.6, f32[16,256]{1,0:T(8,128)S(1)} %copy-done.5, f32[8,172]{1,0:T(8,128)S(1)} %copy-done.7, ...), custom_call_target="tpu_custom_call" | custom-call | tf_op jit(solution)/shard_map/pallas_call | solution.py:387
  167.6 1.4 copy-done.1
  169.0 1.4 copy-done.2
  170.4 1.4 copy-done.3
  171.7 0.0 copy-start.12
  171.7 0.0 copy-start.13
  171.8 9.6 %shard_map.393 = (f32[32,32,256]{2,1,0:T(8,128)S(1)}, f32[8,256]{1,0:T(8,128)S(1)}) custom-call(bf16[2816,256]{1,0:T(8,128)(2,1)S(1)} %copy-done.1, bf16[32,32,256]{2,1,0:T(8,128)(2,1)S(1)} %get-tuple-element.47.everyone_ref, bf16[256,2816]{1,0:T(8,128)(2,1)S(1)} %copy-done.2, bf16[2816,256]{1,0:T(8,128)(2,1)S(1)} %copy-done.3, f32[684]{0:T(1024)S(1)} %copy-done.14, ...), custom_call_target="tpu_custom_call" | custom-call | tf_op jit(solution)/shard_map/pallas_call | solution.py:568
  181.5 32.6 %shard_map.394.sums_ref = f32[48,256]{1,0:T(8,128)S(1)} custom-call(f32[32,32,256]{2,1,0:T(8,128)S(1)} %get-tuple-element.50.grads_ref, f32[8,256]{1,0:T(8,128)S(1)} %get-tuple-element.51.extra_ref, f32[8,256]{1,0:T(8,128)S(1)} %copy-done.6, f32[16,256]{1,0:T(8,128)S(1)} %copy-done.5, f32[8,172]{1,0:T(8,128)S(1)} %copy-done.7, f32[8,256]{1,0:T(8,128)S(1)} %copy-done.10, ...), custom_call_target="tpu_custom_call" | custom-call | tf_op jit(solution)/shard_map/pallas_call | solution.py:717
  214.0 0.6 copy-done.4
  214.7 1.8 shard_map.395
  216.5 1.3 copy.78
  (24 shorter events, 0.1 us)
Async XLA Ops:
  0.7 5.5 %copy-start = (s32[4,2816,15]{1,0,2:T(4,128)S(1)}, s32[4,2816,15]{1,0,2:T(4,128)}, u32[]{:S(2)}) copy-start(s32[4,2816,15]{1,0,2:T(4,128)} %param.28) | copy-start | bytes 2027524
  6.4 1.1 copy-start.5
  6.4 1.1 copy-start.6
  6.4 1.1 copy-start.7
  6.4 1.1 copy-start.15
  7.5 160.1 %copy-start.14 = (f32[684]{0:T(1024)S(1)}, f32[684]{0:T(1024)}, u32[]{:S(2)}) copy-start(f32[684]{0:T(1024)} %bias_refs_0_.1) | copy-start | bytes 8212
  167.6 1.4 copy-start.1
  169.0 1.4 copy-start.2
  170.4 1.4 copy-start.3
  171.7 9.7 %copy-start.8 = (f32[16,256]{1,0:T(8,128)S(1)}, f32[16,256]{1,0:T(8,128)}, u32[]{:S(2)}) copy-start(f32[16,256]{1,0:T(8,128)} %first_refs_1_.3) | copy-start | bytes 49156
  171.7 9.7 %copy-start.9 = (f32[16,256]{1,0:T(8,128)S(1)}, f32[16,256]{1,0:T(8,128)}, u32[]{:S(2)}) copy-start(f32[16,256]{1,0:T(8,128)} %second_refs_1_.3) | copy-start | bytes 49156
  171.7 9.7 %copy-start.10 = (f32[8,256]{1,0:T(8,128)S(1)}, f32[8,256]{1,0:T(8,128)}, u32[]{:S(2)}) copy-start(f32[8,256]{1,0:T(8,128)} %first_refs_0_.3) | copy-start | bytes 24580
  171.7 9.7 %copy-start.11 = (f32[8,172]{1,0:T(8,128)S(1)}, f32[8,172]{1,0:T(8,128)}, u32[]{:S(2)}) copy-start(f32[8,172]{1,0:T(8,128)} %first_refs_2_.3) | copy-start | bytes 16516
  171.7 9.7 %copy-start.12 = (f32[8,256]{1,0:T(8,128)S(1)}, f32[8,256]{1,0:T(8,128)}, u32[]{:S(2)}) copy-start(f32[8,256]{1,0:T(8,128)} %second_refs_0_.3) | copy-start | bytes 24580
  171.7 9.7 %copy-start.13 = (f32[8,172]{1,0:T(8,128)S(1)}, f32[8,172]{1,0:T(8,128)}, u32[]{:S(2)}) copy-start(f32[8,172]{1,0:T(8,128)} %second_refs_2_.3) | copy-start | bytes 16516
  214.0 0.6 copy-start.4

commit v5 on v4

--- a/solution.py
+++ b/solution.py
@@ -28,20 +28,35 @@
 GROUP = 4
 SETS = 4
 SPARE = 8
-SPARE_EARLY = False
+AHEAD = 2
+AHEAD_ACROSS = 1
+LAG = 1
+FAR_LAG = 2
+SPARE_AFTER = 2
+SPARE_LAG = 3
 TILE = 256
-
-
-def gather_kernel(
-    classes,
+PAUSE = 6
+
+
+class Parts:
+    def __init__(self, refs, base):
+        self.grads, self.half_in, self.half, self.plane_in, self.fourth, self.line_in = refs
+        self.base = base
+
+
+def step_kernel(
     fan_outer,
     table_ref,
     weight_refs,
+    first_refs,
+    second_refs,
+    bias_ref,
     mask_ref,
     place_ref,
     near_ref,
     seed_ref,
     seed_across_ref,
+    out_ref,
     joined_ref,
     weights_ref,
     hits_ref,
@@ -54,6 +69,17 @@
     wide,
     stages,
     lists,
+    first_pre,
+    first_hidden,
+    own_part,
+    inner_sum,
+    early_refs,
+    late_refs,
+    extra_ref,
+    extra_plane,
+    extra_line,
+    sums_plane,
+    sums_line,
     own_sem,
     z_sem,
     spare_sem,
@@ -66,6 +92,8 @@
     send_sem,
     double_send_sem,
     list_sem,
+    sum_sem,
+    sum_send_sem,
 ):
     section, at = lax.axis_index("section"), lax.axis_index("dp")
     z, core = at // 2, at % 2
@@ -89,16 +117,15 @@
     skip_z = (section, ((z + 2) % 4) * 2 + core)
     sources = [level(1 - height), level(2), level(3)]
     crosses = height == 1
+    plane = [((section + k) % 4, at) for k in range(1, 4)]
+    beyond = [((section + k) % 4, z * 2 + 1 - core) for k in range(1, 4)]
+    line = [(section, ((z + k) % 4) * 2 + core) for k in range(1, 4)]
+    neighbours = [twin] + plane + beyond
 
     barrier = pltpu.get_barrier_semaphore()
-    for partner in (twin, beside_x, beside_y, inner_z, skip_z):
+    for partner in neighbours + line:
         pl.semaphore_signal(barrier, inc=1, device_id=partner, device_id_type=MESH)
-
-    @pl.when(crosses)
-    def greet_across():
-        pl.semaphore_signal(barrier, inc=1, device_id=across_z, device_id_type=MESH)
-
-    pl.semaphore_wait(barrier, 5 + height)
+    pl.semaphore_wait(barrier, 10)
 
     sent = []
 
@@ -128,16 +155,14 @@
     def arrived(target, recv):
         pltpu.make_async_copy(target, target, recv).wait()
 
-    for piece in range(CHUNKS):
+    def own_piece(piece, device, number, when=None):
         block = table_ref.at[pl.ds(section * quarter + piece * chunk, chunk)]
-        goal = region(at, section, piece)
-        send(block, goal, z_sem.at[piece], inner_z)
-        send(block, goal, z_sem.at[CHUNKS + piece], across_z, crosses)
-        if SPARE_EARLY:
-            block = table_ref.at[pl.ds(4 * quarter + piece * spare_chunk, spare_chunk)]
-            goal = spare_region(at, piece)
-            send(block, goal, spare_sem.at[piece], inner_z)
-            send(block, goal, spare_sem.at[CHUNKS + piece], across_z, crosses)
+        send(block, region(at, section, piece), z_sem.at[number], device, when)
+
+    for piece in range(min(AHEAD, CHUNKS)):
+        own_piece(piece, inner_z, piece)
+    for piece in range(min(AHEAD_ACROSS, CHUNKS)):
+        own_piece(piece, across_z, CHUNKS + piece, crosses)
     whole = full_ref.at[pl.ds(at * pairs, pairs)]
     own = pltpu.make_async_copy(table_ref, whole, own_sem)
     own.start()
@@ -145,7 +170,7 @@
 
     inner_ref, outer_ref, head_ref = weight_refs
     row_inner, row_outer, row_head = (ref.shape[0] for ref in weight_refs)
-    hidden = inner_ref.shape[1]
+    hidden, classes = inner_ref.shape[1], head_ref.shape[1]
     head_at = row_inner + row_outer
     packed[0:row_inner, :] = inner_ref[...]
     packed[row_inner:head_at, :] = outer_ref[...]
@@ -188,7 +213,7 @@
     seeds = seed_ref.shape[0]
     tiles = hits_ref.shape[1] // TILE
     total = 3 * CHUNKS
-    steps = total + 2
+    steps = total + max(FAR_LAG, SPARE_LAG)
     per_step = -(-looked_rows // (8 * steps)) * 8
     for j in range(fan_outer):
         wide[j] = jnp.broadcast_to(seed_ref[:, j : j + 1], (seeds, TILE))
@@ -257,12 +282,18 @@
             send(block, block, x_sem.at[step], beside_x)
             send(block, block, y_sem.at[step], beside_y)
             to_twin(block, step)
-            if not SPARE_EARLY and turn == 0:
+            if step + AHEAD < CHUNKS:
+                own_piece(step + AHEAD, inner_z, step + AHEAD)
+            if step + AHEAD_ACROSS < CHUNKS:
+                piece = step + AHEAD_ACROSS
+                own_piece(piece, across_z, CHUNKS + piece, crosses)
+            piece = step - SPARE_AFTER
+            if 0 <= piece < CHUNKS:
                 block = table_ref.at[pl.ds(4 * quarter + piece * spare_chunk, spare_chunk)]
                 goal = spare_region(at, piece)
                 send(block, goal, spare_sem.at[piece], inner_z)
                 send(block, goal, spare_sem.at[CHUNKS + piece], across_z, crosses)
-        late = step - 1
+        late = step - SPARE_LAG
         if 0 <= late < total:
             turn, piece = divmod(late, CHUNKS)
             shard = sources[turn] * 2 + core
@@ -271,17 +302,19 @@
             arrived(block, spare_sem.at[late])
             send(block, block, spare_sem.at[number], goes, crosses)
             to_twin(block, 4 * total + late)
+        late = step - LAG
+        if 0 <= late < total:
+            turn, piece = divmod(late, CHUNKS)
+            shard = sources[turn] * 2 + core
             block = region(shard, beside_x[0], piece)
             arrived(block, x_sem.at[late])
-            if piece % 2 == 0:
-                send(block, block, far_sem.at[late], beside_y)
+            send(block, block, far_sem.at[late], beside_y, core == piece % 2)
             to_twin(block, total + late)
             block = region(shard, beside_y[0], piece)
             arrived(block, y_sem.at[late])
-            if piece % 2 == 1:
-                send(block, block, far_sem.at[late], beside_x)
+            send(block, block, far_sem.at[late], beside_x, core != piece % 2)
             to_twin(block, 2 * total + late)
-        later = step - 2
+        later = step - FAR_LAG
         if 0 <= later < total:
             turn, piece = divmod(later, CHUNKS)
             shard = sources[turn] * 2 + core
@@ -370,8 +403,227 @@
         else:
             pl.when(when)(copy.wait_send)
 
-
-def gathered(classes, fan_outer, node_table, weights, label_mask, place, near, seed_table):
+    summing = []
+
+    def pass_on(source, target, number, device):
+        copy = pltpu.make_async_remote_copy(
+            src_ref=source,
+            dst_ref=target,
+            send_sem=sum_send_sem.at[len(summing)],
+            recv_sem=sum_sem.at[number],
+            device_id=device,
+            device_id_type=MESH,
+        )
+        summing.append(copy)
+        copy.start()
+
+    def passed(target, number):
+        arrived(target, sum_sem.at[number])
+
+    def to_other_core(part):
+        pass_on(part.grads.at[pl.ds((1 - core) * 16, 16)], part.half_in, part.base, twin)
+
+    def to_plane(part):
+        passed(part.half_in, part.base)
+        part.half[...] = part.grads[pl.ds(core * 16, 16)] + part.half_in[...]
+        for partner in plane:
+            block = part.half.at[pl.ds(partner[0] * 4, 4)]
+            pass_on(block, part.plane_in.at[section], part.base + 1 + section, partner)
+        part.plane_in[section] = part.half[pl.ds(section * 4, 4)]
+
+    def to_line(part):
+        for k in range(1, 4):
+            other = (section + k) % 4
+            passed(part.plane_in.at[other], part.base + 1 + other)
+        part.fourth[...] = (part.plane_in[0] + part.plane_in[1]) + (
+            part.plane_in[2] + part.plane_in[3]
+        )
+        for k, partner in enumerate(line):
+            block = part.fourth.at[pl.ds((z + k + 1) % 4, 1)]
+            pass_on(block, part.line_in.at[pl.ds(z, 1)], part.base + 5 + z, partner)
+        part.line_in[z] = part.fourth[z]
+
+    def whole_sum(part):
+        for k in range(1, 4):
+            other = (z + k) % 4
+            passed(part.line_in.at[pl.ds(other, 1)], part.base + 5 + other)
+        return (part.line_in[0] + part.line_in[1]) + (part.line_in[2] + part.line_in[3])
+
+    def share(value, slots, base, me, partners):
+        slots[me] = value
+        for partner in partners:
+            pass_on(slots.at[me], slots.at[me], base + me, partner)
+
+    def collect(slots, base, me):
+        count = slots.shape[0]
+        for k in range(1, count):
+            other = (me + k) % count
+            passed(slots.at[other], base + other)
+        values = [slots[k] for k in range(count)]
+        while len(values) > 1:
+            values = [values[k] + values[k + 1] for k in range(0, len(values), 2)]
+        return values[0]
+
+    early, late_part = Parts(early_refs, 0), Parts(late_refs, 9)
+    dest_count = joined_ref.shape[0]
+    order = block_order()
+    weights = weights_ref[...].astype(jnp.float32)
+    split = (0, row_inner, head_at, head_at + row_head)
+    full_inner, full_outer, full_head = (
+        jnp.concatenate([weights[spot, split[k] : split[k + 1]] for spot in order], axis=0)
+        for k in range(3)
+    )
+    lane = lax.broadcasted_iota(jnp.int32, (1, hidden), 1)
+    tails = weights[0:4, head_at : head_at + 1] + weights[16:20, head_at : head_at + 1]
+    tails = jnp.sum(tails.reshape(4, hidden), axis=0, keepdims=True)
+    scale = jnp.where(lane == classes, 256.0, jnp.where(lane == classes + 1, 1.0, 0.0))
+    label_count = jnp.maximum(jnp.sum(tails * scale), 1.0)
+    full_inner = full_inner.astype(jnp.bfloat16)
+    full_outer = full_outer.astype(jnp.bfloat16)
+    full_head = jnp.where(lane < classes, full_head, 0.0).astype(jnp.bfloat16)
+    bias_inner, bias_outer, bias_head = bias_rows_of(bias_ref, hidden)
+    kept = seed_ref[:, 0:fan_outer]
+    count_two = jnp.sum((kept >= 0).astype(jnp.float32), axis=1, keepdims=True)
+
+    def forward(tile, carry):
+        tile_rows = pl.ds(pl.multiple_of(tile * TILE, TILE), TILE)
+        before = (
+            jnp.dot(joined_ref[tile_rows, :], full_inner, preferred_element_type=jnp.float32)
+            + bias_inner
+        )
+        first_pre[tile_rows, :] = before
+        first_hidden[tile_rows, :] = (before * lax.logistic(before)).astype(jnp.bfloat16)
+        return carry
+
+    lax.fori_loop(0, tiles, forward, 0)
+    mean_sum = jnp.dot(hits_ref[...], first_hidden[...], preferred_element_type=jnp.float32)
+    mean_two = (mean_sum / count_two).astype(jnp.bfloat16)
+    joined_two = jnp.concatenate([first_hidden[0:seeds, :], mean_two], axis=1)
+    pre_two = jnp.dot(joined_two, full_outer, preferred_element_type=jnp.float32) + bias_outer
+    gate_two = lax.logistic(pre_two)
+    hidden_two = (pre_two * gate_two).astype(jnp.bfloat16)
+    logits = jnp.dot(hidden_two, full_head, preferred_element_type=jnp.float32) + bias_head
+    inside = lane < classes
+    highest = jnp.max(jnp.where(inside, logits, -jnp.inf), axis=1, keepdims=True)
+    shifted = jnp.where(inside, logits - highest, 0.0)
+    total_exp = jnp.sum(jnp.where(inside, jnp.exp(shifted), 0.0), axis=1, keepdims=True)
+    log_total = jnp.log(total_exp)
+    chosen = (lane == seed_ref[:, fan_outer : fan_outer + 1]).astype(jnp.float32)
+    row_weight = seed_ref[:, fan_outer + 1 : fan_outer + 2].astype(jnp.float32)
+    loss = jnp.sum((log_total - jnp.sum(shifted * chosen, axis=1, keepdims=True)) * row_weight)
+    grad_logits = (jnp.exp(shifted - log_total) - chosen) * (row_weight / label_count)
+    grad_logits = jnp.where(inside, grad_logits, 0.0).astype(jnp.bfloat16)
+    grad_head = outer_product(hidden_two, grad_logits)
+    grad_two = against(grad_logits, full_head).astype(jnp.bfloat16).astype(jnp.float32)
+    grad_pre_two = (grad_two * gate_two * (1.0 + pre_two * (1.0 - gate_two))).astype(jnp.bfloat16)
+    grad_outer = outer_product(joined_two, grad_pre_two)
+    for number, spot in enumerate(order):
+        early.grads[spot, 0:row_outer, :] = grad_outer[
+            number * row_outer : (number + 1) * row_outer
+        ]
+        early.grads[spot, row_outer : row_outer + row_head, :] = grad_head[
+            number * row_head : (number + 1) * row_head
+        ]
+    to_other_core(early)
+    extra_ref[1:2, :] = jnp.sum(grad_pre_two.astype(jnp.float32), axis=0, keepdims=True)
+    extra_ref[2:3, :] = jnp.sum(grad_logits.astype(jnp.float32), axis=0, keepdims=True)
+    extra_ref[3:4, :] = jnp.where(lane == 0, loss, jnp.where(lane == 1, label_count, 0.0))
+    extra_ref[4:8, :] = jnp.zeros((4, hidden), jnp.float32)
+    grad_joined = against(grad_pre_two, full_outer)
+    share_part = grad_joined[:, hidden:] / count_two
+    share_high = share_part.astype(jnp.bfloat16)
+    share_low = (share_part - share_high.astype(jnp.float32)).astype(jnp.bfloat16)
+    inner_sum[...] = jnp.zeros(inner_sum.shape, jnp.float32)
+    share_both = jnp.concatenate([share_high, share_low], axis=0)
+    own_part[...] = jnp.zeros(own_part.shape, jnp.float32)
+    own_part[0:seeds, :] = grad_joined[:, 0:hidden]
+
+    def backward(tile, bias_sum, own=None):
+        tile_rows = pl.ds(pl.multiple_of(jnp.int32(tile) * TILE, TILE), TILE)
+        hits = hits_back_ref[tile_rows, :]
+        both_hits = jnp.concatenate([hits, hits], axis=1)
+        grad_one = jnp.dot(both_hits, share_both, preferred_element_type=jnp.float32)
+        if own is not None:
+            grad_one = grad_one + own
+        grad_one = grad_one.astype(jnp.bfloat16).astype(jnp.float32)
+        before = first_pre[tile_rows, :]
+        gate = lax.logistic(before)
+        grad_pre = (grad_one * gate * (1.0 + before * (1.0 - gate))).astype(jnp.bfloat16)
+        inner_sum[...] += outer_product(joined_ref[tile_rows, :], grad_pre)
+        return bias_sum + jnp.sum(grad_pre.astype(jnp.float32), axis=0, keepdims=True)
+
+    bias_sum = backward(0, jnp.zeros((1, hidden), jnp.float32), own_part[...])
+    bias_sum = lax.fori_loop(1, PAUSE, backward, bias_sum)
+    to_plane(early)
+    bias_sum = lax.fori_loop(PAUSE, tiles, backward, bias_sum)
+    extra_ref[0:1, :] = bias_sum
+    grad_inner = inner_sum[...]
+    for number, spot in enumerate(order):
+        late_part.grads[spot] = grad_inner[number * row_inner : (number + 1) * row_inner]
+    to_other_core(late_part)
+    share(extra_ref[...], extra_plane, 18, section * 2 + core, neighbours)
+    to_plane(late_part)
+    to_line(early)
+    share(collect(extra_plane, 18, section * 2 + core), extra_line, 26, z, line)
+    to_line(late_part)
+
+    deep_lane = lax.broadcasted_iota(jnp.int32, (8, 128), 1)
+
+    def packed_up(values):
+        found = jnp.zeros((8, 128), jnp.float32)
+        for k, value in enumerate(values):
+            found = jnp.where(deep_lane == k, value, found)
+        return found
+
+    def everywhere(values, number):
+        base = 30 + 12 * number
+        place_in = section * 2 + core
+        share(packed_up(values), sums_plane.at[number], base, place_in, neighbours)
+        plane_sum = collect(sums_plane.at[number], base, place_in)
+        share(plane_sum, sums_line.at[number], base + 8, z, line)
+        return collect(sums_line.at[number], base + 8, z)
+
+    held = [ref[...] for ref in weight_refs]
+    weight_squares = [jnp.sum(weight * weight) for weight in held]
+    rest = whole_sum(early)
+    shard = whole_sum(late_part)
+    extra = collect(extra_line, 26, z)
+    pieces = [shard, rest[0:row_outer], rest[row_outer:, 0:classes]]
+    values = everywhere([jnp.sum(shard * shard) + jnp.sum(rest * rest)] + weight_squares, 0)
+    grad_square = jnp.sum(jnp.where(deep_lane[0:1] == 0, values[0:1], 0.0))
+    bias_square = jnp.sum(extra[0:3] * extra[0:3])
+    clip_norm = jnp.sqrt(jnp.full((1, 1), grad_square + bias_square, jnp.float32))
+    factor = jnp.minimum(1.0, CLIP / clip_norm)
+    update_squares = []
+    for k in range(3):
+        update = moments(held[k], pieces[k] * factor, first_refs[k][...], second_refs[k][...])[2]
+        update_squares.append(jnp.sum(update * update))
+    updates = everywhere(update_squares, 1)
+    rows = row_inner + row_outer + row_head
+    out_ref[0:row_inner, :] = shard
+    out_ref[row_inner:rows, :] = rest
+    out_ref[rows : rows + 8, :] = extra
+    out_ref[rows + 8 : rows + 16, 0:128] = values
+    out_ref[rows + 8 : rows + 16, 128:256] = updates
+    for copy in summing:
+        copy.wait_send()
+
+
+def block_order():
+    return [(e % 2) * 16 + (e // 8) * 4 + (e % 8) // 2 for e in range(32)]
+
+
+def bias_rows_of(ref, hidden):
+    width = ref.shape[0] - 2 * hidden
+    last = ref[pl.ds(2 * hidden, width)].reshape(1, width)
+    return (
+        ref[pl.ds(0, hidden)].reshape(1, hidden),
+        ref[pl.ds(hidden, hidden)].reshape(1, hidden),
+        jnp.concatenate([last, jnp.zeros((1, hidden - width), jnp.float32)], axis=1),
+    )
+
+
+def summed_step(fan_outer, node_table, weights, firsts, seconds, biases, label_mask, place, near, seed_table):
     devices = lax.axis_size(("section", "dp"))
     table_rows, width = node_table.shape
     frontier_high = place.shape[1]
@@ -379,22 +631,33 @@
     dest_count = looked * BLOCK
     seeds = seed_table.shape[0]
     hidden = weights[0].shape[1]
+    row_inner = weights[0].shape[0]
     rows = sum(weight.shape[0] for weight in weights)
     total = 3 * CHUNKS
-    sends = 4 * CHUNKS + 1 + 3 * total + total + total + 5 * total
+    sends = 4 * CHUNKS + 1 + 3 * total + total + 2 * total + 5 * total
     vmem = pl.BlockSpec(memory_space=pltpu.VMEM)
     stage = (pltpu.VMEM((2 * BLOCK * SLOT, width), jnp.float32),) * GROUP
+
+    def on_the_way(depth):
+        return (
+            pltpu.VMEM((devices, depth, hidden), jnp.float32),
+            pltpu.VMEM((16, depth, hidden), jnp.float32),
+            pltpu.VMEM((16, depth, hidden), jnp.float32),
+            pltpu.VMEM((4, 4, depth, hidden), jnp.float32),
+            pltpu.VMEM((4, depth, hidden), jnp.float32),
+            pltpu.VMEM((4, depth, hidden), jnp.float32),
+        )
+
     return pl.pallas_call(
-        functools.partial(gather_kernel, classes, fan_outer),
-        out_shape=(
-            jax.ShapeDtypeStruct((dest_count, 2 * width), jnp.bfloat16),
-            jax.ShapeDtypeStruct((devices, rows, hidden), jnp.bfloat16),
-            jax.ShapeDtypeStruct((seeds, dest_count), jnp.bfloat16),
-            jax.ShapeDtypeStruct((dest_count, seeds), jnp.bfloat16),
-        ),
-        in_specs=[pl.BlockSpec(memory_space=pl.ANY), (vmem,) * 3] + [vmem] * 5,
-        out_specs=(vmem,) * 4,
+        functools.partial(step_kernel, fan_outer),
+        out_shape=jax.ShapeDtypeStruct((rows + 16, hidden), jnp.float32),
+        in_specs=[pl.BlockSpec(memory_space=pl.ANY)] + [(vmem,) * 3] * 3 + [vmem] * 6,
+        out_specs=vmem,
         scratch_shapes=[
+            pltpu.VMEM((dest_count, 2 * width), jnp.bfloat16),
+            pltpu.VMEM((devices, rows, hidden), jnp.bfloat16),
+            pltpu.VMEM((seeds, dest_count), jnp.bfloat16),
+            pltpu.VMEM((dest_count, seeds), jnp.bfloat16),
             pltpu.VMEM((lax.axis_size("dp") * table_rows // 2, 2, width), jnp.bfloat16),
             pltpu.VMEM((rows, hidden), jnp.float32),
             pltpu.VMEM((384, frontier_high), jnp.bfloat16),
@@ -403,6 +666,17 @@
             pltpu.VMEM((fan_outer, seeds, TILE), jnp.int32),
             (stage, stage),
             (pltpu.SMEM((GROUP, BLOCK * SLOT), jnp.int32),) * SETS,
+            pltpu.VMEM((dest_count, hidden), jnp.float32),
+            pltpu.VMEM((dest_count, hidden), jnp.bfloat16),
+            pltpu.VMEM((TILE, hidden), jnp.float32),
+            pltpu.VMEM((hidden, hidden), jnp.float32),
+            on_the_way(rows - row_inner),
+            on_the_way(row_inner),
+            pltpu.VMEM((8, hidden), jnp.float32),
+            pltpu.VMEM((8, 8, hidden), jnp.float32),
+            pltpu.VMEM((4, 8, hidden), jnp.float32),
+            pltpu.VMEM((2, 8, 8, 128), jnp.float32),
+            pltpu.VMEM((2, 4, 8, 128), jnp.float32),
             pltpu.SemaphoreType.DMA(()),
             pltpu.SemaphoreType.DMA((total,)),
             pltpu.SemaphoreType.DMA((total,)),
@@ -415,327 +689,26 @@
             pltpu.SemaphoreType.DMA((sends,)),
             pltpu.SemaphoreType.DMA((5,)),
             pltpu.SemaphoreType.DMA((SETS,)),
+            pltpu.SemaphoreType.DMA((54,)),
+            pltpu.SemaphoreType.DMA((44,)),
         ],
         compiler_params=pltpu.CompilerParams(
-            collective_id=0, has_side_effects=True, vmem_limit_bytes=52 * 2**20
+            collective_id=0, has_side_effects=True, vmem_limit_bytes=56 * 2**20
         ),
     )(
         pltpu.with_memory_space_constraint(
             node_table.reshape(table_rows // 2, 2, width), pltpu.HBM
         ),
         weights,
+        firsts,
+        seconds,
+        biases,
         label_mask,
         place,
         near,
         seed_table,
         seed_table.T,
     )
-
-
-def block_order():
-    return [(e % 2) * 16 + (e // 8) * 4 + (e % 8) // 2 for e in range(32)]
-
-
-def dense_kernel(
-    sizes,
-    joined_ref,
-    everyone_ref,
-    hits_ref,
-    hits_back_ref,
-    bias_ref,
-    seed_ref,
-    grads_ref,
-    extra_ref,
-    first_pre,
-    first_hidden,
-    own_part,
-    inner_sum,
-):
-    classes, fan_outer, row_inner, row_outer, row_head = sizes
-    dest_count, hidden = joined_ref.shape
-    tiles = dest_count // TILE
-    order = block_order()
-    weights = everyone_ref[...].astype(jnp.float32)
-    split = (0, row_inner, row_inner + row_outer, row_inner + row_outer + row_head)
-    full_inner, full_outer, full_head = (
-        jnp.concatenate([weights[place, split[k] : split[k + 1]] for place in order], axis=0)
-        for k in range(3)
-    )
-    lane = lax.broadcasted_iota(jnp.int32, (1, hidden), 1)
-    tails = weights[0:4, split[2] : split[2] + 1] + weights[16:20, split[2] : split[2] + 1]
-    tails = jnp.sum(tails.reshape(4, hidden), axis=0, keepdims=True)
-    scale = jnp.where(lane == classes, 256.0, jnp.where(lane == classes + 1, 1.0, 0.0))
-    label_count = jnp.maximum(jnp.sum(tails * scale), 1.0)
-    full_inner = full_inner.astype(jnp.bfloat16)
-    full_outer = full_outer.astype(jnp.bfloat16)
-    full_head = jnp.where(lane < classes, full_head, 0.0).astype(jnp.bfloat16)
-    bias_inner, bias_outer, bias_head = bias_rows_of(bias_ref, hidden)
-    seeds = seed_ref.shape[0]
-    kept = seed_ref[:, 0:fan_outer]
-    count_two = jnp.sum((kept >= 0).astype(jnp.float32), axis=1, keepdims=True)
-
-    def forward(tile, carry):
-        start_at = pl.multiple_of(tile * TILE, TILE)
-        rows = pl.ds(start_at, TILE)
-        before = (
-            jnp.dot(joined_ref[rows, :], full_inner, preferred_element_type=jnp.float32) + bias_inner
-        )
-        first_pre[rows, :] = before
-        out = (before * lax.logistic(before)).astype(jnp.bfloat16)
-        first_hidden[rows, :] = out
-        return carry
-
-    lax.fori_loop(0, tiles, forward, 0)
-    mean_sum = jnp.dot(hits_ref[...], first_hidden[...], preferred_element_type=jnp.float32)
-    mean_two = (mean_sum / count_two).astype(jnp.bfloat16)
-    joined_two = jnp.concatenate([first_hidden[0:seeds, :], mean_two], axis=1)
-    pre_two = jnp.dot(joined_two, full_outer, preferred_element_type=jnp.float32) + bias_outer
-    gate_two = lax.logistic(pre_two)
-    hidden_two = (pre_two * gate_two).astype(jnp.bfloat16)
-    logits = jnp.dot(hidden_two, full_head, preferred_element_type=jnp.float32) + bias_head
-    inside = lane < classes
-    highest = jnp.max(jnp.where(inside, logits, -jnp.inf), axis=1, keepdims=True)
-    shifted = jnp.where(inside, logits - highest, 0.0)
-    total = jnp.sum(jnp.where(inside, jnp.exp(shifted), 0.0), axis=1, keepdims=True)
-    log_total = jnp.log(total)
-    chosen = (lane == seed_ref[:, fan_outer : fan_outer + 1]).astype(jnp.float32)
-    row_weight = seed_ref[:, fan_outer + 1 : fan_outer + 2].astype(jnp.float32)
-    loss = jnp.sum((log_total - jnp.sum(shifted * chosen, axis=1, keepdims=True)) * row_weight)
-    grad_logits = (jnp.exp(shifted - log_total) - chosen) * (row_weight / label_count)
-    grad_logits = jnp.where(inside, grad_logits, 0.0).astype(jnp.bfloat16)
-    grad_head = outer_product(hidden_two, grad_logits)
-    grad_two = against(grad_logits, full_head).astype(jnp.bfloat16).astype(jnp.float32)
-    grad_pre_two = (grad_two * gate_two * (1.0 + pre_two * (1.0 - gate_two))).astype(jnp.bfloat16)
-    grad_outer = outer_product(joined_two, grad_pre_two)
-    grad_joined = against(grad_pre_two, full_outer)
-    share = grad_joined[:, hidden:] / count_two
-    share_high = share.astype(jnp.bfloat16)
-    share_low = (share - share_high.astype(jnp.float32)).astype(jnp.bfloat16)
-    for number, place in enumerate(order):
-        grads_ref[place, split[1] : split[2], :] = grad_outer[
-            number * row_outer : (number + 1) * row_outer
-        ]
-        grads_ref[place, split[2] : split[3], :] = grad_head[
-            number * row_head : (number + 1) * row_head
-        ]
-    inner_sum[...] = jnp.zeros(inner_sum.shape, jnp.float32)
-    share_parts = jnp.concatenate([share_high, share_low], axis=0)
-
-    def backward(tile, bias_sum, own=None):
-        start_at = pl.multiple_of(jnp.int32(tile) * TILE, TILE)
-        rows = pl.ds(start_at, TILE)
-        hits = hits_back_ref[rows, :]
-        both_hits = jnp.concatenate([hits, hits], axis=1)
-        grad_one = jnp.dot(both_hits, share_parts, preferred_element_type=jnp.float32)
-        if own is not None:
-            grad_one = grad_one + own
-        grad_one = grad_one.astype(jnp.bfloat16).astype(jnp.float32)
-        before = first_pre[rows, :]
-        gate = lax.logistic(before)
-        grad_pre = (grad_one * gate * (1.0 + before * (1.0 - gate))).astype(jnp.bfloat16)
-        inner_sum[...] += outer_product(joined_ref[rows, :], grad_pre)
-        return bias_sum + jnp.sum(grad_pre.astype(jnp.float32), axis=0, keepdims=True)
-
-    own_part[...] = jnp.zeros(own_part.shape, jnp.float32)
-    own_part[0:seeds, :] = grad_joined[:, 0:hidden]
-    bias_sum = backward(0, jnp.zeros((1, hidden), jnp.float32), own_part[...])
-    bias_sum = lax.fori_loop(1, tiles, backward, bias_sum)
-    grad_inner = inner_sum[...]
-    for number, place in enumerate(order):
-        grads_ref[place, split[0] : split[1], :] = grad_inner[
-            number * row_inner : (number + 1) * row_inner
-        ]
-    extra_ref[0:1, :] = bias_sum
-    extra_ref[1:2, :] = jnp.sum(grad_pre_two.astype(jnp.float32), axis=0, keepdims=True)
-    extra_ref[2:3, :] = jnp.sum(grad_logits.astype(jnp.float32), axis=0, keepdims=True)
-    extra_ref[3:4, :] = jnp.where(lane == 0, loss, jnp.where(lane == 1, label_count, 0.0))
-    extra_ref[4:8, :] = jnp.zeros((4, hidden), jnp.float32)
-
-
-def bias_rows_of(ref, hidden):
-    width = ref.shape[0] - 2 * hidden
-    last = ref[pl.ds(2 * hidden, width)].reshape(1, width)
-    return (
-        ref[pl.ds(0, hidden)].reshape(1, hidden),
-        ref[pl.ds(hidden, hidden)].reshape(1, hidden),
-        jnp.concatenate([last, jnp.zeros((1, hidden - width), jnp.float32)], axis=1),
-    )
-
-
-def dense(sizes, joined, everyone, hits, hits_back, biases, seed_table):
-    dest_count, hidden = joined.shape
-    vmem = pl.BlockSpec(memory_space=pltpu.VMEM)
-    return pl.pallas_call(
-        functools.partial(dense_kernel, sizes),
-        out_shape=(
-            jax.ShapeDtypeStruct(everyone.shape, jnp.float32),
-            jax.ShapeDtypeStruct((8, hidden), jnp.float32),
-        ),
-        in_specs=[vmem] * 6,
-        out_specs=(vmem, vmem),
-        scratch_shapes=[
-            pltpu.VMEM((dest_count, hidden), jnp.float32),
-            pltpu.VMEM((dest_count, hidden), jnp.bfloat16),
-            pltpu.VMEM((TILE, hidden), jnp.float32),
-            pltpu.VMEM((hidden, hidden), jnp.float32),
-        ],
-        compiler_params=pltpu.CompilerParams(vmem_limit_bytes=32 * 2**20),
-    )(joined, everyone, hits, hits_back, biases, seed_table)
-
-
-def reduce_kernel(
-    sizes,
-    grads_ref,
-    extra_ref,
-    weight_refs,
-    first_refs,
-    second_refs,
-    out_ref,
-    half,
-    half_in,
-    fourth,
-    plane_in,
-    line_in,
-    extra_plane,
-    extra_line,
-    sums_plane,
-    sums_line,
-    recv_sem,
-    send_sem,
-):
-    section, at = lax.axis_index("section"), lax.axis_index("dp")
-    z, core = at // 2, at % 2
-    rows, hidden = grads_ref.shape[1], grads_ref.shape[2]
-    twin = (section, z * 2 + 1 - core)
-    plane = [((section + k) % 4, at) for k in range(1, 4)]
-    beyond = [((section + k) % 4, z * 2 + 1 - core) for k in range(1, 4)]
-    line = [(section, ((z + k) % 4) * 2 + core) for k in range(1, 4)]
-    barrier = pltpu.get_barrier_semaphore()
-    for partner in [twin] + plane + beyond + line:
-        pl.semaphore_signal(barrier, inc=1, device_id=partner, device_id_type=MESH)
-    pl.semaphore_wait(barrier, 10)
-    copies = []
-
-    def send(source, target, number, device):
-        copy = pltpu.make_async_remote_copy(
-            src_ref=source,
-            dst_ref=target,
-            send_sem=send_sem.at[len(copies)],
-            recv_sem=recv_sem.at[number],
-            device_id=device,
-            device_id_type=MESH,
-        )
-        copies.append(copy)
-        copy.start()
-
-    def arrived(target, number):
-        pltpu.make_async_copy(target, target, recv_sem.at[number]).wait()
-
-    def share(value, slots, base, me, partners):
-        slots[me] = value
-        for partner in partners:
-            send(slots.at[me], slots.at[me], base + me, partner)
-
-    def collect(slots, base, me):
-        count = slots.shape[0]
-        for k in range(1, count):
-            other = (me + k) % count
-            arrived(slots.at[other], base + other)
-        values = [slots[k] for k in range(count)]
-        while len(values) > 1:
-            values = [values[k] + values[k + 1] for k in range(0, len(values), 2)]
-        return values[0]
-
-    place = section * 2 + core
-    neighbours = [twin] + plane + beyond
-
-    send(grads_ref.at[pl.ds((1 - core) * 16, 16)], half_in, 0, twin)
-    share(extra_ref[...], extra_plane, 9, place, neighbours)
-    arrived(half_in, 0)
-    half[...] = grads_ref[pl.ds(core * 16, 16)] + half_in[...]
-    for partner in plane:
-        send(half.at[pl.ds(partner[0] * 4, 4)], plane_in.at[section], 1 + section, partner)
-    share(collect(extra_plane, 9, place), extra_line, 17, z, line)
-    plane_in[section] = half[pl.ds(section * 4, 4)]
-    for k in range(1, 4):
-        other = (section + k) % 4
-        arrived(plane_in.at[other], 1 + other)
-    fourth[...] = (plane_in[0] + plane_in[1]) + (plane_in[2] + plane_in[3])
-    for k, partner in enumerate(line):
-        send(fourth.at[pl.ds((z + k + 1) % 4, 1)], line_in.at[pl.ds(z, 1)], 5 + z, partner)
-    line_in[z] = fourth[z]
-    extra = collect(extra_line, 17, z)
-    for k in range(1, 4):
-        other = (z + k) % 4
-        arrived(line_in.at[pl.ds(other, 1)], 5 + other)
-    shard = (line_in[0] + line_in[1]) + (line_in[2] + line_in[3])
-
-    lane = lax.broadcasted_iota(jnp.int32, (8, 128), 1)
-
-    def packed(values):
-        found = jnp.zeros((8, 128), jnp.float32)
-        for k, value in enumerate(values):
-            found = jnp.where(lane == k, value, found)
-        return found
-
-    def unpacked(found, k):
-        return jnp.sum(jnp.where(lane[0:1] == k, found[0:1], 0.0))
-
-    classes, row_inner, row_outer, row_head = sizes
-    split = (0, row_inner, row_inner + row_outer, rows)
-    widths = (hidden, hidden, classes)
-    pieces = [shard[split[k] : split[k + 1], : widths[k]] for k in range(3)]
-    weights = [ref[...] for ref in weight_refs]
-    values = packed(
-        [jnp.sum(shard * shard)] + [jnp.sum(weight * weight) for weight in weights]
-    )
-    share(values, sums_plane.at[0], 21, place, neighbours)
-    share(collect(sums_plane.at[0], 21, place), sums_line.at[0], 29, z, line)
-    values = collect(sums_line.at[0], 29, z)
-    bias_square = jnp.sum(extra[0:3] * extra[0:3])
-    clip_norm = jnp.sqrt(jnp.full((1, 1), unpacked(values, 0) + bias_square, jnp.float32))
-    factor = jnp.minimum(1.0, CLIP / clip_norm)
-    parts = []
-    for k in range(3):
-        update = moments(weights[k], pieces[k] * factor, first_refs[k][...], second_refs[k][...])[2]
-        parts.append(jnp.sum(update * update))
-    updates = packed(parts)
-    share(updates, sums_plane.at[1], 33, place, neighbours)
-    share(collect(sums_plane.at[1], 33, place), sums_line.at[1], 41, z, line)
-    updates = collect(sums_line.at[1], 41, z)
-    out_ref[0:rows, :] = shard
-    out_ref[rows : rows + 8, :] = extra
-    out_ref[rows + 8 : rows + 16, 0:128] = values
-    out_ref[rows + 8 : rows + 16, 128:256] = updates
-    for copy in copies:
-        copy.wait_send()
-
-
-def reduced(sizes, grads, extra, weights, firsts, seconds):
-    blocks, rows, hidden = grads.shape
-    vmem = pl.BlockSpec(memory_space=pltpu.VMEM)
-    return pl.pallas_call(
-        functools.partial(reduce_kernel, sizes),
-        out_shape=jax.ShapeDtypeStruct((rows + 16, hidden), jnp.float32),
-        in_specs=[vmem, vmem, (vmem,) * 3, (vmem,) * 3, (vmem,) * 3],
-        out_specs=vmem,
-        scratch_shapes=[
-            pltpu.VMEM((16, rows, hidden), jnp.float32),
-            pltpu.VMEM((16, rows, hidden), jnp.float32),
-            pltpu.VMEM((4, rows, hidden), jnp.float32),
-            pltpu.VMEM((4, 4, rows, hidden), jnp.float32),
-            pltpu.VMEM((4, rows, hidden), jnp.float32),
-            pltpu.VMEM((8, 8, hidden), jnp.float32),
-            pltpu.VMEM((4, 8, hidden), jnp.float32),
-            pltpu.VMEM((2, 8, 8, 128), jnp.float32),
-            pltpu.VMEM((2, 4, 8, 128), jnp.float32),
-            pltpu.SemaphoreType.DMA((45,)),
-            pltpu.SemaphoreType.DMA((37,)),
-        ],
-        compiler_params=pltpu.CompilerParams(
-            collective_id=1, has_side_effects=True, vmem_limit_bytes=16 * 2**20
-        ),
-    )(grads, extra, weights, firsts, seconds)
 
 
 def final_kernel(
@@ -858,7 +831,8 @@
         and len(mask_sizes) == 2
         and mask_sizes[0] * mask_sizes[1] <= 65536
         and all(rows % 8 == 0 for rows in weight_rows)
-        and sum(weight_rows) % 32 == 0
+        and sum(weight_rows) % 16 == 0
+        and dest_count // TILE > PAUSE
     )
 
 
@@ -1011,13 +985,18 @@
             ],
             axis=1,
         )
-        joined_one, everyone, hits, hits_back = gathered(
-            classes, fan_outer, node_table, weights, whole_mask, place, near, seed_table
+        sums = summed_step(
+            fan_outer,
+            node_table,
+            weights,
+            firsts,
+            seconds,
+            biases,
+            whole_mask,
+            place,
+            near,
+            seed_table,
         )
-        grads, extra = dense(
-            (classes, fan_outer, *rows), joined_one, everyone, hits, hits_back, biases, seed_table
-        )
-        sums = reduced((classes, *rows), grads, extra, weights, firsts, seconds)
         loss, count, clip, norms, news, moment, square, average, bias_outs = finished(
             (classes, *rows),
             sums,

time: 218 us -> 203 us (0.931)
  Pallas kernels: 204 us -> 191 us
  local copies, waits for them, and re-layouts: 10.6 us -> 7.71 us
    pallas_call x3 -> x1, Pallas kernels: 202 us -> 189 us  [summed_step(): pl.pallas_call(functools.partial(step_kernel, fan_outer), out_shape=jax.S...]
    unnamed x33 -> x3, local copies, waits for them, and re-layouts: 6.08 us -> 1.32 us
where the time goes in v5:
time: 203 us; the launch traced here: 202 us
  Pallas kernels  191 us (94%)
  local copies, waits for them, and re-layouts  7.71 us (4%)
  other arithmetic  2.8 us (1%)
    pallas_call x1, Pallas kernels, summed_step(): pl.pallas_call(functools.partial(step_kernel, fan_outer), out_shape=jax.S...  189 us

profile of v5, /device:TPU:0, one launch (start us, length us, event | category | flops | bytes accessed | tf_op | source)
XLA Modules:
  0.0 202.1 jit_solution(9803012111801762599)
XLA Ops:
  0.7 0.0 copy-start
  0.7 1.1 broadcast_multiply_fusion
  1.7 0.9 add.16
  2.7 0.7 copy.54
  3.4 0.0 copy-done
  3.4 0.1 constant_dynamic-slice_fusion.4
  3.6 0.8 dynamic-slice_reduce_fusion
  4.5 0.4 copy.56
  4.9 1.2 reshape.72.near_ref
  6.1 0.7 fusion.3
  6.8 0.7 constant_dynamic-slice_fusion.3
  7.5 0.8 constant_dynamic-slice_fusion.2
  8.4 0.1 pad.3.clone
  8.4 0.1 add_add_fusion
  8.5 0.8 copy.58.seed_ref
  9.3 0.7 fusion.4.seed_across_ref
  9.9 188.9 %shard_map.392.sums_ref = f32[48,256]{1,0:T(8,128)} custom-call(bf16[8192,2,128]{2,1,0:T(2,128)(2,1)} %bitcast.22, f32[8,256]{1,0:T(8,128)} %weight_refs_0_.3, f32[16,256]{1,0:T(8,128)} %weight_refs_1_.3, f32[8,172]{1,0:T(8,128)} %weight_refs_2_.3, f32[8,256]{1,0:T(8,128)} %first_refs_0_.3, f32[16,256]{1,0:T(8,128)} %first_refs_1_.3, ...), custom_call_target="tpu_custom_call" | custom-call | tf_op jit(solution)/shard_map/pallas_call | solution.py:651
  198.8 1.9 shard_map.393
  200.8 1.3 copy.59
  (5 shorter events, 0.1 us)
Async XLA Ops:
  0.7 2.8 %copy-start = (s32[4,2816,15]{1,0,2:T(4,128)S(1)}, s32[4,2816,15]{1,0,2:T(4,128)}, u32[]{:S(2)}) copy-start(s32[4,2816,15]{1,0,2:T(4,128)} %param.28) | copy-start | bytes 2027524

commit v6 on v5

--- a/solution.py
+++ b/solution.py
@@ -28,14 +28,15 @@
 GROUP = 4
 SETS = 4
 SPARE = 8
-AHEAD = 2
+AHEAD = 1
 AHEAD_ACROSS = 1
-LAG = 1
-FAR_LAG = 2
+LAG = 2
+FAR_LAG = 5
 SPARE_AFTER = 2
-SPARE_LAG = 3
+SPARE_LAG = 4
 TILE = 256
 PAUSE = 6
+FORWARD_SLOT = 2
 
 
 class Parts:
@@ -52,10 +53,12 @@
     second_refs,
     bias_ref,
     mask_ref,
-    place_ref,
+    owner_ref,
+    local_ref,
     near_ref,
-    seed_ref,
-    seed_across_ref,
+    seed_near_ref,
+    seed_count_ref,
+    label_ref,
     out_ref,
     joined_ref,
     weights_ref,
@@ -67,8 +70,14 @@
     idx_ref,
     mix_ref,
     wide,
+    seed_ref,
+    seed_across_ref,
     stages,
     lists,
+    full_inner_ref,
+    full_outer_ref,
+    full_head_ref,
+    count_ref,
     first_pre,
     first_hidden,
     own_part,
@@ -78,8 +87,7 @@
     extra_ref,
     extra_plane,
     extra_line,
-    sums_plane,
-    sums_line,
+    sums,
     own_sem,
     z_sem,
     spare_sem,
@@ -123,9 +131,10 @@
     neighbours = [twin] + plane + beyond
 
     barrier = pltpu.get_barrier_semaphore()
-    for partner in neighbours + line:
+    others = [((section + k // 8) % 4, (at + k % 8) % 8) for k in range(1, 32)]
+    for partner in others:
         pl.semaphore_signal(barrier, inc=1, device_id=partner, device_id_type=MESH)
-    pl.semaphore_wait(barrier, 10)
+    pl.semaphore_wait(barrier, 31)
 
     sent = []
 
@@ -203,15 +212,36 @@
 
     double_start(0)
 
-    placed = place_ref[...]
+    def eye(size):
+        same_place = lax.broadcasted_iota(jnp.int32, (size, size), 0) == lax.broadcasted_iota(
+            jnp.int32, (size, size), 1
+        )
+        return same_place.astype(jnp.float32).astype(jnp.bfloat16)
+
+    def as_low(values):
+        return values.astype(jnp.float32).astype(jnp.bfloat16)
+
+    placed = owner_ref[...] * (2 * pairs) + local_ref[...]
     pair_at = placed // 2
-    high = place_ref.shape[1]
-    parts[0:128, :] = (pair_at % 256).astype(jnp.float32).astype(jnp.bfloat16)
-    parts[128:256, :] = (pair_at // 256).astype(jnp.float32).astype(jnp.bfloat16)
-    parts[256:384, :] = (placed % 2).astype(jnp.float32).astype(jnp.bfloat16)
+    high = owner_ref.shape[0]
+    for k, values in enumerate((pair_at % 256, pair_at // 256, placed % 2)):
+        parts[128 * k : 128 * (k + 1), :] = against(eye(128), as_low(values)).astype(jnp.bfloat16)
     looked_rows = near_ref.shape[0]
     seeds = seed_ref.shape[0]
     tiles = hits_ref.shape[1] // TILE
+    seed_row = pl.ds(section, 1)
+    live_seeds = seed_count_ref[seed_row, :]
+    for j in range(fan_outer):
+        near_seeds = seed_near_ref[j, seed_row, :]
+        seed_across_ref[j : j + 1, :] = jnp.where(live_seeds > j, near_seeds, -1)
+    seed_across_ref[fan_outer : fan_outer + 1, :] = label_ref[seed_row, :]
+    seed_across_ref[fan_outer + 1 : fan_outer + 2, :] = mask_ref[seed_row, :]
+    seed_across_ref[fan_outer + 2 :, :] = jnp.zeros((SLOT - fan_outer - 2, seeds), jnp.int32)
+    shifted_up = seed_across_ref[...] + 1
+    seed_ref[...] = (
+        64.0 * against(eye(seeds), as_low(shifted_up // 64))
+        + against(eye(seeds), as_low(shifted_up % 64))
+    ).astype(jnp.int32) - 1
     total = 3 * CHUNKS
     steps = total + max(FAR_LAG, SPARE_LAG)
     per_step = -(-looked_rows // (8 * steps)) * 8
@@ -264,6 +294,22 @@
         for j in range(fan_outer):
             hits = hits + (seed_across_ref[j : j + 1, :] == dest).astype(jnp.float32)
         hits_back_ref[start_at : start_at + TILE, :] = hits.astype(jnp.bfloat16)
+
+    def sort_weights():
+        everyone = weights_ref[...].astype(jnp.float32)
+        order = block_order()
+        inner, outer, head = (
+            jnp.concatenate([everyone[spot, lower:upper] for spot in order], axis=0)
+            for lower, upper in ((0, row_inner), (row_inner, head_at), (head_at, head_at + row_head))
+        )
+        full_inner_ref[...] = inner.astype(jnp.bfloat16)
+        full_outer_ref[...] = outer.astype(jnp.bfloat16)
+        full_head_ref[...] = jnp.where(lane < classes, head, 0.0).astype(jnp.bfloat16)
+        tails = everyone[0:4, head_at : head_at + 1] + everyone[16:20, head_at : head_at + 1]
+        tails = jnp.sum(tails.reshape(4, hidden), axis=0, keepdims=True)
+        scale = jnp.where(lane == classes, 256.0, jnp.where(lane == classes + 1, 1.0, 0.0))
+        count = jnp.sum(tails * scale, axis=1, keepdims=True)
+        count_ref[...] = jnp.broadcast_to(jnp.maximum(count, 1.0), count_ref.shape)
 
     twins = []
 
@@ -332,6 +378,7 @@
         for tile in range(step * tiles // steps, (step + 1) * tiles // steps):
             mark(tile)
 
+    sort_weights()
     for number in sorted(twins):
         kind, step = divmod(number, total)
         turn, piece = divmod(step, CHUNKS)
@@ -345,10 +392,10 @@
     own.wait()
 
     blocks = looked_rows
-    lane = lax.broadcasted_iota(jnp.int32, (BLOCK, 2 * BLOCK * SLOT), 1)
-    same = lane // (2 * SLOT) == lax.broadcasted_iota(jnp.int32, lane.shape, 0)
-    near_part = jnp.logical_and(same, lane % (2 * SLOT) < 2 * SLOT - 2).astype(jnp.float32)
-    self_part = jnp.logical_and(same, lane % (2 * SLOT) >= 2 * SLOT - 2).astype(jnp.float32)
+    unit_at = lax.broadcasted_iota(jnp.int32, (BLOCK, 2 * BLOCK * SLOT), 1)
+    same = unit_at // (2 * SLOT) == lax.broadcasted_iota(jnp.int32, unit_at.shape, 0)
+    near_part = jnp.logical_and(same, unit_at % (2 * SLOT) < 2 * SLOT - 2).astype(jnp.float32)
+    self_part = jnp.logical_and(same, unit_at % (2 * SLOT) >= 2 * SLOT - 2).astype(jnp.float32)
     turns = blocks // GROUP
 
     def fetch(turn, slot):
@@ -374,7 +421,21 @@
         start_at = pl.multiple_of(block * BLOCK, BLOCK)
         joined_ref[pl.ds(start_at, BLOCK), :] = both.astype(jnp.bfloat16)
 
+    bias_inner, bias_outer, bias_head = bias_rows_of(bias_ref, hidden)
+
+    def forward(tile):
+        tile_rows = pl.ds(pl.multiple_of(tile * TILE, TILE), TILE)
+        before = (
+            jnp.dot(
+                joined_ref[tile_rows, :], full_inner_ref[...], preferred_element_type=jnp.float32
+            )
+            + bias_inner
+        )
+        first_pre[tile_rows, :] = before
+        first_hidden[tile_rows, :] = (before * lax.logistic(before)).astype(jnp.bfloat16)
+
     near_stages, far_stages = stages
+    joined_ref[0:TILE, :] = jnp.zeros((TILE, joined_ref.shape[1]), jnp.bfloat16)
     for slot in range(SETS):
         fetch(slot, slot).start()
     for member in range(GROUP):
@@ -390,6 +451,8 @@
                     jnp.maximum((turn - 1) * GROUP + member, 0), stages[1 - slot % 2][member]
                 )
             fetch(turn + SETS, slot).start()
+            if slot == FORWARD_SLOT:
+                forward(jnp.maximum(number - 1, 0))
         return carry
 
     lax.fori_loop(0, blocks // (GROUP * SETS), round_of, 0)
@@ -397,6 +460,7 @@
         fetch(0, slot).wait()
     for member in range(GROUP):
         reduce(blocks - GROUP + member, stages[(SETS - 1) % 2][member])
+    forward(tiles - 1)
     for copy, when in sent:
         if when is None:
             copy.wait_send()
@@ -465,37 +529,11 @@
         return values[0]
 
     early, late_part = Parts(early_refs, 0), Parts(late_refs, 9)
-    dest_count = joined_ref.shape[0]
     order = block_order()
-    weights = weights_ref[...].astype(jnp.float32)
-    split = (0, row_inner, head_at, head_at + row_head)
-    full_inner, full_outer, full_head = (
-        jnp.concatenate([weights[spot, split[k] : split[k + 1]] for spot in order], axis=0)
-        for k in range(3)
-    )
-    lane = lax.broadcasted_iota(jnp.int32, (1, hidden), 1)
-    tails = weights[0:4, head_at : head_at + 1] + weights[16:20, head_at : head_at + 1]
-    tails = jnp.sum(tails.reshape(4, hidden), axis=0, keepdims=True)
-    scale = jnp.where(lane == classes, 256.0, jnp.where(lane == classes + 1, 1.0, 0.0))
-    label_count = jnp.maximum(jnp.sum(tails * scale), 1.0)
-    full_inner = full_inner.astype(jnp.bfloat16)
-    full_outer = full_outer.astype(jnp.bfloat16)
-    full_head = jnp.where(lane < classes, full_head, 0.0).astype(jnp.bfloat16)
-    bias_inner, bias_outer, bias_head = bias_rows_of(bias_ref, hidden)
+    full_outer, full_head = full_outer_ref[...], full_head_ref[...]
+    label_count = count_ref[:, 0:1]
     kept = seed_ref[:, 0:fan_outer]
     count_two = jnp.sum((kept >= 0).astype(jnp.float32), axis=1, keepdims=True)
-
-    def forward(tile, carry):
-        tile_rows = pl.ds(pl.multiple_of(tile * TILE, TILE), TILE)
-        before = (
-            jnp.dot(joined_ref[tile_rows, :], full_inner, preferred_element_type=jnp.float32)
-            + bias_inner
-        )
-        first_pre[tile_rows, :] = before
-        first_hidden[tile_rows, :] = (before * lax.logistic(before)).astype(jnp.bfloat16)
-        return carry
-
-    lax.fori_loop(0, tiles, forward, 0)
     mean_sum = jnp.dot(hits_ref[...], first_hidden[...], preferred_element_type=jnp.float32)
     mean_two = (mean_sum / count_two).astype(jnp.bfloat16)
     joined_two = jnp.concatenate([first_hidden[0:seeds, :], mean_two], axis=1)
@@ -567,44 +605,48 @@
     share(collect(extra_plane, 18, section * 2 + core), extra_line, 26, z, line)
     to_line(late_part)
 
-    deep_lane = lax.broadcasted_iota(jnp.int32, (8, 128), 1)
-
-    def packed_up(values):
-        found = jnp.zeros((8, 128), jnp.float32)
+    short_lane = lax.broadcasted_iota(jnp.int32, (1, 128), 1)
+    my_number = section * 8 + at
+
+    def square_sum(value):
+        return jnp.sum(jnp.sum(value * value, axis=0, keepdims=True), axis=1, keepdims=True)
+
+    def everywhere(values, number):
+        base = 30 + 32 * number
+        found = jnp.zeros((1, 128), jnp.float32)
         for k, value in enumerate(values):
-            found = jnp.where(deep_lane == k, value, found)
-        return found
-
-    def everywhere(values, number):
-        base = 30 + 12 * number
-        place_in = section * 2 + core
-        share(packed_up(values), sums_plane.at[number], base, place_in, neighbours)
-        plane_sum = collect(sums_plane.at[number], base, place_in)
-        share(plane_sum, sums_line.at[number], base + 8, z, line)
-        return collect(sums_line.at[number], base + 8, z)
+            found = jnp.where(short_lane == k, value, found)
+        sums[number, my_number] = found
+        for partner in others:
+            mine_there = sums.at[number, my_number]
+            pass_on(mine_there, mine_there, base + my_number, partner)
+        for partner in others:
+            other = partner[0] * 8 + partner[1]
+            passed(sums.at[number, other], base + other)
+        return jnp.sum(sums[number], axis=0)
 
     held = [ref[...] for ref in weight_refs]
-    weight_squares = [jnp.sum(weight * weight) for weight in held]
+    weight_squares = [square_sum(weight) for weight in held]
     rest = whole_sum(early)
     shard = whole_sum(late_part)
     extra = collect(extra_line, 26, z)
     pieces = [shard, rest[0:row_outer], rest[row_outer:, 0:classes]]
-    values = everywhere([jnp.sum(shard * shard) + jnp.sum(rest * rest)] + weight_squares, 0)
-    grad_square = jnp.sum(jnp.where(deep_lane[0:1] == 0, values[0:1], 0.0))
-    bias_square = jnp.sum(extra[0:3] * extra[0:3])
-    clip_norm = jnp.sqrt(jnp.full((1, 1), grad_square + bias_square, jnp.float32))
+    values = everywhere([square_sum(shard) + square_sum(rest)] + weight_squares, 0)
+    grad_square = jnp.sum(jnp.where(short_lane == 0, values, 0.0), axis=1, keepdims=True)
+    clip_norm = jnp.sqrt(grad_square + square_sum(extra[0:3]))
     factor = jnp.minimum(1.0, CLIP / clip_norm)
     update_squares = []
     for k in range(3):
         update = moments(held[k], pieces[k] * factor, first_refs[k][...], second_refs[k][...])[2]
-        update_squares.append(jnp.sum(update * update))
+        update_squares.append(square_sum(update))
     updates = everywhere(update_squares, 1)
     rows = row_inner + row_outer + row_head
     out_ref[0:row_inner, :] = shard
     out_ref[row_inner:rows, :] = rest
     out_ref[rows : rows + 8, :] = extra
-    out_ref[rows + 8 : rows + 16, 0:128] = values
-    out_ref[rows + 8 : rows + 16, 128:256] = updates
+    out_ref[rows + 8 : rows + 9, 0:128] = values
+    out_ref[rows + 8 : rows + 9, 128:256] = updates
+    out_ref[rows + 9 :, :] = jnp.zeros((7, hidden), jnp.float32)
     for copy in summing:
         copy.wait_send()
 
@@ -623,13 +665,27 @@
     )
 
 
-def summed_step(fan_outer, node_table, weights, firsts, seconds, biases, label_mask, place, near, seed_table):
+def summed_step(
+    node_table,
+    weights,
+    firsts,
+    seconds,
+    biases,
+    label_mask,
+    owner_ids,
+    row_ids,
+    near,
+    outer_neighbours,
+    outer_counts,
+    labels,
+):
     devices = lax.axis_size(("section", "dp"))
     table_rows, width = node_table.shape
-    frontier_high = place.shape[1]
+    frontier_high = owner_ids.size // 128
+    fan_outer = outer_neighbours.shape[2]
     looked = near.shape[0]
     dest_count = looked * BLOCK
-    seeds = seed_table.shape[0]
+    seeds = outer_neighbours.shape[1]
     hidden = weights[0].shape[1]
     row_inner = weights[0].shape[0]
     rows = sum(weight.shape[0] for weight in weights)
@@ -651,7 +707,7 @@
     return pl.pallas_call(
         functools.partial(step_kernel, fan_outer),
         out_shape=jax.ShapeDtypeStruct((rows + 16, hidden), jnp.float32),
-        in_specs=[pl.BlockSpec(memory_space=pl.ANY)] + [(vmem,) * 3] * 3 + [vmem] * 6,
+        in_specs=[pl.BlockSpec(memory_space=pl.ANY)] + [(vmem,) * 3] * 3 + [vmem] * 8,
         out_specs=vmem,
         scratch_shapes=[
             pltpu.VMEM((dest_count, 2 * width), jnp.bfloat16),
@@ -664,8 +720,14 @@
             pltpu.VMEM((looked // GROUP, GROUP, 256), jnp.int32),
             pltpu.VMEM((looked, 512), jnp.float32),
             pltpu.VMEM((fan_outer, seeds, TILE), jnp.int32),
+            pltpu.VMEM((seeds, SLOT), jnp.int32),
+            pltpu.VMEM((SLOT, seeds), jnp.int32),
             (stage, stage),
             (pltpu.SMEM((GROUP, BLOCK * SLOT), jnp.int32),) * SETS,
+            pltpu.VMEM((hidden, hidden), jnp.bfloat16),
+            pltpu.VMEM((2 * hidden, hidden), jnp.bfloat16),
+            pltpu.VMEM((hidden, hidden), jnp.bfloat16),
+            pltpu.VMEM((1, hidden), jnp.float32),
             pltpu.VMEM((dest_count, hidden), jnp.float32),
             pltpu.VMEM((dest_count, hidden), jnp.bfloat16),
             pltpu.VMEM((TILE, hidden), jnp.float32),
@@ -675,8 +737,7 @@
             pltpu.VMEM((8, hidden), jnp.float32),
             pltpu.VMEM((8, 8, hidden), jnp.float32),
             pltpu.VMEM((4, 8, hidden), jnp.float32),
-            pltpu.VMEM((2, 8, 8, 128), jnp.float32),
-            pltpu.VMEM((2, 4, 8, 128), jnp.float32),
+            pltpu.VMEM((2, devices, 1, 128), jnp.float32),
             pltpu.SemaphoreType.DMA(()),
             pltpu.SemaphoreType.DMA((total,)),
             pltpu.SemaphoreType.DMA((total,)),
@@ -689,8 +750,8 @@
             pltpu.SemaphoreType.DMA((sends,)),
             pltpu.SemaphoreType.DMA((5,)),
             pltpu.SemaphoreType.DMA((SETS,)),
-            pltpu.SemaphoreType.DMA((54,)),
-            pltpu.SemaphoreType.DMA((44,)),
+            pltpu.SemaphoreType.DMA((30 + 2 * devices,)),
+            pltpu.SemaphoreType.DMA((24 + 2 * (devices - 1),)),
         ],
         compiler_params=pltpu.CompilerParams(
             collective_id=0, has_side_effects=True, vmem_limit_bytes=56 * 2**20
@@ -704,10 +765,12 @@
         seconds,
         biases,
         label_mask,
-        place,
+        owner_ids.reshape(-1, 128),
+        row_ids.reshape(-1, 128),
         near,
-        seed_table,
-        seed_table.T,
+        outer_neighbours.transpose(2, 0, 1),
+        outer_counts,
+        labels,
     )
 
 
@@ -742,7 +805,7 @@
         return jnp.sum(jnp.where(lane == k, found, 0.0), axis=1, keepdims=True)
 
     bias_grad = sums_ref[rows : rows + 3, :]
-    bias_square = jnp.sum(jnp.sum(bias_grad * bias_grad, axis=1, keepdims=True), axis=0, keepdims=True)
+    bias_square = jnp.sum(jnp.sum(bias_grad * bias_grad, axis=0, keepdims=True), axis=1, keepdims=True)
     clip_norm = jnp.sqrt(number(0, 0) + bias_square)
     factor = jnp.minimum(1.0, CLIP / clip_norm)
     wide = lax.broadcasted_iota(jnp.int32, (8, 128), 1)
@@ -758,9 +821,9 @@
         moment_refs[k][...] = first
         square_refs[k][...] = second
         average_refs[k][...] = AVERAGE * smooth_refs[k][...] + (1.0 - AVERAGE) * fresh
-        norms = jnp.where(jnp.logical_and(deep == k, wide == 0), weight_norm, norms)
-        norms = jnp.where(jnp.logical_and(deep == k, wide == 1), update_norm, norms)
-    norms_ref[...] = norms[0:3, 0:2]
+        norms = jnp.where(jnp.logical_and(deep == 0, wide == k), weight_norm, norms)
+        norms = jnp.where(jnp.logical_and(deep == 1, wide == k), update_norm, norms)
+    norms_ref[...] = norms[0:2, 0:3]
     weight, first, second, smooth = (
         jnp.concatenate(bias_rows_of(ref, hidden), axis=0) for ref in bias_refs
     )
@@ -794,7 +857,7 @@
             scalar,
             scalar,
             scalar,
-            jax.ShapeDtypeStruct((3, 2), jnp.float32),
+            jax.ShapeDtypeStruct((2, 3), jnp.float32),
             like,
             like,
             like,
@@ -826,7 +889,9 @@
         and hidden == 256
         and classes + 2 <= hidden
         and seed_count <= TILE
-        and seed_count % 16 == 0
+        and seed_count % 128 == 0
+        and dest_count < 16384
+        and BLOCK * GROUP * SETS == TILE
         and fan_outer + 2 <= SLOT
         and len(mask_sizes) == 2
         and mask_sizes[0] * mask_sizes[1] <= 65536
@@ -939,7 +1004,8 @@
     dest_count, fan_inner = inner_neighbours.shape[1:]
     seed_count, fan_outer = outer_neighbours.shape[1:]
     classes = weight_head.shape[1]
-    whole_mask = label_mask
+    whole_mask, whole_labels = label_mask, labels
+    whole_outer, whole_outer_counts = outer_neighbours, outer_counts
     mask_sizes = label_mask.shape
 
     def mine(array):
@@ -967,7 +1033,6 @@
         mask_sizes,
         [weight.shape[0] for weight in weights],
     ):
-        place = (owner_ids * node_table.shape[0] + row_ids).reshape(-1, 128).T
         own = jnp.arange(dest_count, dtype=jnp.int32)[:, None]
         near = jnp.concatenate([jnp.where(keep, inner_neighbours, -1), own], axis=1)
         near = near.reshape(-1, BLOCK * SLOT)
@@ -975,27 +1040,19 @@
         seconds = (second_inner, second_outer, second_head)
         smooths = (smooth_inner, smooth_outer, smooth_head)
         rows = [weight.shape[0] for weight in weights]
-        keep_outer = jnp.arange(fan_outer)[None, :] < outer_counts[:, None]
-        seed_table = jnp.concatenate(
-            [
-                jnp.where(keep_outer, outer_neighbours, -1),
-                labels[:, None],
-                label_mask[:, None],
-                jnp.zeros((seed_count, SLOT - fan_outer - 2), jnp.int32),
-            ],
-            axis=1,
-        )
         sums = summed_step(
-            fan_outer,
             node_table,
             weights,
             firsts,
             seconds,
             biases,
             whole_mask,
-            place,
+            owner_ids,
+            row_ids,
             near,
-            seed_table,
+            whole_outer,
+            whole_outer_counts,
+            whole_labels,
         )
         loss, count, clip, norms, news, moment, square, average, bias_outs = finished(
             (classes, *rows),
@@ -1010,7 +1067,7 @@
             loss.reshape(()),
             count.reshape(()),
             clip.reshape(()),
-            norms,
+            norms.T,
             *news,
             bias_outs[0],
             *moment,

time: 203 us -> 186 us (0.916)
  Pallas kernels: 191 us -> 182 us
  local copies, waits for them, and re-layouts: 7.71 us -> 2.88 us
  other arithmetic: 2.8 us -> 0.05 us
    pallas_call x1, Pallas kernels: 189 us -> 180 us  [summed_step(): pl.pallas_call(functools.partial(step_kernel, fan_outer), out_shape=jax.S...]
where the time goes in v6:
time: 186 us
  Pallas kernels  182 us (98%)
  local copies, waits for them, and re-layouts  2.88 us (2%)
    pallas_call x1, Pallas kernels, summed_step(): pl.pallas_call(functools.partial(step_kernel, fan_outer), out_shape=jax.S...  180 us

profile of v6, /device:TPU:0, one launch (start us, length us, event | category | flops | bytes accessed | tf_op | source)
XLA Modules:
  0.0 185.9 jit_solution(14429861218850302914)
XLA Ops:
  0.7 0.0 copy-start
  0.7 0.9 dynamic-slice_reduce_fusion
  1.6 0.2 copy-done
  1.8 0.1 constant_dynamic-slice_fusion
  2.0 0.4 copy.46
  2.4 1.2 reshape.58.near_ref
  3.6 180.2 %shard_map.392.sums_ref = f32[48,256]{1,0:T(8,128)} custom-call(bf16[8192,2,128]{2,1,0:T(2,128)(2,1)} %bitcast.12, f32[8,256]{1,0:T(8,128)} %weight_refs_0_.3, f32[16,256]{1,0:T(8,128)} %weight_refs_1_.3, f32[8,172]{1,0:T(8,128)} %weight_refs_2_.3, f32[8,256]{1,0:T(8,128)} %first_refs_0_.3, f32[16,256]{1,0:T(8,128)} %first_refs_1_.3, ...), custom_call_target="tpu_custom_call" | custom-call | tf_op jit(solution)/shard_map/pallas_call | solution.py:707
  183.8 1.9 %shard_map.393 = (f32[1,1]{1,0:T(1,128)}, f32[1,1]{1,0:T(1,128)}, f32[1,1]{1,0:T(1,128)}, f32[2,3]{1,0:T(2,128)}, f32[8,256]{1,0:T(8,128)}, /*index=5*/f32[16,25...) custom-call(f32[48,256]{1,0:T(8,128)} %shard_map.392.sums_ref, ...), custom_call_target="tpu_custom_call" | custom-call | tf_op jit(solution)/shard_map/pallas_call | solution.py:854
  (3 shorter events, 0.1 us)
Async XLA Ops:
  0.7 1.1 copy-start

commit v7 on v6

--- a/solution.py
+++ b/solution.py
@@ -27,7 +27,8 @@
 CHUNKS = 4
 GROUP = 4
 SETS = 4
-SPARE = 8
+SPARE = 9
+SETTLE = 3
 AHEAD = 1
 AHEAD_ACROSS = 1
 LAG = 2
@@ -36,7 +37,8 @@
 SPARE_LAG = 4
 TILE = 256
 PAUSE = 6
-FORWARD_SLOT = 2
+FORWARD_SLOT = 1
+MEAN_SLOT = 3
 
 
 class Parts:
@@ -80,6 +82,7 @@
     count_ref,
     first_pre,
     first_hidden,
+    mean_ref,
     own_part,
     inner_sum,
     early_refs,
@@ -102,13 +105,17 @@
     list_sem,
     sum_sem,
     sum_send_sem,
+    norm_sem,
+    norm_send_sem,
+    late_sem,
+    late_send_sem,
 ):
     section, at = lax.axis_index("section"), lax.axis_index("dp")
     z, core = at // 2, at % 2
     flipped = z // 2
     height = z + flipped * (3 - 2 * z)
     pairs = table_ref.shape[0]
-    spare = pairs // SPARE
+    spare = pairs * SPARE // 64
     quarter = (pairs - spare) // 4
     chunk = quarter // CHUNKS
     spare_chunk = spare // CHUNKS
@@ -136,7 +143,7 @@
         pl.semaphore_signal(barrier, inc=1, device_id=partner, device_id_type=MESH)
     pl.semaphore_wait(barrier, 31)
 
-    sent = []
+    sent, now, count = [], [0], [0]
 
     def region(shard, part, piece):
         return full_ref.at[pl.ds(shard * pairs + part * quarter + piece * chunk, chunk)]
@@ -145,7 +152,8 @@
         return full_ref.at[pl.ds(shard * pairs + 4 * quarter + piece * spare_chunk, spare_chunk)]
 
     def send(source, target, recv, device, when=None):
-        number = len(sent)
+        number = count[0]
+        count[0] += 1
         copy = pltpu.make_async_remote_copy(
             src_ref=source,
             dst_ref=target,
@@ -154,7 +162,7 @@
             device_id=device,
             device_id_type=MESH,
         )
-        sent.append((copy, when))
+        sent.append((copy, when, now[0]))
         if when is None:
             copy.start()
         else:
@@ -308,16 +316,37 @@
         tails = everyone[0:4, head_at : head_at + 1] + everyone[16:20, head_at : head_at + 1]
         tails = jnp.sum(tails.reshape(4, hidden), axis=0, keepdims=True)
         scale = jnp.where(lane == classes, 256.0, jnp.where(lane == classes + 1, 1.0, 0.0))
-        count = jnp.sum(tails * scale, axis=1, keepdims=True)
-        count_ref[...] = jnp.broadcast_to(jnp.maximum(count, 1.0), count_ref.shape)
+        labels_in_all = jnp.sum(tails * scale, axis=1, keepdims=True)
+        count_ref[...] = jnp.broadcast_to(jnp.maximum(labels_in_all, 1.0), count_ref.shape)
 
     twins = []
 
     def to_twin(block, number):
         send(block, block, twin_sem.at[number], twin)
-        twins.append(number)
+        twins.append((number, now[0]))
+
+    def from_twin(number):
+        kind, step = divmod(number, total)
+        turn, piece = divmod(step, CHUNKS)
+        shard = sources[turn] * 2 + 1 - core
+        if kind == 4:
+            block = spare_region(shard, piece)
+        else:
+            block = region(shard, (section, beside_x[0], beside_y[0], 3 - section)[kind], piece)
+        arrived(block, twin_sem.at[number])
+
+    def settle(until):
+        while twins and twins[0][1] <= until:
+            from_twin(twins.pop(0)[0])
+        while sent and sent[0][2] <= until - SETTLE:
+            copy, when, _ = sent.pop(0)
+            if when is None:
+                copy.wait_send()
+            else:
+                pl.when(when)(copy.wait_send)
 
     for step in range(steps):
+        now[0] = step
         if step < total:
             turn, piece = divmod(step, CHUNKS)
             shard = sources[turn] * 2 + core
@@ -377,17 +406,10 @@
             look_up(first, last)
         for tile in range(step * tiles // steps, (step + 1) * tiles // steps):
             mark(tile)
+        settle(step - 3)
 
     sort_weights()
-    for number in sorted(twins):
-        kind, step = divmod(number, total)
-        turn, piece = divmod(step, CHUNKS)
-        shard = sources[turn] * 2 + 1 - core
-        if kind == 4:
-            block = spare_region(shard, piece)
-        else:
-            block = region(shard, (section, beside_x[0], beside_y[0], 3 - section)[kind], piece)
-        arrived(block, twin_sem.at[number])
+    settle(steps)
     arrived(full_ref.at[pl.ds((z * 2 + 1 - core) * pairs, pairs)], twin_own_sem)
     own.wait()
 
@@ -434,7 +456,15 @@
         first_pre[tile_rows, :] = before
         first_hidden[tile_rows, :] = (before * lax.logistic(before)).astype(jnp.bfloat16)
 
+    def add_mean(tile, carried):
+        tile_rows = pl.ds(pl.multiple_of(tile * TILE, TILE), TILE)
+        found = jnp.dot(
+            hits_ref[:, tile_rows], first_hidden[tile_rows, :], preferred_element_type=jnp.float32
+        )
+        mean_ref[...] = mean_ref[...] * carried + found
+
     near_stages, far_stages = stages
+    mean_ref[...] = jnp.zeros(mean_ref.shape, jnp.float32)
     joined_ref[0:TILE, :] = jnp.zeros((TILE, joined_ref.shape[1]), jnp.bfloat16)
     for slot in range(SETS):
         fetch(slot, slot).start()
@@ -450,9 +480,11 @@
                 reduce(
                     jnp.maximum((turn - 1) * GROUP + member, 0), stages[1 - slot % 2][member]
                 )
-            fetch(turn + SETS, slot).start()
             if slot == FORWARD_SLOT:
                 forward(jnp.maximum(number - 1, 0))
+            if slot == MEAN_SLOT:
+                add_mean(jnp.maximum(number - 1, 0), (number > 1).astype(jnp.float32))
+            fetch(turn + SETS, slot).start()
         return carry
 
     lax.fori_loop(0, blocks // (GROUP * SETS), round_of, 0)
@@ -461,11 +493,8 @@
     for member in range(GROUP):
         reduce(blocks - GROUP + member, stages[(SETS - 1) % 2][member])
     forward(tiles - 1)
-    for copy, when in sent:
-        if when is None:
-            copy.wait_send()
-        else:
-            pl.when(when)(copy.wait_send)
+    add_mean(tiles - 1, 1.0)
+    settle(steps + SETTLE)
 
     summing = []
 
@@ -528,14 +557,14 @@
             values = [values[k] + values[k + 1] for k in range(0, len(values), 2)]
         return values[0]
 
-    early, late_part = Parts(early_refs, 0), Parts(late_refs, 9)
+    early = Parts(early_refs, 0)
+    late_grads, late_half_in, late_half, late_in = late_refs
     order = block_order()
     full_outer, full_head = full_outer_ref[...], full_head_ref[...]
     label_count = count_ref[:, 0:1]
     kept = seed_ref[:, 0:fan_outer]
     count_two = jnp.sum((kept >= 0).astype(jnp.float32), axis=1, keepdims=True)
-    mean_sum = jnp.dot(hits_ref[...], first_hidden[...], preferred_element_type=jnp.float32)
-    mean_two = (mean_sum / count_two).astype(jnp.bfloat16)
+    mean_two = (mean_ref[...] / count_two).astype(jnp.bfloat16)
     joined_two = jnp.concatenate([first_hidden[0:seeds, :], mean_two], axis=1)
     pre_two = jnp.dot(joined_two, full_outer, preferred_element_type=jnp.float32) + bias_outer
     gate_two = lax.logistic(pre_two)
@@ -597,13 +626,25 @@
     extra_ref[0:1, :] = bias_sum
     grad_inner = inner_sum[...]
     for number, spot in enumerate(order):
-        late_part.grads[spot] = grad_inner[number * row_inner : (number + 1) * row_inner]
-    to_other_core(late_part)
+        late_grads[spot] = grad_inner[number * row_inner : (number + 1) * row_inner]
+    pass_on(late_grads.at[pl.ds((1 - core) * 16, 16)], late_half_in, 9, twin)
     share(extra_ref[...], extra_plane, 18, section * 2 + core, neighbours)
-    to_plane(late_part)
+    passed(late_half_in, 9)
+    late_half[...] = late_grads[pl.ds(core * 16, 16)] + late_half_in[...]
+    same_core = [((section + k // 4) % 4, (z + k % 4) % 4) for k in range(1, 16)]
+    my_place = section * 4 + z
+    for to_section, to_z in same_core:
+        pltpu.make_async_remote_copy(
+            src_ref=late_half.at[to_section * 4 + to_z],
+            dst_ref=late_in.at[my_place],
+            send_sem=late_send_sem,
+            recv_sem=late_sem,
+            device_id=(to_section, to_z * 2 + core),
+            device_id_type=MESH,
+        ).start()
+    late_in[my_place] = late_half[my_place]
     to_line(early)
     share(collect(extra_plane, 18, section * 2 + core), extra_line, 26, z, line)
-    to_line(late_part)
 
     short_lane = lax.broadcasted_iota(jnp.int32, (1, 128), 1)
     my_number = section * 8 + at
@@ -612,23 +653,29 @@
         return jnp.sum(jnp.sum(value * value, axis=0, keepdims=True), axis=1, keepdims=True)
 
     def everywhere(values, number):
-        base = 30 + 32 * number
         found = jnp.zeros((1, 128), jnp.float32)
         for k, value in enumerate(values):
             found = jnp.where(short_lane == k, value, found)
         sums[number, my_number] = found
+        mine_there = sums.at[number, my_number]
         for partner in others:
-            mine_there = sums.at[number, my_number]
-            pass_on(mine_there, mine_there, base + my_number, partner)
-        for partner in others:
-            other = partner[0] * 8 + partner[1]
-            passed(sums.at[number, other], base + other)
+            pltpu.make_async_remote_copy(
+                src_ref=mine_there,
+                dst_ref=mine_there,
+                send_sem=norm_send_sem.at[number],
+                recv_sem=norm_sem.at[number],
+                device_id=partner,
+                device_id_type=MESH,
+            ).start()
+        all_others = sums.at[number, pl.ds(0, 31)]
+        arrived(all_others, norm_sem.at[number])
         return jnp.sum(sums[number], axis=0)
 
     held = [ref[...] for ref in weight_refs]
     weight_squares = [square_sum(weight) for weight in held]
     rest = whole_sum(early)
-    shard = whole_sum(late_part)
+    arrived(late_in.at[pl.ds(0, 15)], late_sem)
+    shard = jnp.sum(late_in[...], axis=0)
     extra = collect(extra_line, 26, z)
     pieces = [shard, rest[0:row_outer], rest[row_outer:, 0:classes]]
     values = everywhere([square_sum(shard) + square_sum(rest)] + weight_squares, 0)
@@ -649,6 +696,9 @@
     out_ref[rows + 9 :, :] = jnp.zeros((7, hidden), jnp.float32)
     for copy in summing:
         copy.wait_send()
+    for number in range(2):
+        arrived(sums.at[number, pl.ds(0, 31)], norm_send_sem.at[number])
+    arrived(late_in.at[pl.ds(0, 15)], late_send_sem)
 
 
 def block_order():
@@ -730,10 +780,16 @@
             pltpu.VMEM((1, hidden), jnp.float32),
             pltpu.VMEM((dest_count, hidden), jnp.float32),
             pltpu.VMEM((dest_count, hidden), jnp.bfloat16),
+            pltpu.VMEM((seeds, hidden), jnp.float32),
             pltpu.VMEM((TILE, hidden), jnp.float32),
             pltpu.VMEM((hidden, hidden), jnp.float32),
             on_the_way(rows - row_inner),
-            on_the_way(row_inner),
+            (
+                pltpu.VMEM((devices, row_inner, hidden), jnp.float32),
+                pltpu.VMEM((16, row_inner, hidden), jnp.float32),
+                pltpu.VMEM((16, row_inner, hidden), jnp.float32),
+                pltpu.VMEM((16, row_inner, hidden), jnp.float32),
+            ),
             pltpu.VMEM((8, hidden), jnp.float32),
             pltpu.VMEM((8, 8, hidden), jnp.float32),
             pltpu.VMEM((4, 8, hidden), jnp.float32),
@@ -750,8 +806,12 @@
             pltpu.SemaphoreType.DMA((sends,)),
             pltpu.SemaphoreType.DMA((5,)),
             pltpu.SemaphoreType.DMA((SETS,)),
-            pltpu.SemaphoreType.DMA((30 + 2 * devices,)),
-            pltpu.SemaphoreType.DMA((24 + 2 * (devices - 1),)),
+            pltpu.SemaphoreType.DMA((30,)),
+            pltpu.SemaphoreType.DMA((24,)),
+            pltpu.SemaphoreType.DMA((2,)),
+            pltpu.SemaphoreType.DMA((2,)),
+            pltpu.SemaphoreType.DMA(()),
+            pltpu.SemaphoreType.DMA(()),
         ],
         compiler_params=pltpu.CompilerParams(
             collective_id=0, has_side_effects=True, vmem_limit_bytes=56 * 2**20
@@ -878,8 +938,7 @@
         and peers == 8
         and peers * node_table.size * 2 <= VMEM_TABLE_LIMIT
         and node_table.shape[1] == 128
-        and node_table.shape[0] % (2 * SPARE * CHUNKS) == 0
-        and (node_table.shape[0] // 2 - node_table.shape[0] // 2 // SPARE) % (4 * CHUNKS) == 0
+        and node_table.shape[0] % (512 * CHUNKS) == 0
         and peers * node_table.shape[0] <= 131072
         and owner_ids.shape[0] % 1024 == 0
         and owner_ids.shape[0] <= 32768

time: 186 us -> 183 us (0.984)
  Pallas kernels: 182 us -> 179 us
    pallas_call x1, Pallas kernels: 180 us -> 177 us  [summed_step(): pl.pallas_call(functools.partial(step_kernel, fan_outer), out_shape=jax.S...]
where the time goes in v7:
time: 183 us
  Pallas kernels  179 us (98%)
  local copies, waits for them, and re-layouts  2.88 us (2%)
    pallas_call x1, Pallas kernels, summed_step(): pl.pallas_call(functools.partial(step_kernel, fan_outer), out_shape=jax.S...  177 us

profile of v7, /device:TPU:0, one launch (start us, length us, event | category | flops | bytes accessed | tf_op | source)
XLA Modules:
  0.0 183.1 jit_solution(3257821738281758225)
XLA Ops:
  0.7 0.0 copy-start
  0.7 0.9 dynamic-slice_reduce_fusion
  1.6 0.2 copy-done
  1.8 0.1 constant_dynamic-slice_fusion
  2.0 0.4 copy.46
  2.4 1.2 reshape.58.near_ref
  3.6 177.3 %shard_map.392.sums_ref = f32[48,256]{1,0:T(8,128)} custom-call(bf16[8192,2,128]{2,1,0:T(2,128)(2,1)} %bitcast.12, f32[8,256]{1,0:T(8,128)} %weight_refs_0_.3, f32[16,256]{1,0:T(8,128)} %weight_refs_1_.3, f32[8,172]{1,0:T(8,128)} %weight_refs_2_.3, f32[8,256]{1,0:T(8,128)} %first_refs_0_.3, f32[16,256]{1,0:T(8,128)} %first_refs_1_.3, ...), custom_call_target="tpu_custom_call" | custom-call | tf_op jit(solution)/shard_map/pallas_call | solution.py:757
  181.0 1.9 %shard_map.393 = (f32[1,1]{1,0:T(1,128)}, f32[1,1]{1,0:T(1,128)}, f32[1,1]{1,0:T(1,128)}, f32[2,3]{1,0:T(2,128)}, f32[8,256]{1,0:T(8,128)}, /*index=5*/f32[16,25...) custom-call(f32[48,256]{1,0:T(8,128)} %shard_map.392.sums_ref, ...), custom_call_target="tpu_custom_call" | custom-call | tf_op jit(solution)/shard_map/pallas_call | solution.py:914
  (3 shorter events, 0.1 us)
Async XLA Ops:
  0.7 1.1 copy-start

commit v8 on v7

--- a/solution.py
+++ b/solution.py
@@ -24,7 +24,9 @@
 MESH = pl.DeviceIdType.MESH
 SLOT = 16
 BLOCK = 16
-CHUNKS = 4
+SHARES = (1, 3, 3, 3, 1)
+SPARE_SHARES = (1, 2, 2, 2, 2)
+CHUNKS = len(SHARES)
 GROUP = 4
 SETS = 4
 SPARE = 9
@@ -117,8 +119,8 @@
     pairs = table_ref.shape[0]
     spare = pairs * SPARE // 64
     quarter = (pairs - spare) // 4
-    chunk = quarter // CHUNKS
-    spare_chunk = spare // CHUNKS
+    part_sizes = [quarter // sum(SHARES) * share for share in SHARES]
+    spare_sizes = [spare // sum(SPARE_SHARES) * share for share in SPARE_SHARES]
 
     def level(value):
         return value + flipped * (3 - 2 * value)
@@ -146,10 +148,12 @@
     sent, now, count = [], [0], [0]
 
     def region(shard, part, piece):
-        return full_ref.at[pl.ds(shard * pairs + part * quarter + piece * chunk, chunk)]
+        start_at = shard * pairs + part * quarter + sum(part_sizes[:piece])
+        return full_ref.at[pl.ds(start_at, part_sizes[piece])]
 
     def spare_region(shard, piece):
-        return full_ref.at[pl.ds(shard * pairs + 4 * quarter + piece * spare_chunk, spare_chunk)]
+        start_at = shard * pairs + 4 * quarter + sum(spare_sizes[:piece])
+        return full_ref.at[pl.ds(start_at, spare_sizes[piece])]
 
     def send(source, target, recv, device, when=None):
         number = count[0]
@@ -173,7 +177,8 @@
         pltpu.make_async_copy(target, target, recv).wait()
 
     def own_piece(piece, device, number, when=None):
-        block = table_ref.at[pl.ds(section * quarter + piece * chunk, chunk)]
+        start_at = section * quarter + sum(part_sizes[:piece])
+        block = table_ref.at[pl.ds(start_at, part_sizes[piece])]
         send(block, region(at, section, piece), z_sem.at[number], device, when)
 
     for piece in range(min(AHEAD, CHUNKS)):
@@ -364,7 +369,8 @@
                 own_piece(piece, across_z, CHUNKS + piece, crosses)
             piece = step - SPARE_AFTER
             if 0 <= piece < CHUNKS:
-                block = table_ref.at[pl.ds(4 * quarter + piece * spare_chunk, spare_chunk)]
+                start_at = 4 * quarter + sum(spare_sizes[:piece])
+                block = table_ref.at[pl.ds(start_at, spare_sizes[piece])]
                 goal = spare_region(at, piece)
                 send(block, goal, spare_sem.at[piece], inner_z)
                 send(block, goal, spare_sem.at[CHUNKS + piece], across_z, crosses)
@@ -494,8 +500,6 @@
         reduce(blocks - GROUP + member, stages[(SETS - 1) % 2][member])
     forward(tiles - 1)
     add_mean(tiles - 1, 1.0)
-    settle(steps + SETTLE)
-
     summing = []
 
     def pass_on(source, target, number, device):
@@ -620,9 +624,9 @@
         return bias_sum + jnp.sum(grad_pre.astype(jnp.float32), axis=0, keepdims=True)
 
     bias_sum = backward(0, jnp.zeros((1, hidden), jnp.float32), own_part[...])
-    bias_sum = lax.fori_loop(1, PAUSE, backward, bias_sum)
+    bias_sum = lax.fori_loop(1, PAUSE, backward, bias_sum, unroll=PAUSE - 1)
     to_plane(early)
-    bias_sum = lax.fori_loop(PAUSE, tiles, backward, bias_sum)
+    bias_sum = lax.fori_loop(PAUSE, tiles, backward, bias_sum, unroll=tiles - PAUSE)
     extra_ref[0:1, :] = bias_sum
     grad_inner = inner_sum[...]
     for number, spot in enumerate(order):
@@ -667,6 +671,9 @@
                 device_id=partner,
                 device_id_type=MESH,
             ).start()
+        if number == 1:
+            for copy in summing:
+                copy.wait_send()
         all_others = sums.at[number, pl.ds(0, 31)]
         arrived(all_others, norm_sem.at[number])
         return jnp.sum(sums[number], axis=0)
@@ -674,13 +681,16 @@
     held = [ref[...] for ref in weight_refs]
     weight_squares = [square_sum(weight) for weight in held]
     rest = whole_sum(early)
+    rest_square = square_sum(rest)
+    extra = collect(extra_line, 26, z)
+    bias_square = square_sum(extra[0:3])
+    settle(steps + SETTLE)
     arrived(late_in.at[pl.ds(0, 15)], late_sem)
     shard = jnp.sum(late_in[...], axis=0)
-    extra = collect(extra_line, 26, z)
     pieces = [shard, rest[0:row_outer], rest[row_outer:, 0:classes]]
-    values = everywhere([square_sum(shard) + square_sum(rest)] + weight_squares, 0)
+    values = everywhere([square_sum(shard) + rest_square] + weight_squares, 0)
     grad_square = jnp.sum(jnp.where(short_lane == 0, values, 0.0), axis=1, keepdims=True)
-    clip_norm = jnp.sqrt(grad_square + square_sum(extra[0:3]))
+    clip_norm = jnp.sqrt(grad_square + bias_square)
     factor = jnp.minimum(1.0, CLIP / clip_norm)
     update_squares = []
     for k in range(3):
@@ -694,8 +704,6 @@
     out_ref[rows + 8 : rows + 9, 0:128] = values
     out_ref[rows + 8 : rows + 9, 128:256] = updates
     out_ref[rows + 9 :, :] = jnp.zeros((7, hidden), jnp.float32)
-    for copy in summing:
-        copy.wait_send()
     for number in range(2):
         arrived(sums.at[number, pl.ds(0, 31)], norm_send_sem.at[number])
     arrived(late_in.at[pl.ds(0, 15)], late_send_sem)
@@ -938,7 +946,7 @@
         and peers == 8
         and peers * node_table.size * 2 <= VMEM_TABLE_LIMIT
         and node_table.shape[1] == 128
-        and node_table.shape[0] % (512 * CHUNKS) == 0
+        and node_table.shape[0] % 512 == 0
         and peers * node_table.shape[0] <= 131072
         and owner_ids.shape[0] % 1024 == 0
         and owner_ids.shape[0] <= 32768

time: 183 us -> 181 us (0.989)
  Pallas kernels: 179 us -> 177 us
    pallas_call x1, Pallas kernels: 177 us -> 175 us  [summed_step(): pl.pallas_call(functools.partial(step_kernel, fan_outer), out_shape=jax.S...]
where the time goes in v8:
time: 181 us
  Pallas kernels  177 us (98%)
  local copies, waits for them, and re-layouts  2.88 us (2%)
    pallas_call x1, Pallas kernels, summed_step(): pl.pallas_call(functools.partial(step_kernel, fan_outer), out_shape=jax.S...  175 us

profile of v8, /device:TPU:0, one launch (start us, length us, event | category | flops | bytes accessed | tf_op | source)
XLA Modules:
  0.0 180.9 jit_solution(7074480033662252872)
XLA Ops:
  0.7 0.0 copy-start
  0.7 0.9 dynamic-slice_reduce_fusion
  1.6 0.2 copy-done
  1.8 0.1 constant_dynamic-slice_fusion
  2.0 0.4 copy.46
  2.4 1.2 reshape.58.near_ref
  3.6 175.1 %shard_map.392.sums_ref = f32[48,256]{1,0:T(8,128)} custom-call(bf16[8192,2,128]{2,1,0:T(2,128)(2,1)} %bitcast.12, f32[8,256]{1,0:T(8,128)} %weight_refs_0_.3, f32[16,256]{1,0:T(8,128)} %weight_refs_1_.3, f32[8,172]{1,0:T(8,128)} %weight_refs_2_.3, f32[8,256]{1,0:T(8,128)} %first_refs_0_.3, f32[16,256]{1,0:T(8,128)} %first_refs_1_.3, ...), custom_call_target="tpu_custom_call" | custom-call | tf_op jit(solution)/shard_map/pallas_call | solution.py:765
  178.8 1.9 %shard_map.393 = (f32[1,1]{1,0:T(1,128)}, f32[1,1]{1,0:T(1,128)}, f32[1,1]{1,0:T(1,128)}, f32[2,3]{1,0:T(2,128)}, f32[8,256]{1,0:T(8,128)}, /*index=5*/f32[16,25...) custom-call(f32[48,256]{1,0:T(8,128)} %shard_map.392.sums_ref, ...), custom_call_target="tpu_custom_call" | custom-call | tf_op jit(solution)/shard_map/pallas_call | solution.py:922
  (3 shorter events, 0.1 us)
Async XLA Ops:
  0.7 1.1 copy-start

commit v9 on v8

--- a/solution.py
+++ b/solution.py
@@ -34,7 +34,7 @@
 AHEAD = 1
 AHEAD_ACROSS = 1
 LAG = 2
-FAR_LAG = 5
+FAR_LAG = 6
 SPARE_AFTER = 2
 SPARE_LAG = 4
 TILE = 256

time: 181 us -> 181 us (level)
  no operation moved by 1% of the time
where the time goes in v9:
time: 181 us
  Pallas kernels  177 us (98%)
  local copies, waits for them, and re-layouts  2.88 us (2%)
    pallas_call x1, Pallas kernels, summed_step(): pl.pallas_call(functools.partial(step_kernel, fan_outer), out_shape=jax.S...  175 us

profile of v9, /device:TPU:0, one launch (start us, length us, event | category | flops | bytes accessed | tf_op | source)
XLA Modules:
  0.0 180.7 jit_solution(5792592465478501322)
XLA Ops:
  0.7 0.0 copy-start
  0.7 0.9 dynamic-slice_reduce_fusion
  1.6 0.2 copy-done
  1.8 0.1 constant_dynamic-slice_fusion
  2.0 0.4 copy.46
  2.4 1.2 reshape.58.near_ref
  3.6 174.9 %shard_map.392.sums_ref = f32[48,256]{1,0:T(8,128)} custom-call(bf16[8192,2,128]{2,1,0:T(2,128)(2,1)} %bitcast.12, f32[8,256]{1,0:T(8,128)} %weight_refs_0_.3, f32[16,256]{1,0:T(8,128)} %weight_refs_1_.3, f32[8,172]{1,0:T(8,128)} %weight_refs_2_.3, f32[8,256]{1,0:T(8,128)} %first_refs_0_.3, f32[16,256]{1,0:T(8,128)} %first_refs_1_.3, ...), custom_call_target="tpu_custom_call" | custom-call | tf_op jit(solution)/shard_map/pallas_call | solution.py:765
  178.6 1.9 %shard_map.393 = (f32[1,1]{1,0:T(1,128)}, f32[1,1]{1,0:T(1,128)}, f32[1,1]{1,0:T(1,128)}, f32[2,3]{1,0:T(2,128)}, f32[8,256]{1,0:T(8,128)}, /*index=5*/f32[16,25...) custom-call(f32[48,256]{1,0:T(8,128)} %shard_map.392.sums_ref, ...), custom_call_target="tpu_custom_call" | custom-call | tf_op jit(solution)/shard_map/pallas_call | solution.py:922
  (3 shorter events, 0.1 us)
Async XLA Ops:
  0.7 1.1 copy-start
